TPU v7x, 128 devices: a whole 4x4x4 slice. The times are simulated.
128 devices in a mesh: sub: 2 (over z_hi), row: 8 (over x, z_lo), col: 8 (over y, core).
Axes of the slice: x: 4, y: 4, z: 4 (z_hi: 2, z_lo: 2; z = z_hi * 2 + z_lo), core: 2. Of those that a mesh axis runs over, the one named last changes fastest.
Arguments:
- top_inverse: float32 [4096, 4096], P(('sub', 'row'), 'col'), may hold values from -1 to 4, as said below
- ancestors: int32 [2, 1024], replicated, may hold values from 0 to 4095, as said below
- child_panel: float32 [2, 1024, 3072], P('sub', 'row', 'col'), may hold values from -0.109375 to 0.109375
- child_inverse: float32 [2, 3072, 3072], P('sub', 'row', 'col'), may hold values from -1 to 3, as said below
Outputs:
- top_block: float32 [4096, 4096], P(('sub', 'row'), 'col')
- cross_block: float32 [2, 1024, 3072], P('sub', 'row', 'col')
- child_block: float32 [2, 3072, 3072], P('sub', 'row', 'col')
Inputs may be any that keep to these rules, and one draw needn't show every extreme that they name: `ancestors`: each row lists 1024 distinct rows of the top separator in increasing order, always including the first and the last. `top_inverse`: zero above the diagonal, positive diagonal. `child_inverse`: each block zero above the diagonal, positive diagonal.
All inputs are finite; a program needn't handle non-finite values.
Results may differ from a plain program's by a relative error of at most 0.00014.
Values sent between devices are 32-bit elements; how exact they have to be, the bound alone decides.
No kernel may reach another device: no remote copies, remote signals or barrier semaphores. Data moves between devices by JAX's collectives and lax.ppermute only.
A program may use at most 128 MiB of HBM per device.

v0:
```python
import jax
import jax.numpy as jnp
from jax import lax
from jax.experimental import pallas as pl
from jax.experimental.pallas import tpu as pltpu
from jax.sharding import Mesh, PartitionSpec as P

AXES = ("sub", "x", "zl", "y", "core")
SIZES = (2, 4, 2, 4, 2)
ROWS = ("sub", "x", "zl")
COLS = ("y", "core")
F32 = jnp.float32
VMEM_BYTES = 60 * 2**20


def along(value, axis, step):
    return lax.ppermute(value, axis, [(i, (i + step) % 4) for i in range(4)])


def along_z(value, step):
    return lax.ppermute(value, ("sub", "zl"), [(i, (i + step) % 4) for i in range(4)])


def other(value, axis):
    return lax.ppermute(value, axis, [(0, 1), (1, 0)])


def parts(value):
    high = value.astype(jnp.bfloat16)
    return high, (value - high.astype(F32)).astype(jnp.bfloat16)


def product(a, b, da, db):
    a_high, a_low = parts(a)
    b_high, b_low = parts(b)

    def one(first, second):
        return lax.dot_general(
            first, second, (((da,), (db,)), ((), ())), preferred_element_type=F32
        )

    return one(a_high, b_high) + (one(a_high, b_low) + one(a_low, b_high))


def fetch(pairs, sems):
    copies = [pltpu.make_async_copy(s, d, sems.at[i]) for i, (s, d) in enumerate(pairs)]
    for copy in copies:
        copy.start()
    return copies


def finish(copies):
    for copy in copies:
        copy.wait()


def call(kernel, where, inputs, outs, scratch, copies, indices=(), direct=()):
    n_in = len(inputs)
    smem = pl.BlockSpec(memory_space=pltpu.SMEM)
    anywhere = pl.BlockSpec(memory_space=pl.ANY)
    vmem = pl.BlockSpec(memory_space=pltpu.VMEM)
    return pl.pallas_call(
        kernel,
        out_shape=list(outs),
        in_specs=[smem] * (1 + len(indices)) + [anywhere] * n_in,
        out_specs=[anywhere if i in direct else vmem for i in range(len(outs))],
        scratch_shapes=list(scratch) + [pltpu.SemaphoreType.DMA((copies,))],
        compiler_params=pltpu.CompilerParams(vmem_limit_bytes=VMEM_BYTES),
        cost_estimate=pl.CostEstimate(flops=1, bytes_accessed=1, transcendentals=0),
    )(where, *indices, *inputs)


def shape(*dims):
    return jax.ShapeDtypeStruct(dims, F32)


def spot(where):
    return [where[i] for i in range(5)]


def select_kernel(where, index, *refs):
    pieces, (out, *sent), (stripe, picked, sems) = refs[:8], refs[8:14], refs[14:]
    sub, x, zl, y, core = spot(where)
    size, depth = pieces[0].shape
    finish(fetch([(p, stripe.at[pl.ds(i * size, size)]) for i, p in enumerate(pieces)], sems))
    half = size // 2
    pairs = []
    for i in range(5):
        target = (2 * sub + zl + i % 4) % 4
        for h in range(2):
            place = (y - 2 * (target // 2) - h + 8) % 4 + (4 if i == 4 else 0)
            row = pl.multiple_of(place * size + (target % 2) * half, half)
            pairs.append((stripe.at[pl.ds(row, half)], sent[i].at[pl.ds(h * half, half)]))
    copies = fetch(pairs, sems)

    def eight(i, carry):
        for k in range(8):
            at = i * 8 + k
            picked[pl.ds(at, 1), :] = stripe[pl.ds(index[at], 1), :]
        return carry

    count = picked.shape[0]
    lax.fori_loop(0, count // 8, eight, 0)
    order, share = count // 2, out.shape[2]
    for child in range(2):
        left = picked[pl.ds(child * order, order), :]
        start = pl.multiple_of(child * order + (2 * y + core) * share, share)
        right = picked[pl.ds(start, share), :]
        block = product(left, right, 1, 1).reshape(order // share, share, share)
        out[pl.ds(child * (order // share), order // share)] = block
    finish(copies)


def cross_kernel(where, *refs):
    covs, factors, out, (held, right, sems) = refs[:8], refs[8:12], refs[12], refs[13:]
    sub, x, zl, y, core = spot(where)
    depth = right.shape[0] // 4
    pairs = [(c, held.at[i]) for i, c in enumerate(covs)]
    pairs += [(f, right.at[pl.ds(i * depth, depth)]) for i, f in enumerate(factors)]
    finish(fetch(pairs, sems))

    def block(i):
        return held[(y - x + i // 2 + 8) % 4 + jnp.where(core == i % 2, 0, 4)]

    out[...] = -product(jnp.concatenate([block(i) for i in range(8)], 1), right[...], 1, 0)


def factor_kernel(where, *refs):
    panels, inverses, out, (left, right, sems) = refs[:8], refs[8:12], refs[12], refs[13:]
    sub, x, zl, y, core = spot(where)
    pairs = [
        (p, left.at[(core + i // 4) % 2, (y - i % 4 + 4) % 4]) for i, p in enumerate(panels)
    ]
    pairs += [(v, right.at[(x - i + 4) % 4]) for i, v in enumerate(inverses)]
    finish(fetch(pairs, sems))
    both = jnp.concatenate(
        [jnp.concatenate([left[p, i] for i in range(4)], 1) for p in range(2)], 0
    )
    out[...] = product(both, right[...].reshape(both.shape[1], out.shape[1]), 1, 0)


def whole_kernel(where, *refs):
    mine, came, both, turned = refs
    total = mine[...] + came[...]
    both[...] = total
    rows = turned.shape[1]

    @pl.when(where[2] == 0)
    def _():
        turned[...] = total[:rows].T

    @pl.when(where[2] == 1)
    def _():
        turned[...] = total[rows:].T


def fetch_left(lefts, left, core, zl, y):
    mine = jnp.where(core == zl, 0, 1)
    return [(p, left.at[(mine + i // 4) % 2, (y - i % 4 + 4) % 4]) for i, p in enumerate(lefts)]


def gram_kernel(where, *refs):
    lefts, rights, (keep, send), (left, right, sems) = refs[:8], refs[8:12], refs[12:14], refs[14:]
    sub, x, zl, y, core = spot(where)
    pairs = fetch_left(lefts, left, core, zl, y)
    pairs += [(v, right.at[(x - i + 4) % 4]) for i, v in enumerate(rights)]
    finish(fetch(pairs, sems))
    depth = right.shape[0] * right.shape[1]
    for slot, out in ((1, send), (0, keep)):
        both = jnp.concatenate([left[slot, i] for i in range(4)], 1)
        out[...] = product(both, right[...].reshape(depth, right.shape[2]), 1, 0)


def update_kernel(where, *refs):
    keep_gram, send_gram, refs = refs[0], refs[1], refs[2:]
    lefts, rights, (keep, send), (left, right, sems) = refs[:8], refs[8:12], refs[12:14], refs[14:]
    sub, x, zl, y, core = spot(where)
    pairs = fetch_left(lefts, left, core, zl, y)
    pairs += [(v, right.at[(x - i + 4) % 4]) for i, v in enumerate(rights)]
    finish(fetch(pairs + [(keep_gram, keep), (send_gram, send)], sems))
    depth = right.shape[0] * right.shape[1]
    for slot, out in ((1, send), (0, keep)):
        both = jnp.concatenate([left[slot, i] for i in range(4)], 1)
        out[...] = out[...] - product(both, right[...].reshape(depth, right.shape[2]), 1, 0)


def flip_kernel(value, out):
    out[...] = value[...].T


def top_kernel(where, *refs):
    lefts, rights, out, (left, right, sems) = refs[:8], refs[8], refs[9], refs[10:]
    sub, x, zl, y, core = spot(where)
    depth = right.shape[0] // 4
    pairs = [(p, left.at[(core + i // 4) % 2, i % 4]) for i, p in enumerate(lefts)]
    for i in range(4):
        pairs.append((rights.at[(2 * sub + zl - i + 4) % 4], right.at[pl.ds(i * depth, depth)]))
    finish(fetch(pairs, sems))
    rows = out.shape[1]
    for parity in range(2):
        both = jnp.concatenate([left[parity, i] for i in range(4)], 1)
        total = product(both, right[...], 1, 0)
        for h in range(2):
            out[2 * h + parity] = total[h * rows : (h + 1) * rows]


def after(value, *first):
    return lax.optimization_barrier((value, *first))[0]


def on_device(top_inverse, ancestors, child_panel, child_inverse):
    sub, x, zl, y, core = (lax.axis_index(a) for a in AXES)
    where = jnp.stack([sub, x, zl, y, core]).astype(jnp.int32)
    panel = child_panel[0]
    inverse = child_inverse[0]
    rows, width = panel.shape
    stripe, block = top_inverse.shape
    order = ancestors.shape[1]
    share = order // 8

    def vmem(*dims):
        return pltpu.VMEM(dims, F32)

    def flipped(value):
        return pl.pallas_call(
            flip_kernel,
            out_shape=shape(value.shape[1], value.shape[0]),
            cost_estimate=pl.CostEstimate(flops=1, bytes_accessed=1, transcendentals=0),
        )(value)

    def swap_xy(value):
        pairs = [(4 * a + b, 4 * b + a) for a in range(4) for b in range(4)]
        return lax.ppermute(value, ("x", "y"), pairs)

    def over_y(value):
        return [value] + [along(value, "y", e) for e in (1, 2, 3)]

    def both_cores(values):
        return values + [other(v, "core") for v in values]

    stripes = over_y(flipped(top_inverse))
    flip = [(2 * a + c, 2 * (1 - a) + (1 - c)) for a in (0, 1) for c in (0, 1) if a != c]
    panel = jnp.where(core == zl, panel, lax.ppermute(panel, ("zl", "core"), flip))
    inverse_x = {0: inverse} | {d: along(inverse, "x", d) for d in (1, 3)}
    top_z = lax.all_gather(top_inverse, ("sub", "zl"), axis=0)
    inverse_t = flipped(inverse)
    stripes, panel, inverse_t, inverse = lax.optimization_barrier(
        (stripes, panel, inverse_t, inverse)
    )

    panels = over_y(panel)
    inverse_x[2] = along(inverse, "x", 2)
    inverse_x = [inverse_x[d] for d in range(4)]
    inverse_t = swap_xy(inverse_t)
    owner = ancestors // block
    place = (y - owner // 2) % 4 + jnp.where(owner % 2 == core, 0, 4)
    index = (place * block + ancestors % block).reshape(-1)
    part, own0, own1, own2, own3, there0 = call(
        select_kernel, where, both_cores(stripes),
        [shape(16, share, share)] + [shape(block, stripe)] * 5,
        [vmem(8 * block, stripe), vmem(2 * order, stripe)], 10, (index,), (1, 2, 3, 4, 5),
    )
    part, own1, own2, own3, panels, inverse_x = lax.optimization_barrier(
        (part, own1, own2, own3, panels, inverse_x)
    )

    cov = lax.all_to_all(part, ROWS, 0, 0).sum(0)
    (factor_part,) = call(
        factor_kernel, where, both_cores(panels) + inverse_x,
        [shape(2 * rows, width)], [vmem(2, 4, rows, width), vmem(4, width, width)], 12,
    )
    factor, factor_t = pl.pallas_call(
        whole_kernel,
        out_shape=[shape(2 * rows, width), shape(width, rows)],
        in_specs=[pl.BlockSpec(memory_space=pltpu.SMEM)]
        + [pl.BlockSpec(memory_space=pltpu.VMEM)] * 2,
        out_specs=[pl.BlockSpec(memory_space=pltpu.VMEM)] * 2,
        compiler_params=pltpu.CompilerParams(vmem_limit_bytes=VMEM_BYTES),
        cost_estimate=pl.CostEstimate(flops=1, bytes_accessed=1, transcendentals=0),
    )(where, factor_part, other(factor_part, "zl"))
    inverse_columns = over_y(inverse_t)
    cov, factor, factor_t, inverse_columns = lax.optimization_barrier(
        (cov, factor, factor_t, inverse_columns)
    )

    factor_x = [factor] + [along(factor, "x", d) for d in (1, 2, 3)]
    cov_y = over_y(cov)
    (cross,) = call(
        cross_kernel, where, both_cores(cov_y) + factor_x, [shape(rows, width)],
        [vmem(8, rows, share), vmem(8 * rows, width)], 12,
    )
    own = [along_z(after(v, *cov_y), d + 1) for d, v in enumerate((own1, own2, own3))]
    factor_t = swap_xy(after(factor_t, factor_x[1], factor_x[2], factor_x[3]))
    cross, inverse_columns = lax.optimization_barrier((cross, inverse_columns))

    cross_x = [cross] + [along(cross, "x", d) for d in (1, 2, 3)]
    factor_columns = over_y(factor_t)
    there = [there0] + [other(v, "core") for v in own]
    (top_part,) = call(
        top_kernel, where, [own0] + own + there + [top_z], [shape(4, stripe, block)],
        [vmem(2, 4, block, stripe), vmem(4 * stripe, block)], 12,
    )
    grams = call(
        gram_kernel, where, both_cores(inverse_columns) + inverse_x, [shape(width, width)] * 2,
        [vmem(2, 4, width, width), vmem(4, width, width)], 12,
    )
    grams, cross_x, factor_columns = lax.optimization_barrier((grams, cross_x, factor_columns))

    block_keep, block_send = call(
        update_kernel, where, list(grams) + both_cores(factor_columns) + cross_x,
        [shape(width, width)] * 2, [vmem(2, 4, width, rows), vmem(4, rows, width)], 14,
    )
    child_block = block_keep + other(block_send, "zl")
    top_block = lax.all_to_all(after(top_part, *cross_x[1:]), "x", 0, 0).sum(0)
    return top_block, cross[None], child_block[None]


def solution(mesh):
    fine = Mesh(mesh.devices.reshape(SIZES), AXES)
    child = P("sub", ("x", "zl"), COLS)
    top = P(ROWS, COLS)
    return jax.shard_map(
        on_device,
        mesh=fine,
        in_specs=(top, P(), child, child),
        out_specs=(top, child, child),
        check_vma=False,
    )
```

profile of v0, /device:TPU:2, one launch (start us, length us, event | category | flops | bytes accessed | tf_op | source)
XLA Modules:
  0.0 248.6 jit_solution(4972123207761073087)
XLA Ops:
  7.2 0.8 collective-permute-start.3
  8.1 1.6 collective-permute-start.11
  9.6 2.0 shard_map.67.refs_0_
  11.7 1.6 collective-permute-start
  13.2 2.9 %collective-permute-start.1 = (f32[512,256]{1,0:T(8,128)}, f32[512,256]{1,0:T(8,128)}, u32[]{:S(2)}, u32[]{:S(2)}) collective-permute-start(f32[512,256]{1,0:T(8,128)} %shard_map.67.refs_0_), channel_id=1, source_target_pairs={{0,4},{2,6},{4,0},{6,2},{1,5},{3,7},{5,1},{7,3},{8,12},{10,14},{12... | collective-permute-start | bytes 1572872 | tf_op jit(solution)/shard_map/ppermute | solution.py:17
  16.1 1.3 collective-permute-start.2
  17.5 0.5 collective-permute-start.13
  18.0 2.2 shard_map.68
  20.2 5.5 %collective-permute-done.refs_1_ = f32[512,256]{1,0:T(8,128)S(1)} collective-permute-done((f32[512,256]{1,0:T(8,128)}, f32[512,256]{1,0:T(8,128)S(1)}, u32[]{:S(2)}, u32[]{:S(2)}) %collective-permute-start) | collective-permute-done | bytes 524320 | tf_op jit(solution)/shard_map/ppermute | solution.py:17
  25.7 12.6 %collective-permute-done.1.refs_2_ = f32[512,256]{1,0:T(8,128)} collective-permute-done((f32[512,256]{1,0:T(8,128)}, f32[512,256]{1,0:T(8,128)}, u32[]{:S(2)}, u32[]{:S(2)}) %collective-permute-start.1) | collective-permute-done | bytes 524320 | tf_op jit(solution)/shard_map/ppermute | solution.py:17
  38.4 0.6 collective-permute-done.2.refs_3_
  39.0 1.3 collective-permute-start.4
  40.9 1.2 collective-permute-start.12
  42.1 0.8 collective-permute-done.4.refs_4_
  42.9 2.0 collective-permute-start.10
  45.0 2.8 %collective-permute-start.9 = (f32[128,384]{1,0:T(8,128)S(1)}, f32[128,384]{1,0:T(8,128)}, u32[]{:S(2)}, u32[]{:S(2)}) collective-permute-start(f32[128,384]{1,0:T(8,128)S(1)} %broadcast_select_fusion.refs_0_), channel_id=1, source_target_pairs={{0,4},{2,6},{4,0},{6,2},{1,5},{3,7},{5,1},{7,3},{8,12},{10,14},{12... | collective-permute-start | bytes 589832 | tf_op jit(solution)/shard_map/ppermute | solution.py:17
  47.8 4.8 %collective-permute-start.19 = (f32[384,384]{1,0:T(8,128)}, f32[384,384]{1,0:T(8,128)S(1)}, u32[]{:S(2)}, u32[]{:S(2)}) collective-permute-start(f32[384,384]{1,0:T(8,128)} %shard_map.68), channel_id=1, source_target_pairs={{0,0},{2,16},{4,32},{6,48},{16,2},{18,18},{20,34},{22,50},{32,4},{... | collective-permute-start | bytes 1769480 | tf_op jit(solution)/shard_map/ppermute | solution.py:233
  52.7 0.6 copy.9
  53.3 0.7 stack.23.where
  53.9 12.5 %shard_map.69 = (f32[16,128,128]{2,1,0:T(8,128)}, f32[512,256]{1,0:T(8,128)}, f32[512,256]{1,0:T(8,128)}, f32[512,256]{1,0:T(8,128)}, f32[512,256]{1,0:T(8,128)}, /*index=5*/f32[512,256]{1,0:T(8,128)}) custom-call(s32[5]{0:T(128)} %stack.23.where, s32[2048]{0:T(1024)} %bitcast.26, f32[512,256]{1,0:T(8,128)} %shard_map.67.refs_0_, f32[512,256]{1,0:T(8,128)} %copy-done.10, ...), custom_call_target="tpu_custom_call" | custom-call | flops 1 | bytes 1 | tf_op jit(solution)/shard_map/pallas_call | solution.py:62
  66.5 7.6 %all-to-all-start = ((f32[16,128,128]{2,1,0:T(8,128)}), f32[16,128,128]{2,1,0:T(8,128)S(1)}, u32[]{:S(2)}, u32[]{:S(2)}) async-start(f32[16,128,128]{2,1,0:T(8,128)} %get-tuple-element.73), calls=%async_computation | async-start | bytes 2097152 | tf_op jit(solution)/shard_map/all_to_all | solution.py:267
  75.2 9.1 %collective-permute-done.19.refs_0_ = f32[384,384]{1,0:T(8,128)S(1)} collective-permute-done((f32[384,384]{1,0:T(8,128)}, f32[384,384]{1,0:T(8,128)S(1)}, u32[]{:S(2)}, u32[]{:S(2)}) %collective-permute-start.19) | collective-permute-done | bytes 589856 | tf_op jit(solution)/shard_map/ppermute | solution.py:233
  84.4 6.6 %collective-permute-start.21 = (f32[384,384]{1,0:T(8,128)S(1)}, f32[384,384]{1,0:T(8,128)}, u32[]{:S(2)}, u32[]{:S(2)}) collective-permute-start(f32[384,384]{1,0:T(8,128)S(1)} %collective-permute-done.19.refs_0_), channel_id=1, source_target_pairs={{0,4},{2,6},{4,0},{6,2},{1,5},{3,7},{5,1},{7,3},{8,12},{10,14},{12... | collective-permute-start | bytes 1769480 | tf_op jit(solution)/shard_map/ppermute | solution.py:17
  91.0 2.5 %collective-permute-start.22 = (f32[384,384]{1,0:T(8,128)S(1)}, f32[384,384]{1,0:T(8,128)}, u32[]{:S(2)}, u32[]{:S(2)}) collective-permute-start(f32[384,384]{1,0:T(8,128)S(1)} %collective-permute-done.19.refs_0_), channel_id=1, source_target_pairs={{0,6},{2,0},{4,2},{6,4},{1,7},{3,1},{5,3},{7,5},{8,14},{10,8},{12,... | collective-permute-start | bytes 1769480 | tf_op jit(solution)/shard_map/ppermute | solution.py:17
  93.6 5.1 %shard_map.70.refs_0_ = f32[256,384]{1,0:T(8,128)} custom-call(s32[5]{0:T(128)} %stack.23.where, f32[128,384]{1,0:T(8,128)} %copy-done.4, f32[128,384]{1,0:T(8,128)} %copy-done.20, f32[128,384]{1,0:T(8,128)} %collective-permute-done.9.refs_2_, f32[128,384]{1,0:T(8,128)} %copy-done.19, f32[128,384]{1,0:T(8,128)} %copy-done.21, f32[128,384]{1,0:T(8,128)} %copy-done.22, ...), custom_call_target="tpu_custom_call" | custom-call | flops 1 | bytes 1 | tf_op jit(solution)/shard_map/pallas_call | solution.py:62
  98.7 1.1 collective-permute-start.18
  99.8 9.3 %collective-permute-done.18.refs_1_ = f32[256,384]{1,0:T(8,128)S(1)} collective-permute-done((f32[256,384]{1,0:T(8,128)}, f32[256,384]{1,0:T(8,128)S(1)}, u32[]{:S(2)}, u32[]{:S(2)}) %collective-permute-start.18) | collective-permute-done | bytes 393248 | tf_op jit(solution)/shard_map/ppermute | solution.py:25
  109.1 0.8 copy-done.17
  109.9 2.1 shard_map.71
  112.1 5.0 %collective-permute-done.21.refs_2_ = f32[384,384]{1,0:T(8,128)} collective-permute-done((f32[384,384]{1,0:T(8,128)S(1)}, f32[384,384]{1,0:T(8,128)}, u32[]{:S(2)}, u32[]{:S(2)}) %collective-permute-start.21) | collective-permute-done | bytes 589856 | tf_op jit(solution)/shard_map/ppermute | solution.py:17
  117.5 4.3 %collective-permute-start.37 = (f32[256,384]{1,0:T(8,128)}, f32[256,384]{1,0:T(8,128)S(1)}, u32[]{:S(2)}, u32[]{:S(2)}) collective-permute-start(f32[256,384]{1,0:T(8,128)} %get-tuple-element.92.refs_8_), channel_id=1, source_target_pairs={{0,32},{16,48},{32,0},{48,16},{1,33},{17,49},{33,1},{49,17},{2,34}... | collective-permute-start | bytes 1179656 | tf_op jit(solution)/shard_map/ppermute | solution.py:17
  121.8 2.6 %collective-permute-start.38 = (f32[256,384]{1,0:T(8,128)}, f32[256,384]{1,0:T(8,128)S(1)}, u32[]{:S(2)}, u32[]{:S(2)}) collective-permute-start(f32[256,384]{1,0:T(8,128)} %get-tuple-element.92.refs_8_), channel_id=1, source_target_pairs={{0,48},{16,0},{32,16},{48,32},{1,49},{17,1},{33,17},{49,33},{2,50}... | collective-permute-start | bytes 1179656 | tf_op jit(solution)/shard_map/ppermute | solution.py:17
  124.7 3.7 %collective-permute-start.24 = (f32[128,128]{1,0:T(8,128)S(1)}, f32[128,128]{1,0:T(8,128)S(1)}, u32[]{:S(2)}, u32[]{:S(2)}) collective-permute-start(f32[128,128]{1,0:T(8,128)S(1)} %reduce_sum.18.refs_0_), channel_id=1, source_target_pairs={{0,4},{2,6},{4,0},{6,2},{1,5},{3,7},{5,1},{7,3},{8,12},{10,14},{12... | collective-permute-start | bytes 196616 | tf_op jit(solution)/shard_map/ppermute | solution.py:17
  128.3 1.6 collective-permute-done.23.refs_1_
  130.0 1.2 collective-permute-start.25
  131.3 3.0 %collective-permute-done.25.refs_3_ = f32[128,128]{1,0:T(8,128)S(1)} collective-permute-done((f32[128,128]{1,0:T(8,128)S(1)}, f32[128,128]{1,0:T(8,128)S(1)}, u32[]{:S(2)}, u32[]{:S(2)}) %collective-permute-start.25) | collective-permute-done | bytes 65568 | tf_op jit(solution)/shard_map/ppermute | solution.py:17
  134.9 3.7 %collective-permute-done.38.refs_11_ = f32[256,384]{1,0:T(8,128)S(1)} collective-permute-done((f32[256,384]{1,0:T(8,128)}, f32[256,384]{1,0:T(8,128)S(1)}, u32[]{:S(2)}, u32[]{:S(2)}) %collective-permute-start.38) | collective-permute-done | bytes 393248 | tf_op jit(solution)/shard_map/ppermute | solution.py:17
  138.5 5.1 %collective-permute-start.46 = (f32[384,128]{1,0:T(8,128)}, f32[384,128]{1,0:T(8,128)S(1)}, u32[]{:S(2)}, u32[]{:S(2)}) collective-permute-start(f32[384,128]{1,0:T(8,128)} %get-tuple-element.105), channel_id=1, source_target_pairs={{0,0},{2,16},{4,32},{6,48},{16,2},{18,18},{20,34},{22,50},{32,4},{... | collective-permute-start | bytes 589832 | tf_op jit(solution)/shard_map/ppermute | solution.py:233
  144.4 0.6 copy-done.40
  145.0 3.7 %shard_map.73.refs_10_ = f32[128,384]{1,0:T(8,128)} custom-call(s32[5]{0:T(128)} %stack.23.where, f32[128,128]{1,0:T(8,128)} %copy-done.18, f32[128,128]{1,0:T(8,128)} %copy-done.34, f32[128,128]{1,0:T(8,128)} %copy-done.35, f32[128,128]{1,0:T(8,128)} %copy-done.36, f32[128,128]{1,0:T(8,128)} %copy-done.37, f32[128,128]{1,0:T(8,128)} %copy-done.38, ...), custom_call_target="tpu_custom_call" | custom-call | flops 1 | bytes 1 | tf_op jit(solution)/shard_map/pallas_call | solution.py:62
  148.7 1.2 collective-permute-start.43
  149.9 2.6 %collective-permute-start.28 = (f32[512,256]{1,0:T(8,128)}, f32[512,256]{1,0:T(8,128)S(1)}, u32[]{:S(2)}, u32[]{:S(2)}) collective-permute-start(f32[512,256]{1,0:T(8,128)} %get-tuple-element.90), channel_id=1, source_target_pairs={{0,72},{8,0},{64,8},{72,64},{1,73},{9,1},{65,9},{73,65},{2,74},{10... | collective-permute-start | bytes 1572872 | tf_op jit(solution)/shard_map/ppermute | solution.py:21
  152.4 1.4 collective-permute-start.27
  153.8 3.1 %collective-permute-start.44 = (f32[128,384]{1,0:T(8,128)}, f32[128,384]{1,0:T(8,128)S(1)}, u32[]{:S(2)}, u32[]{:S(2)}) collective-permute-start(f32[128,384]{1,0:T(8,128)} %shard_map.73.refs_10_), channel_id=1, source_target_pairs={{0,32},{16,48},{32,0},{48,16},{1,33},{17,49},{33,1},{49,17},{2,34}... | collective-permute-start | bytes 589832 | tf_op jit(solution)/shard_map/ppermute | solution.py:17
  156.9 2.5 collective-permute-start.45
  159.4 1.4 collective-permute-start.26
  160.8 2.6 %collective-permute-done.44.refs_12_ = f32[128,384]{1,0:T(8,128)S(1)} collective-permute-done((f32[128,384]{1,0:T(8,128)}, f32[128,384]{1,0:T(8,128)S(1)}, u32[]{:S(2)}, u32[]{:S(2)}) %collective-permute-start.44) | collective-permute-done | bytes 196640 | tf_op jit(solution)/shard_map/ppermute | solution.py:17
  163.4 3.1 %collective-permute-done.45.refs_13_ = f32[128,384]{1,0:T(8,128)} collective-permute-done((f32[128,384]{1,0:T(8,128)}, f32[128,384]{1,0:T(8,128)}, u32[]{:S(2)}, u32[]{:S(2)}) %collective-permute-start.45) | collective-permute-done | bytes 196640 | tf_op jit(solution)/shard_map/ppermute | solution.py:17
  166.5 8.8 %collective-permute-done.28.refs_3_ = f32[512,256]{1,0:T(8,128)S(1)} collective-permute-done((f32[512,256]{1,0:T(8,128)}, f32[512,256]{1,0:T(8,128)S(1)}, u32[]{:S(2)}, u32[]{:S(2)}) %collective-permute-start.28) | collective-permute-done | bytes 524320 | tf_op jit(solution)/shard_map/ppermute | solution.py:21
  175.3 0.5 collective-permute-start.42
  175.8 3.2 %collective-permute-done.26.refs_1_ = f32[512,256]{1,0:T(8,128)} collective-permute-done((f32[512,256]{1,0:T(8,128)}, f32[512,256]{1,0:T(8,128)}, u32[]{:S(2)}, u32[]{:S(2)}) %collective-permute-start.26) | collective-permute-done | bytes 524320 | tf_op jit(solution)/shard_map/ppermute | solution.py:21
  179.0 8.0 %collective-permute-done.47.refs_3_ = f32[384,128]{1,0:T(8,128)S(1)} collective-permute-done((f32[384,128]{1,0:T(8,128)S(1)}, f32[384,128]{1,0:T(8,128)S(1)}, u32[]{:S(2)}, u32[]{:S(2)}) %collective-permute-start.47) | collective-permute-done | bytes 196640 | tf_op jit(solution)/shard_map/ppermute | solution.py:17
  187.0 0.6 collective-permute-start.30
  187.9 1.7 collective-permute-start.49
  189.6 8.4 %shard_map.74 = (f32[384,384]{1,0:T(8,128)}, f32[384,384]{1,0:T(8,128)}) custom-call(s32[5]{0:T(128)} %stack.23.where, f32[384,384]{1,0:T(8,128)} %copy-done.5, f32[384,384]{1,0:T(8,128)} %copy-done.6, f32[384,384]{1,0:T(8,128)} %collective-permute-done.21.refs_2_, f32[384,384]{1,0:T(8,128)} %collective-permute-done.22.refs_3_, f32[384,384]{1,0:T(8,128)} %copy-done.7, ...), custom_call_target="tpu_custom_call" | custom-call | flops 1 | bytes 1 | tf_op jit(solution)/shard_map/pallas_call | solution.py:62
  198.0 1.5 collective-permute-done.49.refs_5_
  199.6 0.7 copy-done.12
  200.5 8.4 %shard_map.72 = f32[4,256,512]{2,1,0:T(8,128)} custom-call(s32[5]{0:T(128)} %stack.23.where, f32[512,256]{1,0:T(8,128)} %get-tuple-element.65.refs_0_, f32[512,256]{1,0:T(8,128)} %collective-permute-done.26.refs_1_, f32[512,256]{1,0:T(8,128)} %collective-permute-done.27.refs_2_, f32[512,256]{1,0:T(8,128)} %copy-done.11, ...), custom_call_target="tpu_custom_call" | custom-call | flops 1 | bytes 1 | tf_op jit(solution)/shard_map/pallas_call | solution.py:62
  208.9 5.5 %all-to-all-start.1 = ((f32[4,256,512]{2,1,0:T(8,128)}), f32[4,256,512]{2,1,0:T(8,128)S(1)}, u32[]{:S(2)}, u32[]{:S(2)}) async-start(f32[4,256,512]{2,1,0:T(8,128)} %shard_map.72), calls=%async_computation.1 | async-start | bytes 4194304 | tf_op jit(solution)/shard_map/all_to_all | solution.py:314
  217.3 0.7 copy-done.33
  218.0 5.1 %shard_map.75 = (f32[384,384]{1,0:T(8,128)}, f32[384,384]{1,0:T(8,128)}) custom-call(s32[5]{0:T(128)} %stack.23.where, f32[384,384]{1,0:T(8,128)} %get-tuple-element.110.refs_0_, f32[384,384]{1,0:T(8,128)} %get-tuple-element.111.refs_1_, f32[384,128]{1,0:T(8,128)} %copy-done.24, f32[384,128]{1,0:T(8,128)} %copy-done.28, ...), custom_call_target="tpu_custom_call" | custom-call | flops 1 | bytes 1 | tf_op jit(solution)/shard_map/pallas_call | solution.py:62
  223.2 15.6 %collective-permute-done.54 = f32[384,384]{1,0:T(8,128)S(1)} collective-permute-done((f32[384,384]{1,0:T(8,128)}, f32[384,384]{1,0:T(8,128)S(1)}, u32[]{:S(2)}, u32[]{:S(2)}) %collective-permute-start.54) | collective-permute-done | bytes 589856 | tf_op jit(solution)/shard_map/ppermute | solution.py:25
  238.8 1.9 add_bitcast_fusion
  240.7 1.0 reduce_sum.19
  (153 shorter events, 7.6 us)
Async XLA Ops:
  7.2 33.7 %copy-start = (f32[1,384,384]{2,1,0:T(8,128)S(1)}, f32[1,384,384]{2,1,0:T(8,128)}, u32[]{:S(2)}) copy-start(f32[1,384,384]{2,1,0:T(8,128)} %param.7) | copy-start | bytes 1769476
  7.2 45.4 %copy-start.41 = (s32[2,1024]{1,0:T(2,128)S(1)}, s32[2,1024]{1,0:T(2,128)}, u32[]{:S(2)}) copy-start(s32[2,1024]{1,0:T(2,128)} %param.5) | copy-start | bytes 24580
  7.2 192.4 %all-gather.3.cloned.1.call-start = ((), (), s32[]{:S(2)}) async-start(), calls=%async_computation.2 | async-start | bytes 2621440 | tf_op jit(solution)/shard_map/all_gather | solution.py:245
  7.2 10.2 %collective-permute-start.3 = (f32[128,384]{1,0:T(8,128)}, f32[128,384]{1,0:T(8,128)S(1)}, u32[]{:S(2)}, u32[]{:S(2)}) collective-permute-start(f32[128,384]{1,0:T(8,128)} %bitcast.25), channel_id=1, source_target_pairs={{1,8},{8,1},{3,10},{10,3},{5,12},{12,5},{7,14},{14,7},{17,24},{24,... | collective-permute-start | bytes 589832 | tf_op jit(solution)/shard_map/ppermute | solution.py:243
  8.1 32.7 %collective-permute-start.11 = (f32[384,384]{1,0:T(8,128)}, f32[384,384]{1,0:T(8,128)S(1)}, u32[]{:S(2)}, u32[]{:S(2)}) collective-permute-start(f32[384,384]{1,0:T(8,128)} %bitcast.17), channel_id=1, source_target_pairs={{0,16},{16,32},{32,48},{48,0},{1,17},{17,33},{33,49},{49,1},{2,18}... | collective-permute-start | bytes 1769480 | tf_op jit(solution)/shard_map/ppermute | solution.py:17
  11.7 14.1 %collective-permute-start = (f32[512,256]{1,0:T(8,128)}, f32[512,256]{1,0:T(8,128)S(1)}, u32[]{:S(2)}, u32[]{:S(2)}) collective-permute-start(f32[512,256]{1,0:T(8,128)} %shard_map.67.refs_0_), channel_id=1, source_target_pairs={{0,2},{2,4},{4,6},{6,0},{1,3},{3,5},{5,7},{7,1},{8,10},{10,12},{12... | collective-permute-start | bytes 1572872 | tf_op jit(solution)/shard_map/ppermute | solution.py:17
  13.2 25.1 %collective-permute-start.1 = (f32[512,256]{1,0:T(8,128)}, f32[512,256]{1,0:T(8,128)}, u32[]{:S(2)}, u32[]{:S(2)}) collective-permute-start(f32[512,256]{1,0:T(8,128)} %shard_map.67.refs_0_), channel_id=1, source_target_pairs={{0,4},{2,6},{4,0},{6,2},{1,5},{3,7},{5,1},{7,3},{8,12},{10,14},{12... | collective-permute-start | bytes 1572872 | tf_op jit(solution)/shard_map/ppermute | solution.py:17
  16.1 22.8 %collective-permute-start.2 = (f32[512,256]{1,0:T(8,128)}, f32[512,256]{1,0:T(8,128)}, u32[]{:S(2)}, u32[]{:S(2)}) collective-permute-start(f32[512,256]{1,0:T(8,128)} %shard_map.67.refs_0_), channel_id=1, source_target_pairs={{0,6},{2,0},{4,2},{6,4},{1,7},{3,1},{5,3},{7,5},{8,14},{10,8},{12,... | collective-permute-start | bytes 1572872 | tf_op jit(solution)/shard_map/ppermute | solution.py:17
  17.5 23.4 %collective-permute-start.13 = (f32[384,384]{1,0:T(8,128)}, f32[384,384]{1,0:T(8,128)S(1)}, u32[]{:S(2)}, u32[]{:S(2)}) collective-permute-start(f32[384,384]{1,0:T(8,128)} %bitcast.18), channel_id=1, source_target_pairs={{0,48},{16,0},{32,16},{48,32},{1,49},{17,1},{33,17},{49,33},{2,50}... | collective-permute-start | bytes 1769480 | tf_op jit(solution)/shard_map/ppermute | solution.py:17
  20.2 53.9 %copy-start.4 = (f32[128,384]{1,0:T(8,128)}, f32[128,384]{1,0:T(8,128)S(1)}, u32[]{:S(2)}) copy-start(f32[128,384]{1,0:T(8,128)S(1)} %broadcast_select_fusion.refs_0_) | copy-start | bytes 589828
  39.0 3.9 %collective-permute-start.4 = (f32[512,256]{1,0:T(8,128)}, f32[512,256]{1,0:T(8,128)}, u32[]{:S(2)}, u32[]{:S(2)}) collective-permute-start(f32[512,256]{1,0:T(8,128)} %shard_map.67.refs_0_), channel_id=1, source_target_pairs={{0,1},{1,0},{2,3},{3,2},{4,5},{5,4},{6,7},{7,6},{8,9},{9,8},{10,11... | collective-permute-start | bytes 1572872 | tf_op jit(solution)/shard_map/ppermute | solution.py:25
  40.3 4.6 %collective-permute-start.5 = (f32[512,256]{1,0:T(8,128)S(1)}, f32[512,256]{1,0:T(8,128)}, u32[]{:S(2)}, u32[]{:S(2)}) collective-permute-start(f32[512,256]{1,0:T(8,128)S(1)} %collective-permute-done.refs_1_), channel_id=1, source_target_pairs={{0,1},{1,0},{2,3},{3,2},{4,5},{5,4},{6,7},{7,6},{8,9},{9,8},{10,11... | collective-permute-start | bytes 1572872 | tf_op jit(solution)/shard_map/ppermute | solution.py:25
  40.3 4.7 %collective-permute-start.6 = (f32[512,256]{1,0:T(8,128)}, f32[512,256]{1,0:T(8,128)}, u32[]{:S(2)}, u32[]{:S(2)}) collective-permute-start(f32[512,256]{1,0:T(8,128)} %collective-permute-done.1.refs_2_), channel_id=1, source_target_pairs={{0,1},{1,0},{2,3},{3,2},{4,5},{5,4},{6,7},{7,6},{8,9},{9,8},{10,11... | collective-permute-start | bytes 1572872 | tf_op jit(solution)/shard_map/ppermute | solution.py:25
  40.8 7.0 %collective-permute-start.7 = (f32[512,256]{1,0:T(8,128)}, f32[512,256]{1,0:T(8,128)}, u32[]{:S(2)}, u32[]{:S(2)}) collective-permute-start(f32[512,256]{1,0:T(8,128)} %collective-permute-done.2.refs_3_), channel_id=1, source_target_pairs={{0,1},{1,0},{2,3},{3,2},{4,5},{5,4},{6,7},{7,6},{8,9},{9,8},{10,11... | collective-permute-start | bytes 1572872 | tf_op jit(solution)/shard_map/ppermute | solution.py:25
  40.9 25.6 %collective-permute-start.12 = (f32[384,384]{1,0:T(8,128)S(1)}, f32[384,384]{1,0:T(8,128)S(1)}, u32[]{:S(2)}, u32[]{:S(2)}) collective-permute-start(f32[384,384]{1,0:T(8,128)S(1)} %bitcast.22), channel_id=1, source_target_pairs={{0,32},{16,48},{32,0},{48,16},{1,33},{17,49},{33,1},{49,17},{2,34}... | collective-permute-start | bytes 1769480 | tf_op jit(solution)/shard_map/ppermute | solution.py:17
  42.9 23.6 %collective-permute-start.10 = (f32[128,384]{1,0:T(8,128)S(1)}, f32[128,384]{1,0:T(8,128)S(1)}, u32[]{:S(2)}, u32[]{:S(2)}) collective-permute-start(f32[128,384]{1,0:T(8,128)S(1)} %broadcast_select_fusion.refs_0_), channel_id=1, source_target_pairs={{0,6},{2,0},{4,2},{6,4},{1,7},{3,1},{5,3},{7,5},{8,14},{10,8},{12,... | collective-permute-start | bytes 589832 | tf_op jit(solution)/shard_map/ppermute | solution.py:17
  44.9 21.6 %collective-permute-start.8 = (f32[128,384]{1,0:T(8,128)S(1)}, f32[128,384]{1,0:T(8,128)S(1)}, u32[]{:S(2)}, u32[]{:S(2)}) collective-permute-start(f32[128,384]{1,0:T(8,128)S(1)} %broadcast_select_fusion.refs_0_), channel_id=1, source_target_pairs={{0,2},{2,4},{4,6},{6,0},{1,3},{3,5},{5,7},{7,1},{8,10},{10,12},{12... | collective-permute-start | bytes 589832 | tf_op jit(solution)/shard_map/ppermute | solution.py:17
  45.0 21.5 %collective-permute-start.9 = (f32[128,384]{1,0:T(8,128)S(1)}, f32[128,384]{1,0:T(8,128)}, u32[]{:S(2)}, u32[]{:S(2)}) collective-permute-start(f32[128,384]{1,0:T(8,128)S(1)} %broadcast_select_fusion.refs_0_), channel_id=1, source_target_pairs={{0,4},{2,6},{4,0},{6,2},{1,5},{3,7},{5,1},{7,3},{8,12},{10,14},{12... | collective-permute-start | bytes 589832 | tf_op jit(solution)/shard_map/ppermute | solution.py:17
  47.8 36.6 %collective-permute-start.19 = (f32[384,384]{1,0:T(8,128)}, f32[384,384]{1,0:T(8,128)S(1)}, u32[]{:S(2)}, u32[]{:S(2)}) collective-permute-start(f32[384,384]{1,0:T(8,128)} %shard_map.68), channel_id=1, source_target_pairs={{0,0},{2,16},{4,32},{6,48},{16,2},{18,18},{20,34},{22,50},{32,4},{... | collective-permute-start | bytes 1769480 | tf_op jit(solution)/shard_map/ppermute | solution.py:233
  66.5 45.5 %all-to-all-start = ((f32[16,128,128]{2,1,0:T(8,128)}), f32[16,128,128]{2,1,0:T(8,128)S(1)}, u32[]{:S(2)}, u32[]{:S(2)}) async-start(f32[16,128,128]{2,1,0:T(8,128)} %get-tuple-element.73), calls=%async_computation | async-start | bytes 2097152 | tf_op jit(solution)/shard_map/all_to_all | solution.py:267
  74.1 10.2 %collective-permute-start.14 = (f32[128,384]{1,0:T(8,128)S(1)}, f32[128,384]{1,0:T(8,128)S(1)}, u32[]{:S(2)}, u32[]{:S(2)}) collective-permute-start(f32[128,384]{1,0:T(8,128)S(1)} %broadcast_select_fusion.refs_0_), channel_id=1, source_target_pairs={{0,1},{1,0},{2,3},{3,2},{4,5},{5,4},{6,7},{7,6},{8,9},{9,8},{10,11... | collective-permute-start | bytes 589832 | tf_op jit(solution)/shard_map/ppermute | solution.py:25
  74.2 16.8 %collective-permute-start.15 = (f32[128,384]{1,0:T(8,128)S(1)}, f32[128,384]{1,0:T(8,128)S(1)}, u32[]{:S(2)}, u32[]{:S(2)}) collective-permute-start(f32[128,384]{1,0:T(8,128)S(1)} %collective-permute-done.8.refs_1_), channel_id=1, source_target_pairs={{0,1},{1,0},{2,3},{3,2},{4,5},{5,4},{6,7},{7,6},{8,9},{9,8},{10,11... | collective-permute-start | bytes 589832 | tf_op jit(solution)/shard_map/ppermute | solution.py:25
  74.7 18.8 %collective-permute-start.16 = (f32[128,384]{1,0:T(8,128)}, f32[128,384]{1,0:T(8,128)}, u32[]{:S(2)}, u32[]{:S(2)}) collective-permute-start(f32[128,384]{1,0:T(8,128)} %collective-permute-done.9.refs_2_), channel_id=1, source_target_pairs={{0,1},{1,0},{2,3},{3,2},{4,5},{5,4},{6,7},{7,6},{8,9},{9,8},{10,11... | collective-permute-start | bytes 589832 | tf_op jit(solution)/shard_map/ppermute | solution.py:25
  74.8 18.7 %collective-permute-start.17 = (f32[128,384]{1,0:T(8,128)S(1)}, f32[128,384]{1,0:T(8,128)}, u32[]{:S(2)}, u32[]{:S(2)}) collective-permute-start(f32[128,384]{1,0:T(8,128)S(1)} %collective-permute-done.10.refs_3_), channel_id=1, source_target_pairs={{0,1},{1,0},{2,3},{3,2},{4,5},{5,4},{6,7},{7,6},{8,9},{9,8},{10,11... | collective-permute-start | bytes 589832 | tf_op jit(solution)/shard_map/ppermute | solution.py:25
  84.4 79.0 %copy-start.5 = (f32[384,384]{1,0:T(8,128)}, f32[384,384]{1,0:T(8,128)S(1)}, u32[]{:S(2)}) copy-start(f32[384,384]{1,0:T(8,128)S(1)} %collective-permute-done.19.refs_0_) | copy-start | bytes 1769476
  84.4 27.7 %collective-permute-start.20 = (f32[384,384]{1,0:T(8,128)S(1)}, f32[384,384]{1,0:T(8,128)S(1)}, u32[]{:S(2)}, u32[]{:S(2)}) collective-permute-start(f32[384,384]{1,0:T(8,128)S(1)} %collective-permute-done.19.refs_0_), channel_id=1, source_target_pairs={{0,2},{2,4},{4,6},{6,0},{1,3},{3,5},{5,7},{7,1},{8,10},{10,12},{12... | collective-permute-start | bytes 1769480 | tf_op jit(solution)/shard_map/ppermute | solution.py:17
  84.4 32.7 %collective-permute-start.21 = (f32[384,384]{1,0:T(8,128)S(1)}, f32[384,384]{1,0:T(8,128)}, u32[]{:S(2)}, u32[]{:S(2)}) collective-permute-start(f32[384,384]{1,0:T(8,128)S(1)} %collective-permute-done.19.refs_0_), channel_id=1, source_target_pairs={{0,4},{2,6},{4,0},{6,2},{1,5},{3,7},{5,1},{7,3},{8,12},{10,14},{12... | collective-permute-start | bytes 1769480 | tf_op jit(solution)/shard_map/ppermute | solution.py:17
  91.0 26.0 %collective-permute-start.22 = (f32[384,384]{1,0:T(8,128)S(1)}, f32[384,384]{1,0:T(8,128)}, u32[]{:S(2)}, u32[]{:S(2)}) collective-permute-start(f32[384,384]{1,0:T(8,128)S(1)} %collective-permute-done.19.refs_0_), channel_id=1, source_target_pairs={{0,6},{2,0},{4,2},{6,4},{1,7},{3,1},{5,3},{7,5},{8,14},{10,8},{12,... | collective-permute-start | bytes 1769480 | tf_op jit(solution)/shard_map/ppermute | solution.py:17
  98.7 10.4 %collective-permute-start.18 = (f32[256,384]{1,0:T(8,128)}, f32[256,384]{1,0:T(8,128)S(1)}, u32[]{:S(2)}, u32[]{:S(2)}) collective-permute-start(f32[256,384]{1,0:T(8,128)} %shard_map.70.refs_0_), channel_id=1, source_target_pairs={{0,8},{8,0},{1,9},{9,1},{2,10},{10,2},{3,11},{11,3},{4,12},{12,4},... | collective-permute-start | bytes 1179656 | tf_op jit(solution)/shard_map/ppermute | solution.py:25
  112.0 31.7 %copy-start.18 = (f32[128,128]{1,0:T(8,128)}, f32[128,128]{1,0:T(8,128)S(1)}, u32[]{:S(2)}) copy-start(f32[128,128]{1,0:T(8,128)S(1)} %reduce_sum.18.refs_0_) | copy-start | bytes 196612
  112.0 77.5 %copy-start.6 = (f32[384,384]{1,0:T(8,128)}, f32[384,384]{1,0:T(8,128)S(1)}, u32[]{:S(2)}) copy-start(f32[384,384]{1,0:T(8,128)S(1)} %collective-permute-done.20.refs_1_) | copy-start | bytes 1769476
  117.0 17.2 %collective-permute-start.36 = (f32[256,384]{1,0:T(8,128)}, f32[256,384]{1,0:T(8,128)S(1)}, u32[]{:S(2)}, u32[]{:S(2)}) collective-permute-start(f32[256,384]{1,0:T(8,128)} %get-tuple-element.92.refs_8_), channel_id=1, source_target_pairs={{0,16},{16,32},{32,48},{48,0},{1,17},{17,33},{33,49},{49,1},{2,18}... | collective-permute-start | bytes 1179656 | tf_op jit(solution)/shard_map/ppermute | solution.py:17
  117.5 17.3 %collective-permute-start.37 = (f32[256,384]{1,0:T(8,128)}, f32[256,384]{1,0:T(8,128)S(1)}, u32[]{:S(2)}, u32[]{:S(2)}) collective-permute-start(f32[256,384]{1,0:T(8,128)} %get-tuple-element.92.refs_8_), channel_id=1, source_target_pairs={{0,32},{16,48},{32,0},{48,16},{1,33},{17,49},{33,1},{49,17},{2,34}... | collective-permute-start | bytes 1179656 | tf_op jit(solution)/shard_map/ppermute | solution.py:17
  121.8 16.7 %collective-permute-start.38 = (f32[256,384]{1,0:T(8,128)}, f32[256,384]{1,0:T(8,128)S(1)}, u32[]{:S(2)}, u32[]{:S(2)}) collective-permute-start(f32[256,384]{1,0:T(8,128)} %get-tuple-element.92.refs_8_), channel_id=1, source_target_pairs={{0,48},{16,0},{32,16},{48,32},{1,49},{17,1},{33,17},{49,33},{2,50}... | collective-permute-start | bytes 1179656 | tf_op jit(solution)/shard_map/ppermute | solution.py:17
  124.4 5.5 %collective-permute-start.23 = (f32[128,128]{1,0:T(8,128)S(1)}, f32[128,128]{1,0:T(8,128)S(1)}, u32[]{:S(2)}, u32[]{:S(2)}) collective-permute-start(f32[128,128]{1,0:T(8,128)S(1)} %reduce_sum.18.refs_0_), channel_id=1, source_target_pairs={{0,2},{2,4},{4,6},{6,0},{1,3},{3,5},{5,7},{7,1},{8,10},{10,12},{12... | collective-permute-start | bytes 196616 | tf_op jit(solution)/shard_map/ppermute | solution.py:17
  124.7 6.6 %collective-permute-start.24 = (f32[128,128]{1,0:T(8,128)S(1)}, f32[128,128]{1,0:T(8,128)S(1)}, u32[]{:S(2)}, u32[]{:S(2)}) collective-permute-start(f32[128,128]{1,0:T(8,128)S(1)} %reduce_sum.18.refs_0_), channel_id=1, source_target_pairs={{0,4},{2,6},{4,0},{6,2},{1,5},{3,7},{5,1},{7,3},{8,12},{10,14},{12... | collective-permute-start | bytes 196616 | tf_op jit(solution)/shard_map/ppermute | solution.py:17
  130.0 4.3 %collective-permute-start.25 = (f32[128,128]{1,0:T(8,128)S(1)}, f32[128,128]{1,0:T(8,128)S(1)}, u32[]{:S(2)}, u32[]{:S(2)}) collective-permute-start(f32[128,128]{1,0:T(8,128)S(1)} %reduce_sum.18.refs_0_), channel_id=1, source_target_pairs={{0,6},{2,0},{4,2},{6,4},{1,7},{3,1},{5,3},{7,5},{8,14},{10,8},{12,... | collective-permute-start | bytes 196616 | tf_op jit(solution)/shard_map/ppermute | solution.py:17
  131.3 12.4 %collective-permute-start.32 = (f32[128,128]{1,0:T(8,128)S(1)}, f32[128,128]{1,0:T(8,128)S(1)}, u32[]{:S(2)}, u32[]{:S(2)}) collective-permute-start(f32[128,128]{1,0:T(8,128)S(1)} %reduce_sum.18.refs_0_), channel_id=1, source_target_pairs={{0,1},{1,0},{2,3},{3,2},{4,5},{5,4},{6,7},{7,6},{8,9},{9,8},{10,11... | collective-permute-start | bytes 196616 | tf_op jit(solution)/shard_map/ppermute | solution.py:25
  134.2 9.5 %collective-permute-start.33 = (f32[128,128]{1,0:T(8,128)S(1)}, f32[128,128]{1,0:T(8,128)S(1)}, u32[]{:S(2)}, u32[]{:S(2)}) collective-permute-start(f32[128,128]{1,0:T(8,128)S(1)} %collective-permute-done.23.refs_1_), channel_id=1, source_target_pairs={{0,1},{1,0},{2,3},{3,2},{4,5},{5,4},{6,7},{7,6},{8,9},{9,8},{10,11... | collective-permute-start | bytes 196616 | tf_op jit(solution)/shard_map/ppermute | solution.py:25
  134.3 9.5 %collective-permute-start.34 = (f32[128,128]{1,0:T(8,128)S(1)}, f32[128,128]{1,0:T(8,128)S(1)}, u32[]{:S(2)}, u32[]{:S(2)}) collective-permute-start(f32[128,128]{1,0:T(8,128)S(1)} %collective-permute-done.24.refs_2_), channel_id=1, source_target_pairs={{0,1},{1,0},{2,3},{3,2},{4,5},{5,4},{6,7},{7,6},{8,9},{9,8},{10,11... | collective-permute-start | bytes 196616 | tf_op jit(solution)/shard_map/ppermute | solution.py:25
  134.8 9.0 %collective-permute-start.35 = (f32[128,128]{1,0:T(8,128)S(1)}, f32[128,128]{1,0:T(8,128)S(1)}, u32[]{:S(2)}, u32[]{:S(2)}) collective-permute-start(f32[128,128]{1,0:T(8,128)S(1)} %collective-permute-done.25.refs_3_), channel_id=1, source_target_pairs={{0,1},{1,0},{2,3},{3,2},{4,5},{5,4},{6,7},{7,6},{8,9},{9,8},{10,11... | collective-permute-start | bytes 196616 | tf_op jit(solution)/shard_map/ppermute | solution.py:25
  138.5 18.4 %collective-permute-start.46 = (f32[384,128]{1,0:T(8,128)}, f32[384,128]{1,0:T(8,128)S(1)}, u32[]{:S(2)}, u32[]{:S(2)}) collective-permute-start(f32[384,128]{1,0:T(8,128)} %get-tuple-element.105), channel_id=1, source_target_pairs={{0,0},{2,16},{4,32},{6,48},{16,2},{18,18},{20,34},{22,50},{32,4},{... | collective-permute-start | bytes 589832 | tf_op jit(solution)/shard_map/ppermute | solution.py:233
  148.7 10.7 %collective-permute-start.43 = (f32[128,384]{1,0:T(8,128)}, f32[128,384]{1,0:T(8,128)S(1)}, u32[]{:S(2)}, u32[]{:S(2)}) collective-permute-start(f32[128,384]{1,0:T(8,128)} %shard_map.73.refs_10_), channel_id=1, source_target_pairs={{0,16},{16,32},{32,48},{48,0},{1,17},{17,33},{33,49},{49,1},{2,18}... | collective-permute-start | bytes 589832 | tf_op jit(solution)/shard_map/ppermute | solution.py:17
  149.9 25.4 %collective-permute-start.28 = (f32[512,256]{1,0:T(8,128)}, f32[512,256]{1,0:T(8,128)S(1)}, u32[]{:S(2)}, u32[]{:S(2)}) collective-permute-start(f32[512,256]{1,0:T(8,128)} %get-tuple-element.90), channel_id=1, source_target_pairs={{0,72},{8,0},{64,8},{72,64},{1,73},{9,1},{65,9},{73,65},{2,74},{10... | collective-permute-start | bytes 1572872 | tf_op jit(solution)/shard_map/ppermute | solution.py:21
  152.4 22.9 %collective-permute-start.27 = (f32[512,256]{1,0:T(8,128)}, f32[512,256]{1,0:T(8,128)}, u32[]{:S(2)}, u32[]{:S(2)}) collective-permute-start(f32[512,256]{1,0:T(8,128)} %get-tuple-element.88), channel_id=1, source_target_pairs={{0,64},{8,72},{64,0},{72,8},{1,65},{9,73},{65,1},{73,9},{2,66},{10... | collective-permute-start | bytes 1572872 | tf_op jit(solution)/shard_map/ppermute | solution.py:21
  153.8 9.5 %collective-permute-start.44 = (f32[128,384]{1,0:T(8,128)}, f32[128,384]{1,0:T(8,128)S(1)}, u32[]{:S(2)}, u32[]{:S(2)}) collective-permute-start(f32[128,384]{1,0:T(8,128)} %shard_map.73.refs_10_), channel_id=1, source_target_pairs={{0,32},{16,48},{32,0},{48,16},{1,33},{17,49},{33,1},{49,17},{2,34}... | collective-permute-start | bytes 589832 | tf_op jit(solution)/shard_map/ppermute | solution.py:17
  156.9 9.5 %collective-permute-start.45 = (f32[128,384]{1,0:T(8,128)}, f32[128,384]{1,0:T(8,128)}, u32[]{:S(2)}, u32[]{:S(2)}) collective-permute-start(f32[128,384]{1,0:T(8,128)} %shard_map.73.refs_10_), channel_id=1, source_target_pairs={{0,48},{16,0},{32,16},{48,32},{1,49},{17,1},{33,17},{49,33},{2,50}... | collective-permute-start | bytes 589832 | tf_op jit(solution)/shard_map/ppermute | solution.py:17
  159.4 19.6 %collective-permute-start.26 = (f32[512,256]{1,0:T(8,128)}, f32[512,256]{1,0:T(8,128)}, u32[]{:S(2)}, u32[]{:S(2)}) collective-permute-start(f32[512,256]{1,0:T(8,128)} %get-tuple-element.86), channel_id=1, source_target_pairs={{0,8},{8,64},{64,72},{72,0},{1,9},{9,65},{65,73},{73,1},{2,10},{10... | collective-permute-start | bytes 1572872 | tf_op jit(solution)/shard_map/ppermute | solution.py:21
  163.4 23.6 %collective-permute-start.39 = (f32[384,384]{1,0:T(8,128)S(1)}, f32[384,384]{1,0:T(8,128)S(1)}, u32[]{:S(2)}, u32[]{:S(2)}) collective-permute-start(f32[384,384]{1,0:T(8,128)S(1)} %collective-permute-done.19.refs_0_), channel_id=1, source_target_pairs={{0,1},{1,0},{2,3},{3,2},{4,5},{5,4},{6,7},{7,6},{8,9},{9,8},{10,11... | collective-permute-start | bytes 1769480 | tf_op jit(solution)/shard_map/ppermute | solution.py:25
  166.4 21.2 %collective-permute-start.40 = (f32[384,384]{1,0:T(8,128)S(1)}, f32[384,384]{1,0:T(8,128)S(1)}, u32[]{:S(2)}, u32[]{:S(2)}) collective-permute-start(f32[384,384]{1,0:T(8,128)S(1)} %collective-permute-done.20.refs_1_), channel_id=1, source_target_pairs={{0,1},{1,0},{2,3},{3,2},{4,5},{5,4},{6,7},{7,6},{8,9},{9,8},{10,11... | collective-permute-start | bytes 1769480 | tf_op jit(solution)/shard_map/ppermute | solution.py:25
  175.3 12.4 %collective-permute-start.41 = (f32[384,384]{1,0:T(8,128)}, f32[384,384]{1,0:T(8,128)S(1)}, u32[]{:S(2)}, u32[]{:S(2)}) collective-permute-start(f32[384,384]{1,0:T(8,128)} %collective-permute-done.21.refs_2_), channel_id=1, source_target_pairs={{0,1},{1,0},{2,3},{3,2},{4,5},{5,4},{6,7},{7,6},{8,9},{9,8},{10,11... | collective-permute-start | bytes 1769480 | tf_op jit(solution)/shard_map/ppermute | solution.py:25
  175.3 12.6 %collective-permute-start.42 = (f32[384,384]{1,0:T(8,128)}, f32[384,384]{1,0:T(8,128)}, u32[]{:S(2)}, u32[]{:S(2)}) collective-permute-start(f32[384,384]{1,0:T(8,128)} %collective-permute-done.22.refs_3_), channel_id=1, source_target_pairs={{0,1},{1,0},{2,3},{3,2},{4,5},{5,4},{6,7},{7,6},{8,9},{9,8},{10,11... | collective-permute-start | bytes 1769480 | tf_op jit(solution)/shard_map/ppermute | solution.py:25
  179.0 8.0 %collective-permute-start.47 = (f32[384,128]{1,0:T(8,128)S(1)}, f32[384,128]{1,0:T(8,128)S(1)}, u32[]{:S(2)}, u32[]{:S(2)}) collective-permute-start(f32[384,128]{1,0:T(8,128)S(1)} %collective-permute-done.46.refs_2_), channel_id=1, source_target_pairs={{0,2},{2,4},{4,6},{6,0},{1,3},{3,5},{5,7},{7,1},{8,10},{10,12},{12... | collective-permute-start | bytes 589832 | tf_op jit(solution)/shard_map/ppermute | solution.py:17
  187.0 12.6 %collective-permute-start.31 = (f32[512,256]{1,0:T(8,128)S(1)}, f32[512,256]{1,0:T(8,128)}, u32[]{:S(2)}, u32[]{:S(2)}) collective-permute-start(f32[512,256]{1,0:T(8,128)S(1)} %collective-permute-done.28.refs_3_), channel_id=1, source_target_pairs={{0,1},{1,0},{2,3},{3,2},{4,5},{5,4},{6,7},{7,6},{8,9},{9,8},{10,11... | collective-permute-start | bytes 1572872 | tf_op jit(solution)/shard_map/ppermute | solution.py:25
  187.0 12.5 %collective-permute-start.30 = (f32[512,256]{1,0:T(8,128)}, f32[512,256]{1,0:T(8,128)S(1)}, u32[]{:S(2)}, u32[]{:S(2)}) collective-permute-start(f32[512,256]{1,0:T(8,128)} %collective-permute-done.27.refs_2_), channel_id=1, source_target_pairs={{0,1},{1,0},{2,3},{3,2},{4,5},{5,4},{6,7},{7,6},{8,9},{9,8},{10,11... | collective-permute-start | bytes 1572872 | tf_op jit(solution)/shard_map/ppermute | solution.py:25
  187.6 12.0 %collective-permute-start.29 = (f32[512,256]{1,0:T(8,128)}, f32[512,256]{1,0:T(8,128)S(1)}, u32[]{:S(2)}, u32[]{:S(2)}) collective-permute-start(f32[512,256]{1,0:T(8,128)} %collective-permute-done.26.refs_1_), channel_id=1, source_target_pairs={{0,1},{1,0},{2,3},{3,2},{4,5},{5,4},{6,7},{7,6},{8,9},{9,8},{10,11... | collective-permute-start | bytes 1572872 | tf_op jit(solution)/shard_map/ppermute | solution.py:25
  187.7 10.3 %collective-permute-start.48 = (f32[384,128]{1,0:T(8,128)}, f32[384,128]{1,0:T(8,128)}, u32[]{:S(2)}, u32[]{:S(2)}) collective-permute-start(f32[384,128]{1,0:T(8,128)} %copy-done.24), channel_id=1, source_target_pairs={{0,4},{2,6},{4,0},{6,2},{1,5},{3,7},{5,1},{7,3},{8,12},{10,14},{12... | collective-permute-start | bytes 589832 | tf_op jit(solution)/shard_map/ppermute | solution.py:17
  187.9 11.7 %collective-permute-start.49 = (f32[384,128]{1,0:T(8,128)}, f32[384,128]{1,0:T(8,128)}, u32[]{:S(2)}, u32[]{:S(2)}) collective-permute-start(f32[384,128]{1,0:T(8,128)} %copy-done.24), channel_id=1, source_target_pairs={{0,6},{2,0},{4,2},{6,4},{1,7},{3,1},{5,3},{7,5},{8,14},{10,8},{12,... | collective-permute-start | bytes 589832 | tf_op jit(solution)/shard_map/ppermute | solution.py:17
  208.9 31.8 %all-to-all-start.1 = ((f32[4,256,512]{2,1,0:T(8,128)}), f32[4,256,512]{2,1,0:T(8,128)S(1)}, u32[]{:S(2)}, u32[]{:S(2)}) async-start(f32[4,256,512]{2,1,0:T(8,128)} %shard_map.72), calls=%async_computation.1 | async-start | bytes 4194304 | tf_op jit(solution)/shard_map/all_to_all | solution.py:314
  214.4 1.4 collective-permute-start.50
  214.4 1.7 collective-permute-start.51
  214.9 1.7 collective-permute-start.52
  215.0 1.9 collective-permute-start.53
  223.1 15.8 %collective-permute-start.54 = (f32[384,384]{1,0:T(8,128)}, f32[384,384]{1,0:T(8,128)S(1)}, u32[]{:S(2)}, u32[]{:S(2)}) collective-permute-start(f32[384,384]{1,0:T(8,128)} %get-tuple-element.118), channel_id=1, source_target_pairs={{0,8},{8,0},{1,9},{9,1},{2,10},{10,2},{3,11},{11,3},{4,12},{12,4},... | collective-permute-start | bytes 1769480 | tf_op jit(solution)/shard_map/ppermute | solution.py:25
  (36 other events, 372.3 us)
Sparse Core Ops, SparseCore 0:
  42.2 32.9 all-gather.2
where the time goes:
time: 250 us; the launch traced here: 249 us
  waiting for transfers between devices  95.7 us (38%)
  starting transfers between devices  80.5 us (32%)
  Pallas kernels  49.4 us (20%)
  between operations  14.6 us (6%)
  local copies, waits for them, and re-layouts  5.3 us (2%)
  other arithmetic  3.14 us (1%)
    ppermute x24, waiting for transfers between devices, along(): return lax.ppermute(value, axis, [(i, (i + step) % 4) for i in range(4)])  47.3 us
    ppermute x24, starting transfers between devices, along(): return lax.ppermute(value, axis, [(i, (i + step) % 4) for i in range(4)])  44.2 us
    pallas_call x6, Pallas kernels, call(): pl.pallas_call(kernel, out_shape=list(outs), in_specs=[smem] * (1 + len(i...  43.1 us
    ppermute x25, waiting for transfers between devices, other(): return lax.ppermute(value, axis, [(0, 1), (1, 0)])  27.2 us
    ppermute x3, waiting for transfers between devices, along_z(): lax.ppermute(value, ('sub', 'zl'), [(i, (i + step) % 4) for i in range(4)])  12 us
    ppermute x2, starting transfers between devices, swap_xy(): return lax.ppermute(value, ('x', 'y'), pairs)  9.94 us
    ppermute x2, waiting for transfers between devices, swap_xy(): return lax.ppermute(value, ('x', 'y'), pairs)  9.13 us
    all_to_all x1, starting transfers between devices, on_device(): cov = lax.all_to_all(part, ROWS, 0, 0).sum(0)  7.61 us
  transfers between devices with their start and end apart: 58, of which 22 were waited for; matrix products, arithmetic and copies ran while one was open for 1% of the time, Pallas kernels for 17%

commit v1 on v0

--- a/solution.py
+++ b/solution.py
@@ -112,17 +112,24 @@
 
 
 def cross_kernel(where, *refs):
-    covs, factors, out, (held, right, sems) = refs[:8], refs[8:12], refs[12], refs[13:]
+    covs, factors, mine, out, sent = refs[:8], refs[8:12], refs[12:16], refs[16], refs[17:21]
+    held, right, turned, sems = refs[21:]
     sub, x, zl, y, core = spot(where)
     depth = right.shape[0] // 4
     pairs = [(c, held.at[i]) for i, c in enumerate(covs)]
     pairs += [(f, right.at[pl.ds(i * depth, depth)]) for i, f in enumerate(factors)]
+    pairs += [(p, turned.at[(y - x - e + 8) % 4]) for e, p in enumerate(mine)]
     finish(fetch(pairs, sems))
 
     def block(i):
         return held[(y - x + i // 2 + 8) % 4 + jnp.where(core == i % 2, 0, 4)]
 
-    out[...] = -product(jnp.concatenate([block(i) for i in range(8)], 1), right[...], 1, 0)
+    cross = -product(jnp.concatenate([block(i) for i in range(8)], 1), right[...], 1, 0)
+    out[...] = cross
+    rows = out.shape[0]
+    for d in range(4):
+        sent[d][:rows] = cross
+        sent[d][rows:] = turned[d]
 
 
 def factor_kernel(where, *refs):
@@ -139,30 +146,29 @@
     out[...] = product(both, right[...].reshape(both.shape[1], out.shape[1]), 1, 0)
 
 
-def whole_kernel(where, *refs):
-    mine, came, both, turned = refs
+def whole_kernel(where, mine, came, both, own):
     total = mine[...] + came[...]
     both[...] = total
-    rows = turned.shape[1]
+    rows = own.shape[0]
 
     @pl.when(where[2] == 0)
     def _():
-        turned[...] = total[:rows].T
+        own[...] = total[:rows]
 
     @pl.when(where[2] == 1)
     def _():
-        turned[...] = total[rows:].T
-
-
-def fetch_left(lefts, left, core, zl, y):
+        own[...] = total[rows:]
+
+
+def fetch_left(lefts, left, core, zl, at):
     mine = jnp.where(core == zl, 0, 1)
-    return [(p, left.at[(mine + i // 4) % 2, (y - i % 4 + 4) % 4]) for i, p in enumerate(lefts)]
+    return [(p, left.at[(mine + i // 4) % 2, (at - i % 4 + 4) % 4]) for i, p in enumerate(lefts)]
 
 
 def gram_kernel(where, *refs):
     lefts, rights, (keep, send), (left, right, sems) = refs[:8], refs[8:12], refs[12:14], refs[14:]
     sub, x, zl, y, core = spot(where)
-    pairs = fetch_left(lefts, left, core, zl, y)
+    pairs = fetch_left(lefts, left, core, zl, x)
     pairs += [(v, right.at[(x - i + 4) % 4]) for i, v in enumerate(rights)]
     finish(fetch(pairs, sems))
     depth = right.shape[0] * right.shape[1]
@@ -172,16 +178,29 @@
 
 
 def update_kernel(where, *refs):
-    keep_gram, send_gram, refs = refs[0], refs[1], refs[2:]
-    lefts, rights, (keep, send), (left, right, sems) = refs[:8], refs[8:12], refs[12:14], refs[14:]
-    sub, x, zl, y, core = spot(where)
-    pairs = fetch_left(lefts, left, core, zl, y)
-    pairs += [(v, right.at[(x - i + 4) % 4]) for i, v in enumerate(rights)]
-    finish(fetch(pairs + [(keep_gram, keep), (send_gram, send)], sems))
-    depth = right.shape[0] * right.shape[1]
+    keep_gram, send_gram, near, far = refs[0], refs[1], refs[2:6], refs[6:10]
+    keep, send, left, right, sems = refs[10:]
+    sub, x, zl, y, core = spot(where)
+    mine = jnp.where(core == zl, 0, 1)
+    rows = right.shape[1]
+    pairs = [(keep_gram, keep), (send_gram, send)]
+    for d in range(4):
+        place = (x - d + 4) % 4
+        pairs.append((near[d].at[pl.ds(0, rows)], right.at[place]))
+        pairs.append((near[d].at[pl.ds(rows, rows)], left.at[mine, place]))
+        pairs.append((far[d].at[pl.ds(rows, rows)], left.at[1 - mine, place]))
+    finish(fetch(pairs, sems))
+    straight = right[...].reshape(4 * rows, right.shape[2])
     for slot, out in ((1, send), (0, keep)):
-        both = jnp.concatenate([left[slot, i] for i in range(4)], 1)
-        out[...] = out[...] - product(both, right[...].reshape(depth, right.shape[2]), 1, 0)
+        both = left[slot].reshape(4 * rows, left.shape[3])
+        out[...] = out[...] - product(both, straight, 0, 0)
+
+
+def turn_kernel(where, *refs):
+    stack, outs, (held, sems) = refs[0], refs[1:5], refs[5:]
+    sub, x, zl, y, core = spot(where)
+    finish(fetch([(stack.at[(x + d) % 4], held.at[d]) for d in range(4)], sems))
+    finish(fetch([(held.at[d], outs[d]) for d in range(4)], sems))
 
 
 def flip_kernel(value, out):
@@ -191,15 +210,15 @@
 def top_kernel(where, *refs):
     lefts, rights, out, (left, right, sems) = refs[:8], refs[8], refs[9], refs[10:]
     sub, x, zl, y, core = spot(where)
-    depth = right.shape[0] // 4
-    pairs = [(p, left.at[(core + i // 4) % 2, i % 4]) for i, p in enumerate(lefts)]
-    for i in range(4):
-        pairs.append((rights.at[(2 * sub + zl - i + 4) % 4], right.at[pl.ds(i * depth, depth)]))
-    finish(fetch(pairs, sems))
+    pairs = [
+        (p, left.at[(core + i // 4) % 2, (2 * sub + zl - i % 4 + 4) % 4])
+        for i, p in enumerate(lefts)
+    ]
+    finish(fetch(pairs + [(rights, right)], sems))
     rows = out.shape[1]
     for parity in range(2):
         both = jnp.concatenate([left[parity, i] for i in range(4)], 1)
-        total = product(both, right[...], 1, 0)
+        total = product(both, right[...].reshape(both.shape[1], out.shape[2]), 1, 0)
         for h in range(2):
             out[2 * h + parity] = total[h * rows : (h + 1) * rows]
 
@@ -228,10 +247,6 @@
             cost_estimate=pl.CostEstimate(flops=1, bytes_accessed=1, transcendentals=0),
         )(value)
 
-    def swap_xy(value):
-        pairs = [(4 * a + b, 4 * b + a) for a in range(4) for b in range(4)]
-        return lax.ppermute(value, ("x", "y"), pairs)
-
     def over_y(value):
         return [value] + [along(value, "y", e) for e in (1, 2, 3)]
 
@@ -241,17 +256,15 @@
     stripes = over_y(flipped(top_inverse))
     flip = [(2 * a + c, 2 * (1 - a) + (1 - c)) for a in (0, 1) for c in (0, 1) if a != c]
     panel = jnp.where(core == zl, panel, lax.ppermute(panel, ("zl", "core"), flip))
-    inverse_x = {0: inverse} | {d: along(inverse, "x", d) for d in (1, 3)}
+    inverse_x = [inverse] + [along(inverse, "x", d) for d in (1, 2, 3)]
+    inverse_t = flipped(inverse)
     top_z = lax.all_gather(top_inverse, ("sub", "zl"), axis=0)
-    inverse_t = flipped(inverse)
-    stripes, panel, inverse_t, inverse = lax.optimization_barrier(
-        (stripes, panel, inverse_t, inverse)
-    )
-
+    stripes, panel, inverse_x, inverse_t = lax.optimization_barrier(
+        (stripes, panel, inverse_x, inverse_t)
+    )
+
+    inverse_y = lax.all_gather(inverse_t, "y", axis=0)
     panels = over_y(panel)
-    inverse_x[2] = along(inverse, "x", 2)
-    inverse_x = [inverse_x[d] for d in range(4)]
-    inverse_t = swap_xy(inverse_t)
     owner = ancestors // block
     place = (y - owner // 2) % 4 + jnp.where(owner % 2 == core, 0, 4)
     index = (place * block + ancestors % block).reshape(-1)
@@ -260,8 +273,8 @@
         [shape(16, share, share)] + [shape(block, stripe)] * 5,
         [vmem(8 * block, stripe), vmem(2 * order, stripe)], 10, (index,), (1, 2, 3, 4, 5),
     )
-    part, own1, own2, own3, panels, inverse_x = lax.optimization_barrier(
-        (part, own1, own2, own3, panels, inverse_x)
+    part, own1, own2, own3, panels, top_z = lax.optimization_barrier(
+        (part, own1, own2, own3, panels, top_z)
     )
 
     cov = lax.all_to_all(part, ROWS, 0, 0).sum(0)
@@ -269,49 +282,55 @@
         factor_kernel, where, both_cores(panels) + inverse_x,
         [shape(2 * rows, width)], [vmem(2, 4, rows, width), vmem(4, width, width)], 12,
     )
-    factor, factor_t = pl.pallas_call(
+    turned = call(
+        turn_kernel, where, [after(inverse_y, factor_part)], [shape(width, width)] * 4,
+        [vmem(4, width, width)], 4, (), (0, 1, 2, 3),
+    )
+    inverse_columns = [turned[0]] + [along(turned[d], "x", d) for d in (1, 2, 3)]
+    factor, factor_own = pl.pallas_call(
         whole_kernel,
-        out_shape=[shape(2 * rows, width), shape(width, rows)],
+        out_shape=[shape(2 * rows, width), shape(rows, width)],
         in_specs=[pl.BlockSpec(memory_space=pltpu.SMEM)]
         + [pl.BlockSpec(memory_space=pltpu.VMEM)] * 2,
         out_specs=[pl.BlockSpec(memory_space=pltpu.VMEM)] * 2,
         compiler_params=pltpu.CompilerParams(vmem_limit_bytes=VMEM_BYTES),
         cost_estimate=pl.CostEstimate(flops=1, bytes_accessed=1, transcendentals=0),
     )(where, factor_part, other(factor_part, "zl"))
-    inverse_columns = over_y(inverse_t)
-    cov, factor, factor_t, inverse_columns = lax.optimization_barrier(
-        (cov, factor, factor_t, inverse_columns)
+    cov_y = over_y(cov)
+    cov_y, factor, factor_own, own1, own2, own3, inverse_columns[0] = lax.optimization_barrier(
+        (cov_y, factor, factor_own, own1, own2, own3, inverse_columns[0])
     )
 
     factor_x = [factor] + [along(factor, "x", d) for d in (1, 2, 3)]
-    cov_y = over_y(cov)
-    (cross,) = call(
-        cross_kernel, where, both_cores(cov_y) + factor_x, [shape(rows, width)],
-        [vmem(8, rows, share), vmem(8 * rows, width)], 12,
-    )
-    own = [along_z(after(v, *cov_y), d + 1) for d, v in enumerate((own1, own2, own3))]
-    factor_t = swap_xy(after(factor_t, factor_x[1], factor_x[2], factor_x[3]))
-    cross, inverse_columns = lax.optimization_barrier((cross, inverse_columns))
-
-    cross_x = [cross] + [along(cross, "x", d) for d in (1, 2, 3)]
-    factor_columns = over_y(factor_t)
-    there = [there0] + [other(v, "core") for v in own]
-    (top_part,) = call(
-        top_kernel, where, [own0] + own + there + [top_z], [shape(4, stripe, block)],
-        [vmem(2, 4, block, stripe), vmem(4 * stripe, block)], 12,
-    )
+    own = [own0] + [along_z(v, d + 1) for d, v in enumerate((own1, own2, own3))]
+    factor_y = over_y(factor_own)
     grams = call(
         gram_kernel, where, both_cores(inverse_columns) + inverse_x, [shape(width, width)] * 2,
         [vmem(2, 4, width, width), vmem(4, width, width)], 12,
     )
-    grams, cross_x, factor_columns = lax.optimization_barrier((grams, cross_x, factor_columns))
-
+    cov_y[0] = after(cov_y[0], grams[0])
+    cross, *sent = call(
+        cross_kernel, where, both_cores(cov_y) + factor_x + factor_y,
+        [shape(rows, width)] + [shape(2 * rows, width)] * 4,
+        [vmem(8, rows, share), vmem(8 * rows, width), vmem(4, rows, width)], 16,
+    )
+    cross, sent, grams, own = lax.optimization_barrier((cross, sent, grams, own))
+
+    near = [sent[0]] + [along(sent[d], "x", d) for d in (1, 2, 3)]
+    there = [there0] + [other(v, "core") for v in own[1:]]
+    (top_part,) = call(
+        top_kernel, where, own + there + [top_z], [shape(4, stripe, block)],
+        [vmem(2, 4, block, stripe), vmem(4, stripe, block)], 9,
+    )
+    near, top_part = lax.optimization_barrier((near, top_part))
+
+    far = [other(v, "core") for v in near]
     block_keep, block_send = call(
-        update_kernel, where, list(grams) + both_cores(factor_columns) + cross_x,
-        [shape(width, width)] * 2, [vmem(2, 4, width, rows), vmem(4, rows, width)], 14,
+        update_kernel, where, list(grams) + near + far, [shape(width, width)] * 2,
+        [vmem(2, 4, rows, width), vmem(4, rows, width)], 14,
     )
     child_block = block_keep + other(block_send, "zl")
-    top_block = lax.all_to_all(after(top_part, *cross_x[1:]), "x", 0, 0).sum(0)
+    top_block = lax.all_to_all(top_part, "x", 0, 0).sum(0)
     return top_block, cross[None], child_block[None]
 
 

time: 250 us -> 223 us (0.89)
  waiting for transfers between devices: 95.7 us -> 77.2 us
  starting transfers between devices: 80.5 us -> 66.7 us
  Pallas kernels: 49.4 us -> 53.9 us
    ppermute x3, waiting for transfers between devices: 12 us -> 0.01 us  [along_z(): lax.ppermute(value, ('sub', 'zl'), [(i, (i + step) % 4) for i in range(4)])]
    ppermute x2 -> x0, starting transfers between devices: 9.94 us -> none  [swap_xy(): return lax.ppermute(value, ('x', 'y'), pairs)]
    ppermute x2 -> x0, waiting for transfers between devices: 9.13 us -> none  [swap_xy(): return lax.ppermute(value, ('x', 'y'), pairs)]
    ppermute x24, waiting for transfers between devices: 47.3 us -> 54.1 us  [along(): return lax.ppermute(value, axis, [(i, (i + step) % 4) for i in range(4)])]
    ppermute x25, waiting for transfers between devices: 27.2 us -> 22.4 us  [other(): return lax.ppermute(value, axis, [(0, 1), (1, 0)])]
    pallas_call x6 -> x7, Pallas kernels: 43.1 us -> 47.6 us  [call(): pl.pallas_call(kernel, out_shape=list(outs), in_specs=[smem] * (1 + len(i...]
    ppermute x24, starting transfers between devices: 44.2 us -> 40.7 us  [along(): return lax.ppermute(value, axis, [(i, (i + step) % 4) for i in range(4)])]
    unnamed x85 -> x87, local copies, waits for them, and re-layouts: 4.64 us -> 5.73 us
  transfers between devices with their start and end apart: 58 -> 57, of which waited for: 22 -> 25; matrix products, arithmetic and copies ran while one was open for 1% -> 2% of each run, Pallas kernels for 17% -> 24%
where the time goes in v1:
time: 223 us
  waiting for transfers between devices  77.2 us (35%)
  starting transfers between devices  66.7 us (30%)
  Pallas kernels  53.9 us (24%)
  between operations  14.5 us (7%)
  local copies, waits for them, and re-layouts  6.39 us (3%)
  other arithmetic  4.06 us (2%)
    ppermute x24, waiting for transfers between devices, along(): return lax.ppermute(value, axis, [(i, (i + step) % 4) for i in range(4)])  54.1 us
    pallas_call x7, Pallas kernels, call(): pl.pallas_call(kernel, out_shape=list(outs), in_specs=[smem] * (1 + len(i...  47.6 us
    ppermute x24, starting transfers between devices, along(): return lax.ppermute(value, axis, [(i, (i + step) % 4) for i in range(4)])  40.7 us
    ppermute x25, waiting for transfers between devices, other(): return lax.ppermute(value, axis, [(0, 1), (1, 0)])  22.4 us
    all_to_all x1, starting transfers between devices, on_device(): cov = lax.all_to_all(part, ROWS, 0, 0).sum(0)  8.57 us
    ppermute x25, starting transfers between devices, other(): return lax.ppermute(value, axis, [(0, 1), (1, 0)])  7.2 us
    unnamed x87, local copies, waits for them, and re-layouts  5.73 us
    ppermute x3, starting transfers between devices, along_z(): lax.ppermute(value, ('sub', 'zl'), [(i, (i + step) % 4) for i in range(4)])  5.3 us
  transfers between devices with their start and end apart: 57, of which 25 were waited for; matrix products, arithmetic and copies ran while one was open for 2% of the time, Pallas kernels for 24%

profile of v1, /device:TPU:2, one launch (start us, length us, event | category | flops | bytes accessed | tf_op | source)
XLA Modules:
  0.0 222.7 jit_solution(8460296574757064269)
XLA Ops:
  7.2 0.7 all-gather.5.cloned.1.call-update
  8.0 2.0 shard_map.67.refs_0_
  10.0 1.6 collective-permute-start
  11.6 0.7 collective-permute-start.3
  12.2 1.6 collective-permute-start.4
  13.8 1.1 collective-permute-start.5
  14.9 2.2 collective-permute-start.6
  17.1 2.9 %collective-permute-start.1 = (f32[512,256]{1,0:T(8,128)}, f32[512,256]{1,0:T(8,128)S(1)}, u32[]{:S(2)}, u32[]{:S(2)}) collective-permute-start(f32[512,256]{1,0:T(8,128)} %shard_map.67.refs_0_), channel_id=1, source_target_pairs={{0,4},{2,6},{4,0},{6,2},{1,5},{3,7},{5,1},{7,3},{8,12},{10,14},{12... | collective-permute-start | bytes 1572872 | tf_op jit(solution)/shard_map/ppermute | solution.py:17
  20.0 5.3 %collective-permute-done.refs_1_ = f32[512,256]{1,0:T(8,128)S(1)} collective-permute-done((f32[512,256]{1,0:T(8,128)}, f32[512,256]{1,0:T(8,128)S(1)}, u32[]{:S(2)}, u32[]{:S(2)}) %collective-permute-start) | collective-permute-done | bytes 524320 | tf_op jit(solution)/shard_map/ppermute | solution.py:17
  25.2 2.8 %collective-permute-start.2 = (f32[512,256]{1,0:T(8,128)}, f32[512,256]{1,0:T(8,128)}, u32[]{:S(2)}, u32[]{:S(2)}) collective-permute-start(f32[512,256]{1,0:T(8,128)} %shard_map.67.refs_0_), channel_id=1, source_target_pairs={{0,6},{2,0},{4,2},{6,4},{1,7},{3,1},{5,3},{7,5},{8,14},{10,8},{12,... | collective-permute-start | bytes 1572872 | tf_op jit(solution)/shard_map/ppermute | solution.py:17
  28.0 2.2 shard_map.68
  30.2 1.0 broadcast_select_fusion.refs_0_
  31.2 6.4 %collective-permute-done.1.refs_2_ = f32[512,256]{1,0:T(8,128)S(1)} collective-permute-done((f32[512,256]{1,0:T(8,128)}, f32[512,256]{1,0:T(8,128)S(1)}, u32[]{:S(2)}, u32[]{:S(2)}) %collective-permute-start.1) | collective-permute-done | bytes 524320 | tf_op jit(solution)/shard_map/ppermute | solution.py:17
  37.6 5.3 %collective-permute-done.2.refs_3_ = f32[512,256]{1,0:T(8,128)} collective-permute-done((f32[512,256]{1,0:T(8,128)}, f32[512,256]{1,0:T(8,128)}, u32[]{:S(2)}, u32[]{:S(2)}) %collective-permute-start.2) | collective-permute-done | bytes 524320 | tf_op jit(solution)/shard_map/ppermute | solution.py:17
  44.5 3.1 %collective-permute-start.11 = (f32[128,384]{1,0:T(8,128)S(1)}, f32[128,384]{1,0:T(8,128)}, u32[]{:S(2)}, u32[]{:S(2)}) collective-permute-start(f32[128,384]{1,0:T(8,128)S(1)} %broadcast_select_fusion.refs_0_), channel_id=1, source_target_pairs={{0,2},{2,4},{4,6},{6,0},{1,3},{3,5},{5,7},{7,1},{8,10},{10,12},{12... | collective-permute-start | bytes 589832 | tf_op jit(solution)/shard_map/ppermute | solution.py:17
  47.7 2.3 %collective-permute-start.12 = (f32[128,384]{1,0:T(8,128)S(1)}, f32[128,384]{1,0:T(8,128)S(1)}, u32[]{:S(2)}, u32[]{:S(2)}) collective-permute-start(f32[128,384]{1,0:T(8,128)S(1)} %broadcast_select_fusion.refs_0_), channel_id=1, source_target_pairs={{0,4},{2,6},{4,0},{6,2},{1,5},{3,7},{5,1},{7,3},{8,12},{10,14},{12... | collective-permute-start | bytes 589832 | tf_op jit(solution)/shard_map/ppermute | solution.py:17
  50.0 1.6 collective-permute-start.13
  52.3 0.7 stack.23.where
  53.0 12.5 %shard_map.69 = (f32[16,128,128]{2,1,0:T(8,128)}, f32[512,256]{1,0:T(8,128)}, f32[512,256]{1,0:T(8,128)}, f32[512,256]{1,0:T(8,128)}, f32[512,256]{1,0:T(8,128)}, /*index=5*/f32[512,256]{1,0:T(8,128)}) custom-call(s32[5]{0:T(128)} %stack.23.where, s32[2048]{0:T(1024)} %bitcast.27, f32[512,256]{1,0:T(8,128)} %shard_map.67.refs_0_, f32[512,256]{1,0:T(8,128)} %copy-done.12, ...), custom_call_target="tpu_custom_call" | custom-call | flops 1 | bytes 1 | tf_op jit(solution)/shard_map/pallas_call | solution.py:62
  65.6 8.6 %all-to-all-start = ((f32[16,128,128]{2,1,0:T(8,128)}), f32[16,128,128]{2,1,0:T(8,128)S(1)}, u32[]{:S(2)}, u32[]{:S(2)}) async-start(f32[16,128,128]{2,1,0:T(8,128)} %get-tuple-element.80), calls=%async_computation | async-start | bytes 2097152 | tf_op jit(solution)/shard_map/all_to_all | solution.py:280
  76.9 0.7 copy-done.32
  77.6 5.1 %shard_map.70.mine = f32[256,384]{1,0:T(8,128)} custom-call(s32[5]{0:T(128)} %stack.23.where, f32[128,384]{1,0:T(8,128)} %copy-done.4, f32[128,384]{1,0:T(8,128)} %collective-permute-done.11.refs_1_, f32[128,384]{1,0:T(8,128)} %copy-done.27, f32[128,384]{1,0:T(8,128)} %copy-done.28, f32[128,384]{1,0:T(8,128)} %copy-done.29, f32[128,384]{1,0:T(8,128)} %copy-done.30, ...), custom_call_target="tpu_custom_call" | custom-call | flops 1 | bytes 1 | tf_op jit(solution)/shard_map/pallas_call | solution.py:62
  82.7 1.5 collective-permute-start.21
  84.3 3.8 %shard_map.72 = (f32[384,384]{1,0:T(8,128)}, f32[384,384]{1,0:T(8,128)}, f32[384,384]{1,0:T(8,128)}, f32[384,384]{1,0:T(8,128)}) custom-call(s32[5]{0:T(128)} %stack.23.where, f32[4,384,384]{2,1,0:T(8,128)} %bitcast.24), custom_call_target="tpu_custom_call" | custom-call | flops 1 | bytes 1 | tf_op jit(solution)/shard_map/pallas_call | solution.py:62
  88.1 1.5 collective-permute-start.22
  89.6 1.2 collective-permute-start.23
  91.1 2.1 collective-permute-start.24
  93.2 2.5 %collective-permute-done.21.came = f32[256,384]{1,0:T(8,128)S(1)} collective-permute-done((f32[256,384]{1,0:T(8,128)}, f32[256,384]{1,0:T(8,128)S(1)}, u32[]{:S(2)}, u32[]{:S(2)}) %collective-permute-start.21) | collective-permute-done | bytes 393248 | tf_op jit(solution)/shard_map/ppermute | solution.py:25
  96.4 2.2 collective-permute-start.16
  98.6 2.0 shard_map.71
  100.6 0.9 collective-permute-done.15.refs_2_
  102.0 0.7 collective-permute-done.30.refs_5_
  103.1 1.0 collective-permute-start.36
  104.0 2.9 %collective-permute-start.37 = (f32[128,384]{1,0:T(8,128)}, f32[128,384]{1,0:T(8,128)}, u32[]{:S(2)}, u32[]{:S(2)}) collective-permute-start(f32[128,384]{1,0:T(8,128)} %get-tuple-element.108.refs_12_), channel_id=1, source_target_pairs={{0,4},{2,6},{4,0},{6,2},{1,5},{3,7},{5,1},{7,3},{8,12},{10,14},{12... | collective-permute-start | bytes 589832 | tf_op jit(solution)/shard_map/ppermute | solution.py:17
  106.9 4.6 %collective-permute-done.36.refs_13_ = f32[128,384]{1,0:T(8,128)S(1)} collective-permute-done((f32[128,384]{1,0:T(8,128)}, f32[128,384]{1,0:T(8,128)S(1)}, u32[]{:S(2)}, u32[]{:S(2)}) %collective-permute-start.36) | collective-permute-done | bytes 196640 | tf_op jit(solution)/shard_map/ppermute | solution.py:17
  111.5 1.9 collective-permute-start.38
  113.4 3.2 %collective-permute-done.37.refs_14_ = f32[128,384]{1,0:T(8,128)} collective-permute-done((f32[128,384]{1,0:T(8,128)}, f32[128,384]{1,0:T(8,128)}, u32[]{:S(2)}, u32[]{:S(2)}) %collective-permute-start.37) | collective-permute-done | bytes 196640 | tf_op jit(solution)/shard_map/ppermute | solution.py:17
  117.3 1.1 collective-permute-done.24.refs_3_
  118.5 1.1 collective-permute-start.33
  119.6 10.7 %collective-permute-done.33.refs_9_ = f32[256,384]{1,0:T(8,128)S(1)} collective-permute-done((f32[256,384]{1,0:T(8,128)}, f32[256,384]{1,0:T(8,128)S(1)}, u32[]{:S(2)}, u32[]{:S(2)}) %collective-permute-start.33) | collective-permute-done | bytes 393248 | tf_op jit(solution)/shard_map/ppermute | solution.py:17
  130.8 2.9 %collective-permute-start.40 = (f32[512,256]{1,0:T(8,128)}, f32[512,256]{1,0:T(8,128)}, u32[]{:S(2)}, u32[]{:S(2)}) collective-permute-start(f32[512,256]{1,0:T(8,128)} %get-tuple-element.117), channel_id=1, source_target_pairs={{0,64},{8,72},{64,0},{72,8},{1,65},{9,73},{65,1},{73,9},{2,66},{10... | collective-permute-start | bytes 1572872 | tf_op jit(solution)/shard_map/ppermute | solution.py:21
  133.8 1.8 collective-permute-start.41
  135.5 1.6 collective-permute-start.34
  137.1 0.8 copy-done.11
  137.9 1.5 collective-permute-start.35
  139.5 8.5 %shard_map.73 = (f32[384,384]{1,0:T(8,128)}, f32[384,384]{1,0:T(8,128)}) custom-call(s32[5]{0:T(128)} %stack.23.where, f32[384,384]{1,0:T(8,128)} %get-tuple-element.98.refs_0_, f32[384,384]{1,0:T(8,128)} %copy-done.5, f32[384,384]{1,0:T(8,128)} %copy-done.6, f32[384,384]{1,0:T(8,128)} %copy-done.7, f32[384,384]{1,0:T(8,128)} %copy-done.8, ...), custom_call_target="tpu_custom_call" | custom-call | flops 1 | bytes 1 | tf_op jit(solution)/shard_map/pallas_call | solution.py:62
  147.9 1.5 collective-permute-done.34.refs_10_
  149.5 6.2 %collective-permute-done.35.refs_11_ = f32[256,384]{1,0:T(8,128)} collective-permute-done((f32[256,384]{1,0:T(8,128)}, f32[256,384]{1,0:T(8,128)}, u32[]{:S(2)}, u32[]{:S(2)}) %collective-permute-start.35) | collective-permute-done | bytes 393248 | tf_op jit(solution)/shard_map/ppermute | solution.py:17
  156.3 4.5 %shard_map.74 = (f32[128,384]{1,0:T(8,128)}, f32[256,384]{1,0:T(8,128)}, f32[256,384]{1,0:T(8,128)}, f32[256,384]{1,0:T(8,128)}, f32[256,384]{1,0:T(8,128)}) custom-call(s32[5]{0:T(128)} %stack.23.where, f32[128,128]{1,0:T(8,128)} %copy-done.26, f32[128,128]{1,0:T(8,128)} %copy-done.35, f32[128,128]{1,0:T(8,128)} %copy-done.36, f32[128,128]{1,0:T(8,128)} %copy-done.37, ...), custom_call_target="tpu_custom_call" | custom-call | flops 1 | bytes 1 | tf_op jit(solution)/shard_map/pallas_call | solution.py:62
  162.1 1.6 collective-permute-start.43
  163.6 2.0 collective-permute-start.44
  165.7 0.8 copy-done.15
  166.7 8.4 %shard_map.75 = f32[4,256,512]{2,1,0:T(8,128)} custom-call(s32[5]{0:T(128)} %stack.23.where, f32[512,256]{1,0:T(8,128)} %get-tuple-element.123.refs_0_, f32[512,256]{1,0:T(8,128)} %collective-permute-done.39.refs_1_, f32[512,256]{1,0:T(8,128)} %collective-permute-done.40.refs_2_, f32[512,256]{1,0:T(8,128)} %collective-permute-done.41.refs_3_, ...), custom_call_target="tpu_custom_call" | custom-call | flops 1 | bytes 1 | tf_op jit(solution)/shard_map/pallas_call | solution.py:62
  175.1 0.7 collective-permute-done.43.refs_4_
  175.8 7.4 %collective-permute-done.44.refs_5_ = f32[256,384]{1,0:T(8,128)S(1)} collective-permute-done((f32[256,384]{1,0:T(8,128)}, f32[256,384]{1,0:T(8,128)S(1)}, u32[]{:S(2)}, u32[]{:S(2)}) %collective-permute-start.44) | collective-permute-done | bytes 393248 | tf_op jit(solution)/shard_map/ppermute | solution.py:17
  183.2 0.7 copy-done.21
  183.9 4.2 %all-to-all-start.1 = ((f32[4,256,512]{2,1,0:T(8,128)}), f32[4,256,512]{2,1,0:T(8,128)S(1)}, u32[]{:S(2)}, u32[]{:S(2)}) async-start(f32[4,256,512]{2,1,0:T(8,128)} %shard_map.75), calls=%async_computation.1 | async-start | bytes 4194304 | tf_op jit(solution)/shard_map/all_to_all | solution.py:333
  189.2 0.7 collective-permute-done.48.refs_6_
  190.4 1.1 collective-permute-done.50.refs_8_
  191.5 0.8 copy-done.24
  192.3 5.0 %shard_map.76 = (f32[384,384]{1,0:T(8,128)}, f32[384,384]{1,0:T(8,128)}) custom-call(s32[5]{0:T(128)} %stack.23.where, f32[384,384]{1,0:T(8,128)} %get-tuple-element.131.refs_0_, f32[384,384]{1,0:T(8,128)} %get-tuple-element.132.refs_1_, f32[256,384]{1,0:T(8,128)} %get-tuple-element.133.refs_2_, f32[256,384]{1,0:T(8,128)} %copy-done.19, ...), custom_call_target="tpu_custom_call" | custom-call | flops 1 | bytes 1 | tf_op jit(solution)/shard_map/pallas_call | solution.py:62
  197.6 15.3 %collective-permute-done.52 = f32[384,384]{1,0:T(8,128)S(1)} collective-permute-done((f32[384,384]{1,0:T(8,128)}, f32[384,384]{1,0:T(8,128)S(1)}, u32[]{:S(2)}, u32[]{:S(2)}) %collective-permute-start.52) | collective-permute-done | bytes 589856 | tf_op jit(solution)/shard_map/ppermute | solution.py:25
  212.9 1.9 add_bitcast_fusion
  214.9 1.0 reduce_sum.19
  (155 shorter events, 12.6 us)
Async XLA Ops:
  7.2 44.5 %copy-start.42 = (s32[2,1024]{1,0:T(2,128)S(1)}, s32[2,1024]{1,0:T(2,128)}, u32[]{:S(2)}) copy-start(s32[2,1024]{1,0:T(2,128)} %param.5) | copy-start | bytes 24580
  7.2 58.4 %all-gather.5.cloned.1.call-start = ((), (), s32[]{:S(2)}) async-start(), calls=%async_computation.2 | async-start | bytes 2621440 | tf_op jit(solution)/shard_map/all_gather | solution.py:261
  7.9 76.4 %all-gather.7.cloned.1.call-start = ((), (), s32[]{:S(2)}) async-start(), calls=%async_computation.3 | async-start | bytes 2949120 | tf_op jit(solution)/shard_map/all_gather | solution.py:266
  10.0 33.4 %copy-start.3 = (f32[512,256]{1,0:T(8,128)S(1)}, f32[512,256]{1,0:T(8,128)}, u32[]{:S(2)}) copy-start(f32[512,256]{1,0:T(8,128)} %shard_map.67.refs_0_) | copy-start | bytes 1572868
  10.0 15.2 %collective-permute-start = (f32[512,256]{1,0:T(8,128)}, f32[512,256]{1,0:T(8,128)S(1)}, u32[]{:S(2)}, u32[]{:S(2)}) collective-permute-start(f32[512,256]{1,0:T(8,128)} %shard_map.67.refs_0_), channel_id=1, source_target_pairs={{0,2},{2,4},{4,6},{6,0},{1,3},{3,5},{5,7},{7,1},{8,10},{10,12},{12... | collective-permute-start | bytes 1572872 | tf_op jit(solution)/shard_map/ppermute | solution.py:17
  11.6 5.5 %collective-permute-start.3 = (f32[128,384]{1,0:T(8,128)}, f32[128,384]{1,0:T(8,128)S(1)}, u32[]{:S(2)}, u32[]{:S(2)}) collective-permute-start(f32[128,384]{1,0:T(8,128)} %bitcast.26), channel_id=1, source_target_pairs={{1,8},{8,1},{3,10},{10,3},{5,12},{12,5},{7,14},{14,7},{17,24},{24,... | collective-permute-start | bytes 589832 | tf_op jit(solution)/shard_map/ppermute | solution.py:258
  12.2 30.7 %collective-permute-start.4 = (f32[384,384]{1,0:T(8,128)}, f32[384,384]{1,0:T(8,128)S(1)}, u32[]{:S(2)}, u32[]{:S(2)}) collective-permute-start(f32[384,384]{1,0:T(8,128)} %bitcast.18), channel_id=1, source_target_pairs={{0,16},{16,32},{32,48},{48,0},{1,17},{17,33},{33,49},{49,1},{2,18}... | collective-permute-start | bytes 1769480 | tf_op jit(solution)/shard_map/ppermute | solution.py:17
  13.8 29.1 %collective-permute-start.5 = (f32[384,384]{1,0:T(8,128)}, f32[384,384]{1,0:T(8,128)S(1)}, u32[]{:S(2)}, u32[]{:S(2)}) collective-permute-start(f32[384,384]{1,0:T(8,128)} %bitcast.19), channel_id=1, source_target_pairs={{0,32},{16,48},{32,0},{48,16},{1,33},{17,49},{33,1},{49,17},{2,34}... | collective-permute-start | bytes 1769480 | tf_op jit(solution)/shard_map/ppermute | solution.py:17
  14.9 28.5 %collective-permute-start.6 = (f32[384,384]{1,0:T(8,128)}, f32[384,384]{1,0:T(8,128)S(1)}, u32[]{:S(2)}, u32[]{:S(2)}) collective-permute-start(f32[384,384]{1,0:T(8,128)} %bitcast.20), channel_id=1, source_target_pairs={{0,48},{16,0},{32,16},{48,32},{1,49},{17,1},{33,17},{49,33},{2,50}... | collective-permute-start | bytes 1769480 | tf_op jit(solution)/shard_map/ppermute | solution.py:17
  17.1 20.5 %collective-permute-start.1 = (f32[512,256]{1,0:T(8,128)}, f32[512,256]{1,0:T(8,128)S(1)}, u32[]{:S(2)}, u32[]{:S(2)}) collective-permute-start(f32[512,256]{1,0:T(8,128)} %shard_map.67.refs_0_), channel_id=1, source_target_pairs={{0,4},{2,6},{4,0},{6,2},{1,5},{3,7},{5,1},{7,3},{8,12},{10,14},{12... | collective-permute-start | bytes 1572872 | tf_op jit(solution)/shard_map/ppermute | solution.py:17
  25.2 27.7 %copy-start.12 = (f32[512,256]{1,0:T(8,128)}, f32[512,256]{1,0:T(8,128)S(1)}, u32[]{:S(2)}) copy-start(f32[512,256]{1,0:T(8,128)S(1)} %collective-permute-done.refs_1_) | copy-start | bytes 1572868
  25.2 17.6 %collective-permute-start.2 = (f32[512,256]{1,0:T(8,128)}, f32[512,256]{1,0:T(8,128)}, u32[]{:S(2)}, u32[]{:S(2)}) collective-permute-start(f32[512,256]{1,0:T(8,128)} %shard_map.67.refs_0_), channel_id=1, source_target_pairs={{0,6},{2,0},{4,2},{6,4},{1,7},{3,1},{5,3},{7,5},{8,14},{10,8},{12,... | collective-permute-start | bytes 1572872 | tf_op jit(solution)/shard_map/ppermute | solution.py:17
  31.2 43.0 %copy-start.4 = (f32[128,384]{1,0:T(8,128)}, f32[128,384]{1,0:T(8,128)S(1)}, u32[]{:S(2)}) copy-start(f32[128,384]{1,0:T(8,128)S(1)} %broadcast_select_fusion.refs_0_) | copy-start | bytes 589828
  43.4 4.2 %collective-permute-start.7 = (f32[512,256]{1,0:T(8,128)S(1)}, f32[512,256]{1,0:T(8,128)}, u32[]{:S(2)}, u32[]{:S(2)}) collective-permute-start(f32[512,256]{1,0:T(8,128)S(1)} %copy-done.3), channel_id=1, source_target_pairs={{0,1},{1,0},{2,3},{3,2},{4,5},{5,4},{6,7},{7,6},{8,9},{9,8},{10,11... | collective-permute-start | bytes 1572872 | tf_op jit(solution)/shard_map/ppermute | solution.py:25
  43.9 6.1 %collective-permute-start.8 = (f32[512,256]{1,0:T(8,128)S(1)}, f32[512,256]{1,0:T(8,128)}, u32[]{:S(2)}, u32[]{:S(2)}) collective-permute-start(f32[512,256]{1,0:T(8,128)S(1)} %collective-permute-done.refs_1_), channel_id=1, source_target_pairs={{0,1},{1,0},{2,3},{3,2},{4,5},{5,4},{6,7},{7,6},{8,9},{9,8},{10,11... | collective-permute-start | bytes 1572872 | tf_op jit(solution)/shard_map/ppermute | solution.py:25
  44.0 8.9 %collective-permute-start.9 = (f32[512,256]{1,0:T(8,128)S(1)}, f32[512,256]{1,0:T(8,128)}, u32[]{:S(2)}, u32[]{:S(2)}) collective-permute-start(f32[512,256]{1,0:T(8,128)S(1)} %collective-permute-done.1.refs_2_), channel_id=1, source_target_pairs={{0,1},{1,0},{2,3},{3,2},{4,5},{5,4},{6,7},{7,6},{8,9},{9,8},{10,11... | collective-permute-start | bytes 1572872 | tf_op jit(solution)/shard_map/ppermute | solution.py:25
  44.4 8.5 %collective-permute-start.10 = (f32[512,256]{1,0:T(8,128)}, f32[512,256]{1,0:T(8,128)}, u32[]{:S(2)}, u32[]{:S(2)}) collective-permute-start(f32[512,256]{1,0:T(8,128)} %collective-permute-done.2.refs_3_), channel_id=1, source_target_pairs={{0,1},{1,0},{2,3},{3,2},{4,5},{5,4},{6,7},{7,6},{8,9},{9,8},{10,11... | collective-permute-start | bytes 1572872 | tf_op jit(solution)/shard_map/ppermute | solution.py:25
  44.5 21.0 %collective-permute-start.11 = (f32[128,384]{1,0:T(8,128)S(1)}, f32[128,384]{1,0:T(8,128)}, u32[]{:S(2)}, u32[]{:S(2)}) collective-permute-start(f32[128,384]{1,0:T(8,128)S(1)} %broadcast_select_fusion.refs_0_), channel_id=1, source_target_pairs={{0,2},{2,4},{4,6},{6,0},{1,3},{3,5},{5,7},{7,1},{8,10},{10,12},{12... | collective-permute-start | bytes 589832 | tf_op jit(solution)/shard_map/ppermute | solution.py:17
  47.7 17.8 %collective-permute-start.12 = (f32[128,384]{1,0:T(8,128)S(1)}, f32[128,384]{1,0:T(8,128)S(1)}, u32[]{:S(2)}, u32[]{:S(2)}) collective-permute-start(f32[128,384]{1,0:T(8,128)S(1)} %broadcast_select_fusion.refs_0_), channel_id=1, source_target_pairs={{0,4},{2,6},{4,0},{6,2},{1,5},{3,7},{5,1},{7,3},{8,12},{10,14},{12... | collective-permute-start | bytes 589832 | tf_op jit(solution)/shard_map/ppermute | solution.py:17
  50.0 15.5 %collective-permute-start.13 = (f32[128,384]{1,0:T(8,128)S(1)}, f32[128,384]{1,0:T(8,128)S(1)}, u32[]{:S(2)}, u32[]{:S(2)}) collective-permute-start(f32[128,384]{1,0:T(8,128)S(1)} %broadcast_select_fusion.refs_0_), channel_id=1, source_target_pairs={{0,6},{2,0},{4,2},{6,4},{1,7},{3,1},{5,3},{7,5},{8,14},{10,8},{12,... | collective-permute-start | bytes 589832 | tf_op jit(solution)/shard_map/ppermute | solution.py:17
  65.6 25.2 %all-to-all-start = ((f32[16,128,128]{2,1,0:T(8,128)}), f32[16,128,128]{2,1,0:T(8,128)S(1)}, u32[]{:S(2)}, u32[]{:S(2)}) async-start(f32[16,128,128]{2,1,0:T(8,128)} %get-tuple-element.80), calls=%async_computation | async-start | bytes 2097152 | tf_op jit(solution)/shard_map/all_to_all | solution.py:280
  74.2 1.5 collective-permute-start.17
  74.2 1.9 collective-permute-start.18
  74.7 1.5 collective-permute-start.19
  74.8 1.7 collective-permute-start.20
  82.7 12.9 %collective-permute-start.21 = (f32[256,384]{1,0:T(8,128)}, f32[256,384]{1,0:T(8,128)S(1)}, u32[]{:S(2)}, u32[]{:S(2)}) collective-permute-start(f32[256,384]{1,0:T(8,128)} %shard_map.70.mine), channel_id=1, source_target_pairs={{0,8},{8,0},{1,9},{9,1},{2,10},{10,2},{3,11},{11,3},{4,12},{12,4},... | collective-permute-start | bytes 1179656 | tf_op jit(solution)/shard_map/ppermute | solution.py:25
  88.1 28.6 %collective-permute-start.22 = (f32[384,384]{1,0:T(8,128)}, f32[384,384]{1,0:T(8,128)S(1)}, u32[]{:S(2)}, u32[]{:S(2)}) collective-permute-start(f32[384,384]{1,0:T(8,128)} %get-tuple-element.99), channel_id=1, source_target_pairs={{0,16},{16,32},{32,48},{48,0},{1,17},{17,33},{33,49},{49,1},{2,18}... | collective-permute-start | bytes 1769480 | tf_op jit(solution)/shard_map/ppermute | solution.py:17
  89.6 27.6 %collective-permute-start.23 = (f32[384,384]{1,0:T(8,128)}, f32[384,384]{1,0:T(8,128)S(1)}, u32[]{:S(2)}, u32[]{:S(2)}) collective-permute-start(f32[384,384]{1,0:T(8,128)} %get-tuple-element.100), channel_id=1, source_target_pairs={{0,32},{16,48},{32,0},{48,16},{1,33},{17,49},{33,1},{49,17},{2,34}... | collective-permute-start | bytes 1769480 | tf_op jit(solution)/shard_map/ppermute | solution.py:17
  90.8 64.8 %copy-start.26 = (f32[128,128]{1,0:T(8,128)}, f32[128,128]{1,0:T(8,128)S(1)}, u32[]{:S(2)}) copy-start(f32[128,128]{1,0:T(8,128)S(1)} %reduce_sum.18.refs_0_) | copy-start | bytes 196612
  90.8 5.5 %collective-permute-start.14 = (f32[128,128]{1,0:T(8,128)S(1)}, f32[128,128]{1,0:T(8,128)S(1)}, u32[]{:S(2)}, u32[]{:S(2)}) collective-permute-start(f32[128,128]{1,0:T(8,128)S(1)} %reduce_sum.18.refs_0_), channel_id=1, source_target_pairs={{0,2},{2,4},{4,6},{6,0},{1,3},{3,5},{5,7},{7,1},{8,10},{10,12},{12... | collective-permute-start | bytes 196616 | tf_op jit(solution)/shard_map/ppermute | solution.py:17
  91.1 27.4 %collective-permute-start.24 = (f32[384,384]{1,0:T(8,128)}, f32[384,384]{1,0:T(8,128)S(1)}, u32[]{:S(2)}, u32[]{:S(2)}) collective-permute-start(f32[384,384]{1,0:T(8,128)} %get-tuple-element.101), channel_id=1, source_target_pairs={{0,48},{16,0},{32,16},{48,32},{1,49},{17,1},{33,17},{49,33},{2,50}... | collective-permute-start | bytes 1769480 | tf_op jit(solution)/shard_map/ppermute | solution.py:17
  95.7 5.8 %collective-permute-start.15 = (f32[128,128]{1,0:T(8,128)S(1)}, f32[128,128]{1,0:T(8,128)S(1)}, u32[]{:S(2)}, u32[]{:S(2)}) collective-permute-start(f32[128,128]{1,0:T(8,128)S(1)} %reduce_sum.18.refs_0_), channel_id=1, source_target_pairs={{0,4},{2,6},{4,0},{6,2},{1,5},{3,7},{5,1},{7,3},{8,12},{10,14},{12... | collective-permute-start | bytes 196616 | tf_op jit(solution)/shard_map/ppermute | solution.py:17
  96.4 51.5 %copy-start.35 = (f32[128,128]{1,0:T(8,128)}, f32[128,128]{1,0:T(8,128)S(1)}, u32[]{:S(2)}) copy-start(f32[128,128]{1,0:T(8,128)S(1)} %collective-permute-done.14.refs_1_) | copy-start | bytes 196612
  96.4 5.1 %collective-permute-start.16 = (f32[128,128]{1,0:T(8,128)S(1)}, f32[128,128]{1,0:T(8,128)S(1)}, u32[]{:S(2)}, u32[]{:S(2)}) collective-permute-start(f32[128,128]{1,0:T(8,128)S(1)} %reduce_sum.18.refs_0_), channel_id=1, source_target_pairs={{0,6},{2,0},{4,2},{6,4},{1,7},{3,1},{5,3},{7,5},{8,14},{10,8},{12,... | collective-permute-start | bytes 196616 | tf_op jit(solution)/shard_map/ppermute | solution.py:17
  101.5 1.3 collective-permute-start.30
  101.5 1.5 collective-permute-start.31
  102.8 1.3 collective-permute-start.32
  103.1 8.5 %collective-permute-start.36 = (f32[128,384]{1,0:T(8,128)}, f32[128,384]{1,0:T(8,128)S(1)}, u32[]{:S(2)}, u32[]{:S(2)}) collective-permute-start(f32[128,384]{1,0:T(8,128)} %get-tuple-element.108.refs_12_), channel_id=1, source_target_pairs={{0,2},{2,4},{4,6},{6,0},{1,3},{3,5},{5,7},{7,1},{8,10},{10,12},{12... | collective-permute-start | bytes 589832 | tf_op jit(solution)/shard_map/ppermute | solution.py:17
  104.0 12.6 %collective-permute-start.37 = (f32[128,384]{1,0:T(8,128)}, f32[128,384]{1,0:T(8,128)}, u32[]{:S(2)}, u32[]{:S(2)}) collective-permute-start(f32[128,384]{1,0:T(8,128)} %get-tuple-element.108.refs_12_), channel_id=1, source_target_pairs={{0,4},{2,6},{4,0},{6,2},{1,5},{3,7},{5,1},{7,3},{8,12},{10,14},{12... | collective-permute-start | bytes 589832 | tf_op jit(solution)/shard_map/ppermute | solution.py:17
  111.5 7.0 %collective-permute-start.38 = (f32[128,384]{1,0:T(8,128)}, f32[128,384]{1,0:T(8,128)}, u32[]{:S(2)}, u32[]{:S(2)}) collective-permute-start(f32[128,384]{1,0:T(8,128)} %get-tuple-element.108.refs_12_), channel_id=1, source_target_pairs={{0,6},{2,0},{4,2},{6,4},{1,7},{3,1},{5,3},{7,5},{8,14},{10,8},{12,... | collective-permute-start | bytes 589832 | tf_op jit(solution)/shard_map/ppermute | solution.py:17
  116.6 14.2 %collective-permute-start.25 = (f32[384,384]{1,0:T(8,128)}, f32[384,384]{1,0:T(8,128)S(1)}, u32[]{:S(2)}, u32[]{:S(2)}) collective-permute-start(f32[384,384]{1,0:T(8,128)} %get-tuple-element.98.refs_0_), channel_id=1, source_target_pairs={{0,1},{1,0},{2,3},{3,2},{4,5},{5,4},{6,7},{7,6},{8,9},{9,8},{10,11... | collective-permute-start | bytes 1769480 | tf_op jit(solution)/shard_map/ppermute | solution.py:25
  116.7 17.1 %collective-permute-start.26 = (f32[384,384]{1,0:T(8,128)S(1)}, f32[384,384]{1,0:T(8,128)S(1)}, u32[]{:S(2)}, u32[]{:S(2)}) collective-permute-start(f32[384,384]{1,0:T(8,128)S(1)} %collective-permute-done.22.refs_1_), channel_id=1, source_target_pairs={{0,1},{1,0},{2,3},{3,2},{4,5},{5,4},{6,7},{7,6},{8,9},{9,8},{10,11... | collective-permute-start | bytes 1769480 | tf_op jit(solution)/shard_map/ppermute | solution.py:25
  117.2 18.3 %collective-permute-start.27 = (f32[384,384]{1,0:T(8,128)S(1)}, f32[384,384]{1,0:T(8,128)S(1)}, u32[]{:S(2)}, u32[]{:S(2)}) collective-permute-start(f32[384,384]{1,0:T(8,128)S(1)} %collective-permute-done.23.refs_2_), channel_id=1, source_target_pairs={{0,1},{1,0},{2,3},{3,2},{4,5},{5,4},{6,7},{7,6},{8,9},{9,8},{10,11... | collective-permute-start | bytes 1769480 | tf_op jit(solution)/shard_map/ppermute | solution.py:25
  118.5 18.6 %collective-permute-start.28 = (f32[384,384]{1,0:T(8,128)S(1)}, f32[384,384]{1,0:T(8,128)S(1)}, u32[]{:S(2)}, u32[]{:S(2)}) collective-permute-start(f32[384,384]{1,0:T(8,128)S(1)} %collective-permute-done.24.refs_3_), channel_id=1, source_target_pairs={{0,1},{1,0},{2,3},{3,2},{4,5},{5,4},{6,7},{7,6},{8,9},{9,8},{10,11... | collective-permute-start | bytes 1769480 | tf_op jit(solution)/shard_map/ppermute | solution.py:25
  118.5 11.7 %collective-permute-start.33 = (f32[256,384]{1,0:T(8,128)}, f32[256,384]{1,0:T(8,128)S(1)}, u32[]{:S(2)}, u32[]{:S(2)}) collective-permute-start(f32[256,384]{1,0:T(8,128)} %get-tuple-element.107.refs_8_), channel_id=1, source_target_pairs={{0,16},{16,32},{32,48},{48,0},{1,17},{17,33},{33,49},{49,1},{2,18}... | collective-permute-start | bytes 1179656 | tf_op jit(solution)/shard_map/ppermute | solution.py:17
  130.2 25.4 %copy-start.18 = (f32[256,384]{1,0:T(8,128)}, f32[256,384]{1,0:T(8,128)S(1)}, u32[]{:S(2)}) copy-start(f32[256,384]{1,0:T(8,128)S(1)} %collective-permute-done.33.refs_9_) | copy-start | bytes 1179652
  130.2 30.5 %collective-permute-start.39 = (f32[512,256]{1,0:T(8,128)}, f32[512,256]{1,0:T(8,128)}, u32[]{:S(2)}, u32[]{:S(2)}) collective-permute-start(f32[512,256]{1,0:T(8,128)} %get-tuple-element.116), channel_id=1, source_target_pairs={{0,8},{8,64},{64,72},{72,0},{1,9},{9,65},{65,73},{73,1},{2,10},{10... | collective-permute-start | bytes 1572872 | tf_op jit(solution)/shard_map/ppermute | solution.py:21
  130.8 29.9 %collective-permute-start.40 = (f32[512,256]{1,0:T(8,128)}, f32[512,256]{1,0:T(8,128)}, u32[]{:S(2)}, u32[]{:S(2)}) collective-permute-start(f32[512,256]{1,0:T(8,128)} %get-tuple-element.117), channel_id=1, source_target_pairs={{0,64},{8,72},{64,0},{72,8},{1,65},{9,73},{65,1},{73,9},{2,66},{10... | collective-permute-start | bytes 1572872 | tf_op jit(solution)/shard_map/ppermute | solution.py:21
  133.8 27.0 %collective-permute-start.41 = (f32[512,256]{1,0:T(8,128)}, f32[512,256]{1,0:T(8,128)}, u32[]{:S(2)}, u32[]{:S(2)}) collective-permute-start(f32[512,256]{1,0:T(8,128)} %get-tuple-element.118), channel_id=1, source_target_pairs={{0,72},{8,0},{64,8},{72,64},{1,73},{9,1},{65,9},{73,65},{2,74},{10... | collective-permute-start | bytes 1572872 | tf_op jit(solution)/shard_map/ppermute | solution.py:21
  135.5 13.9 %collective-permute-start.34 = (f32[256,384]{1,0:T(8,128)}, f32[256,384]{1,0:T(8,128)}, u32[]{:S(2)}, u32[]{:S(2)}) collective-permute-start(f32[256,384]{1,0:T(8,128)} %get-tuple-element.107.refs_8_), channel_id=1, source_target_pairs={{0,32},{16,48},{32,0},{48,16},{1,33},{17,49},{33,1},{49,17},{2,34}... | collective-permute-start | bytes 1179656 | tf_op jit(solution)/shard_map/ppermute | solution.py:17
  137.9 17.7 %collective-permute-start.35 = (f32[256,384]{1,0:T(8,128)}, f32[256,384]{1,0:T(8,128)}, u32[]{:S(2)}, u32[]{:S(2)}) collective-permute-start(f32[256,384]{1,0:T(8,128)} %get-tuple-element.107.refs_8_), channel_id=1, source_target_pairs={{0,48},{16,0},{32,16},{48,32},{1,49},{17,1},{33,17},{49,33},{2,50}... | collective-permute-start | bytes 1179656 | tf_op jit(solution)/shard_map/ppermute | solution.py:17
  149.5 6.2 %collective-permute-start.29 = (f32[128,128]{1,0:T(8,128)S(1)}, f32[128,128]{1,0:T(8,128)S(1)}, u32[]{:S(2)}, u32[]{:S(2)}) collective-permute-start(f32[128,128]{1,0:T(8,128)S(1)} %reduce_sum.18.refs_0_), channel_id=1, source_target_pairs={{0,1},{1,0},{2,3},{3,2},{4,5},{5,4},{6,7},{7,6},{8,9},{9,8},{10,11... | collective-permute-start | bytes 196616 | tf_op jit(solution)/shard_map/ppermute | solution.py:25
  160.8 2.9 %collective-permute-start.45 = (f32[512,256]{1,0:T(8,128)}, f32[512,256]{1,0:T(8,128)S(1)}, u32[]{:S(2)}, u32[]{:S(2)}) collective-permute-start(f32[512,256]{1,0:T(8,128)} %collective-permute-done.39.refs_1_), channel_id=1, source_target_pairs={{0,1},{1,0},{2,3},{3,2},{4,5},{5,4},{6,7},{7,6},{8,9},{9,8},{10,11... | collective-permute-start | bytes 1572872 | tf_op jit(solution)/shard_map/ppermute | solution.py:25
  160.9 4.8 %collective-permute-start.46 = (f32[512,256]{1,0:T(8,128)}, f32[512,256]{1,0:T(8,128)S(1)}, u32[]{:S(2)}, u32[]{:S(2)}) collective-permute-start(f32[512,256]{1,0:T(8,128)} %collective-permute-done.40.refs_2_), channel_id=1, source_target_pairs={{0,1},{1,0},{2,3},{3,2},{4,5},{5,4},{6,7},{7,6},{8,9},{9,8},{10,11... | collective-permute-start | bytes 1572872 | tf_op jit(solution)/shard_map/ppermute | solution.py:25
  161.4 4.3 %collective-permute-start.47 = (f32[512,256]{1,0:T(8,128)}, f32[512,256]{1,0:T(8,128)S(1)}, u32[]{:S(2)}, u32[]{:S(2)}) collective-permute-start(f32[512,256]{1,0:T(8,128)} %collective-permute-done.41.refs_3_), channel_id=1, source_target_pairs={{0,1},{1,0},{2,3},{3,2},{4,5},{5,4},{6,7},{7,6},{8,9},{9,8},{10,11... | collective-permute-start | bytes 1572872 | tf_op jit(solution)/shard_map/ppermute | solution.py:25
  161.5 13.6 %collective-permute-start.42 = (f32[256,384]{1,0:T(8,128)}, f32[256,384]{1,0:T(8,128)S(1)}, u32[]{:S(2)}, u32[]{:S(2)}) collective-permute-start(f32[256,384]{1,0:T(8,128)} %get-tuple-element.120), channel_id=1, source_target_pairs={{0,16},{16,32},{32,48},{48,0},{1,17},{17,33},{33,49},{49,1},{2,18}... | collective-permute-start | bytes 1179656 | tf_op jit(solution)/shard_map/ppermute | solution.py:17
  162.1 13.7 %collective-permute-start.43 = (f32[256,384]{1,0:T(8,128)}, f32[256,384]{1,0:T(8,128)S(1)}, u32[]{:S(2)}, u32[]{:S(2)}) collective-permute-start(f32[256,384]{1,0:T(8,128)} %get-tuple-element.121), channel_id=1, source_target_pairs={{0,32},{16,48},{32,0},{48,16},{1,33},{17,49},{33,1},{49,17},{2,34}... | collective-permute-start | bytes 1179656 | tf_op jit(solution)/shard_map/ppermute | solution.py:17
  163.6 19.5 %collective-permute-start.44 = (f32[256,384]{1,0:T(8,128)}, f32[256,384]{1,0:T(8,128)S(1)}, u32[]{:S(2)}, u32[]{:S(2)}) collective-permute-start(f32[256,384]{1,0:T(8,128)} %get-tuple-element.122), channel_id=1, source_target_pairs={{0,48},{16,0},{32,16},{48,32},{1,49},{17,1},{33,17},{49,33},{2,50}... | collective-permute-start | bytes 1179656 | tf_op jit(solution)/shard_map/ppermute | solution.py:17
  183.9 31.0 %all-to-all-start.1 = ((f32[4,256,512]{2,1,0:T(8,128)}), f32[4,256,512]{2,1,0:T(8,128)S(1)}, u32[]{:S(2)}, u32[]{:S(2)}) async-start(f32[4,256,512]{2,1,0:T(8,128)} %shard_map.75), calls=%async_computation.1 | async-start | bytes 4194304 | tf_op jit(solution)/shard_map/all_to_all | solution.py:333
  188.1 1.7 collective-permute-start.48
  188.1 2.3 %collective-permute-start.49 = (f32[256,384]{1,0:T(8,128)S(1)}, f32[256,384]{1,0:T(8,128)S(1)}, u32[]{:S(2)}, u32[]{:S(2)}) collective-permute-start(f32[256,384]{1,0:T(8,128)S(1)} %collective-permute-done.42.refs_3_), channel_id=1, source_target_pairs={{0,1},{1,0},{2,3},{3,2},{4,5},{5,4},{6,7},{7,6},{8,9},{9,8},{10,11... | collective-permute-start | bytes 1179656 | tf_op jit(solution)/shard_map/ppermute | solution.py:25
  188.6 2.9 %collective-permute-start.50 = (f32[256,384]{1,0:T(8,128)S(1)}, f32[256,384]{1,0:T(8,128)S(1)}, u32[]{:S(2)}, u32[]{:S(2)}) collective-permute-start(f32[256,384]{1,0:T(8,128)S(1)} %collective-permute-done.43.refs_4_), channel_id=1, source_target_pairs={{0,1},{1,0},{2,3},{3,2},{4,5},{5,4},{6,7},{7,6},{8,9},{9,8},{10,11... | collective-permute-start | bytes 1179656 | tf_op jit(solution)/shard_map/ppermute | solution.py:25
  188.7 3.6 %collective-permute-start.51 = (f32[256,384]{1,0:T(8,128)}, f32[256,384]{1,0:T(8,128)}, u32[]{:S(2)}, u32[]{:S(2)}) collective-permute-start(f32[256,384]{1,0:T(8,128)} %copy-done.21), channel_id=1, source_target_pairs={{0,1},{1,0},{2,3},{3,2},{4,5},{5,4},{6,7},{7,6},{8,9},{9,8},{10,11... | collective-permute-start | bytes 1179656 | tf_op jit(solution)/shard_map/ppermute | solution.py:25
  197.3 15.7 %collective-permute-start.52 = (f32[384,384]{1,0:T(8,128)}, f32[384,384]{1,0:T(8,128)S(1)}, u32[]{:S(2)}, u32[]{:S(2)}) collective-permute-start(f32[384,384]{1,0:T(8,128)} %get-tuple-element.138), channel_id=1, source_target_pairs={{0,8},{8,0},{1,9},{9,1},{2,10},{10,2},{3,11},{11,3},{4,12},{12,4},... | collective-permute-start | bytes 1769480 | tf_op jit(solution)/shard_map/ppermute | solution.py:25
  (36 other events, 329.3 us)
Sparse Core Ops, SparseCore 0:
  9.7 33.4 all-gather.4
  44.8 35.3 all-gather.6

commit v2 on v1

--- a/solution.py
+++ b/solution.py
@@ -93,14 +93,14 @@
             pairs.append((stripe.at[pl.ds(row, half)], sent[i].at[pl.ds(h * half, half)]))
     copies = fetch(pairs, sems)
 
-    def eight(i, carry):
-        for k in range(8):
-            at = i * 8 + k
-            picked[pl.ds(at, 1), :] = stripe[pl.ds(index[at], 1), :]
+    def some(i, carry):
+        found = [stripe[pl.ds(index[i * 32 + k], 1), :] for k in range(32)]
+        for k in range(32):
+            picked[pl.ds(i * 32 + k, 1), :] = found[k]
         return carry
 
     count = picked.shape[0]
-    lax.fori_loop(0, count // 8, eight, 0)
+    lax.fori_loop(0, count // 32, some, 0)
     order, share = count // 2, out.shape[2]
     for child in range(2):
         left = picked[pl.ds(child * order, order), :]

time: 223 us -> 223 us (level)
  no operation moved by 1% of the time
where the time goes in v2:
time: 223 us; the launch traced here: 222 us
  waiting for transfers between devices  77.2 us (35%)
  starting transfers between devices  66.7 us (30%)
  Pallas kernels  53.1 us (24%)
  between operations  14.5 us (7%)
  local copies, waits for them, and re-layouts  6.39 us (3%)
  other arithmetic  4.06 us (2%)
    ppermute x24, waiting for transfers between devices, along(): return lax.ppermute(value, axis, [(i, (i + step) % 4) for i in range(4)])  54.1 us
    pallas_call x7, Pallas kernels, call(): pl.pallas_call(kernel, out_shape=list(outs), in_specs=[smem] * (1 + len(i...  46.9 us
    ppermute x24, starting transfers between devices, along(): return lax.ppermute(value, axis, [(i, (i + step) % 4) for i in range(4)])  40.7 us
    ppermute x25, waiting for transfers between devices, other(): return lax.ppermute(value, axis, [(0, 1), (1, 0)])  22.4 us
    all_to_all x1, starting transfers between devices, on_device(): cov = lax.all_to_all(part, ROWS, 0, 0).sum(0)  8.57 us
    ppermute x25, starting transfers between devices, other(): return lax.ppermute(value, axis, [(0, 1), (1, 0)])  7.2 us
    unnamed x87, local copies, waits for them, and re-layouts  5.73 us
    ppermute x3, starting transfers between devices, along_z(): lax.ppermute(value, ('sub', 'zl'), [(i, (i + step) % 4) for i in range(4)])  5.3 us
  transfers between devices with their start and end apart: 57, of which 25 were waited for; matrix products, arithmetic and copies ran while one was open for 2% of the time, Pallas kernels for 24%

profile of v2, /device:TPU:2, one launch (start us, length us, event | category | flops | bytes accessed | tf_op | source)
XLA Modules:
  0.0 222.0 jit_solution(50227181115501428)
XLA Ops:
  7.2 0.7 all-gather.5.cloned.1.call-update
  8.0 2.0 shard_map.67.refs_0_
  10.0 1.6 collective-permute-start
  11.6 0.7 collective-permute-start.3
  12.2 1.6 collective-permute-start.4
  13.8 1.1 collective-permute-start.5
  14.9 2.2 collective-permute-start.6
  17.1 2.9 %collective-permute-start.1 = (f32[512,256]{1,0:T(8,128)}, f32[512,256]{1,0:T(8,128)S(1)}, u32[]{:S(2)}, u32[]{:S(2)}) collective-permute-start(f32[512,256]{1,0:T(8,128)} %shard_map.67.refs_0_), channel_id=1, source_target_pairs={{0,4},{2,6},{4,0},{6,2},{1,5},{3,7},{5,1},{7,3},{8,12},{10,14},{12... | collective-permute-start | bytes 1572872 | tf_op jit(solution)/shard_map/ppermute | solution.py:17
  20.0 5.3 %collective-permute-done.refs_1_ = f32[512,256]{1,0:T(8,128)S(1)} collective-permute-done((f32[512,256]{1,0:T(8,128)}, f32[512,256]{1,0:T(8,128)S(1)}, u32[]{:S(2)}, u32[]{:S(2)}) %collective-permute-start) | collective-permute-done | bytes 524320 | tf_op jit(solution)/shard_map/ppermute | solution.py:17
  25.2 2.8 %collective-permute-start.2 = (f32[512,256]{1,0:T(8,128)}, f32[512,256]{1,0:T(8,128)}, u32[]{:S(2)}, u32[]{:S(2)}) collective-permute-start(f32[512,256]{1,0:T(8,128)} %shard_map.67.refs_0_), channel_id=1, source_target_pairs={{0,6},{2,0},{4,2},{6,4},{1,7},{3,1},{5,3},{7,5},{8,14},{10,8},{12,... | collective-permute-start | bytes 1572872 | tf_op jit(solution)/shard_map/ppermute | solution.py:17
  28.0 2.2 shard_map.68
  30.2 1.0 broadcast_select_fusion.refs_0_
  31.2 6.4 %collective-permute-done.1.refs_2_ = f32[512,256]{1,0:T(8,128)S(1)} collective-permute-done((f32[512,256]{1,0:T(8,128)}, f32[512,256]{1,0:T(8,128)S(1)}, u32[]{:S(2)}, u32[]{:S(2)}) %collective-permute-start.1) | collective-permute-done | bytes 524320 | tf_op jit(solution)/shard_map/ppermute | solution.py:17
  37.6 5.3 %collective-permute-done.2.refs_3_ = f32[512,256]{1,0:T(8,128)} collective-permute-done((f32[512,256]{1,0:T(8,128)}, f32[512,256]{1,0:T(8,128)}, u32[]{:S(2)}, u32[]{:S(2)}) %collective-permute-start.2) | collective-permute-done | bytes 524320 | tf_op jit(solution)/shard_map/ppermute | solution.py:17
  44.5 3.1 %collective-permute-start.11 = (f32[128,384]{1,0:T(8,128)S(1)}, f32[128,384]{1,0:T(8,128)}, u32[]{:S(2)}, u32[]{:S(2)}) collective-permute-start(f32[128,384]{1,0:T(8,128)S(1)} %broadcast_select_fusion.refs_0_), channel_id=1, source_target_pairs={{0,2},{2,4},{4,6},{6,0},{1,3},{3,5},{5,7},{7,1},{8,10},{10,12},{12... | collective-permute-start | bytes 589832 | tf_op jit(solution)/shard_map/ppermute | solution.py:17
  47.7 2.3 %collective-permute-start.12 = (f32[128,384]{1,0:T(8,128)S(1)}, f32[128,384]{1,0:T(8,128)S(1)}, u32[]{:S(2)}, u32[]{:S(2)}) collective-permute-start(f32[128,384]{1,0:T(8,128)S(1)} %broadcast_select_fusion.refs_0_), channel_id=1, source_target_pairs={{0,4},{2,6},{4,0},{6,2},{1,5},{3,7},{5,1},{7,3},{8,12},{10,14},{12... | collective-permute-start | bytes 589832 | tf_op jit(solution)/shard_map/ppermute | solution.py:17
  50.0 1.6 collective-permute-start.13
  52.3 0.7 stack.23.where
  53.0 11.7 %shard_map.69 = (f32[16,128,128]{2,1,0:T(8,128)}, f32[512,256]{1,0:T(8,128)}, f32[512,256]{1,0:T(8,128)}, f32[512,256]{1,0:T(8,128)}, f32[512,256]{1,0:T(8,128)}, /*index=5*/f32[512,256]{1,0:T(8,128)}) custom-call(s32[5]{0:T(128)} %stack.23.where, s32[2048]{0:T(1024)} %bitcast.27, f32[512,256]{1,0:T(8,128)} %shard_map.67.refs_0_, f32[512,256]{1,0:T(8,128)} %copy-done.12, ...), custom_call_target="tpu_custom_call" | custom-call | flops 1 | bytes 1 | tf_op jit(solution)/shard_map/pallas_call | solution.py:62
  64.8 8.6 %all-to-all-start = ((f32[16,128,128]{2,1,0:T(8,128)}), f32[16,128,128]{2,1,0:T(8,128)S(1)}, u32[]{:S(2)}, u32[]{:S(2)}) async-start(f32[16,128,128]{2,1,0:T(8,128)} %get-tuple-element.80), calls=%async_computation | async-start | bytes 2097152 | tf_op jit(solution)/shard_map/all_to_all | solution.py:280
  76.1 0.7 copy-done.32
  76.8 5.1 %shard_map.70.mine = f32[256,384]{1,0:T(8,128)} custom-call(s32[5]{0:T(128)} %stack.23.where, f32[128,384]{1,0:T(8,128)} %copy-done.4, f32[128,384]{1,0:T(8,128)} %collective-permute-done.11.refs_1_, f32[128,384]{1,0:T(8,128)} %copy-done.27, f32[128,384]{1,0:T(8,128)} %copy-done.28, f32[128,384]{1,0:T(8,128)} %copy-done.29, f32[128,384]{1,0:T(8,128)} %copy-done.30, ...), custom_call_target="tpu_custom_call" | custom-call | flops 1 | bytes 1 | tf_op jit(solution)/shard_map/pallas_call | solution.py:62
  82.0 1.5 collective-permute-start.21
  83.5 3.8 %shard_map.72 = (f32[384,384]{1,0:T(8,128)}, f32[384,384]{1,0:T(8,128)}, f32[384,384]{1,0:T(8,128)}, f32[384,384]{1,0:T(8,128)}) custom-call(s32[5]{0:T(128)} %stack.23.where, f32[4,384,384]{2,1,0:T(8,128)} %bitcast.24), custom_call_target="tpu_custom_call" | custom-call | flops 1 | bytes 1 | tf_op jit(solution)/shard_map/pallas_call | solution.py:62
  87.3 1.5 collective-permute-start.22
  88.8 1.2 collective-permute-start.23
  90.3 2.1 collective-permute-start.24
  92.4 2.5 %collective-permute-done.21.came = f32[256,384]{1,0:T(8,128)S(1)} collective-permute-done((f32[256,384]{1,0:T(8,128)}, f32[256,384]{1,0:T(8,128)S(1)}, u32[]{:S(2)}, u32[]{:S(2)}) %collective-permute-start.21) | collective-permute-done | bytes 393248 | tf_op jit(solution)/shard_map/ppermute | solution.py:25
  95.6 2.2 collective-permute-start.16
  97.8 2.0 shard_map.71
  99.8 0.9 collective-permute-done.15.refs_2_
  101.3 0.7 collective-permute-done.30.refs_5_
  102.3 1.0 collective-permute-start.36
  103.3 2.9 %collective-permute-start.37 = (f32[128,384]{1,0:T(8,128)}, f32[128,384]{1,0:T(8,128)}, u32[]{:S(2)}, u32[]{:S(2)}) collective-permute-start(f32[128,384]{1,0:T(8,128)} %get-tuple-element.108.refs_12_), channel_id=1, source_target_pairs={{0,4},{2,6},{4,0},{6,2},{1,5},{3,7},{5,1},{7,3},{8,12},{10,14},{12... | collective-permute-start | bytes 589832 | tf_op jit(solution)/shard_map/ppermute | solution.py:17
  106.2 4.6 %collective-permute-done.36.refs_13_ = f32[128,384]{1,0:T(8,128)S(1)} collective-permute-done((f32[128,384]{1,0:T(8,128)}, f32[128,384]{1,0:T(8,128)S(1)}, u32[]{:S(2)}, u32[]{:S(2)}) %collective-permute-start.36) | collective-permute-done | bytes 196640 | tf_op jit(solution)/shard_map/ppermute | solution.py:17
  110.8 1.9 collective-permute-start.38
  112.6 3.2 %collective-permute-done.37.refs_14_ = f32[128,384]{1,0:T(8,128)} collective-permute-done((f32[128,384]{1,0:T(8,128)}, f32[128,384]{1,0:T(8,128)}, u32[]{:S(2)}, u32[]{:S(2)}) %collective-permute-start.37) | collective-permute-done | bytes 196640 | tf_op jit(solution)/shard_map/ppermute | solution.py:17
  116.6 1.1 collective-permute-done.24.refs_3_
  117.7 1.1 collective-permute-start.33
  118.8 10.7 %collective-permute-done.33.refs_9_ = f32[256,384]{1,0:T(8,128)S(1)} collective-permute-done((f32[256,384]{1,0:T(8,128)}, f32[256,384]{1,0:T(8,128)S(1)}, u32[]{:S(2)}, u32[]{:S(2)}) %collective-permute-start.33) | collective-permute-done | bytes 393248 | tf_op jit(solution)/shard_map/ppermute | solution.py:17
  130.1 2.9 %collective-permute-start.40 = (f32[512,256]{1,0:T(8,128)}, f32[512,256]{1,0:T(8,128)}, u32[]{:S(2)}, u32[]{:S(2)}) collective-permute-start(f32[512,256]{1,0:T(8,128)} %get-tuple-element.117), channel_id=1, source_target_pairs={{0,64},{8,72},{64,0},{72,8},{1,65},{9,73},{65,1},{73,9},{2,66},{10... | collective-permute-start | bytes 1572872 | tf_op jit(solution)/shard_map/ppermute | solution.py:21
  133.0 1.8 collective-permute-start.41
  134.8 1.6 collective-permute-start.34
  136.3 0.8 copy-done.11
  137.2 1.5 collective-permute-start.35
  138.7 8.5 %shard_map.73 = (f32[384,384]{1,0:T(8,128)}, f32[384,384]{1,0:T(8,128)}) custom-call(s32[5]{0:T(128)} %stack.23.where, f32[384,384]{1,0:T(8,128)} %get-tuple-element.98.refs_0_, f32[384,384]{1,0:T(8,128)} %copy-done.5, f32[384,384]{1,0:T(8,128)} %copy-done.6, f32[384,384]{1,0:T(8,128)} %copy-done.7, f32[384,384]{1,0:T(8,128)} %copy-done.8, ...), custom_call_target="tpu_custom_call" | custom-call | flops 1 | bytes 1 | tf_op jit(solution)/shard_map/pallas_call | solution.py:62
  147.2 1.5 collective-permute-done.34.refs_10_
  148.7 6.2 %collective-permute-done.35.refs_11_ = f32[256,384]{1,0:T(8,128)} collective-permute-done((f32[256,384]{1,0:T(8,128)}, f32[256,384]{1,0:T(8,128)}, u32[]{:S(2)}, u32[]{:S(2)}) %collective-permute-start.35) | collective-permute-done | bytes 393248 | tf_op jit(solution)/shard_map/ppermute | solution.py:17
  155.5 4.5 %shard_map.74 = (f32[128,384]{1,0:T(8,128)}, f32[256,384]{1,0:T(8,128)}, f32[256,384]{1,0:T(8,128)}, f32[256,384]{1,0:T(8,128)}, f32[256,384]{1,0:T(8,128)}) custom-call(s32[5]{0:T(128)} %stack.23.where, f32[128,128]{1,0:T(8,128)} %copy-done.26, f32[128,128]{1,0:T(8,128)} %copy-done.35, f32[128,128]{1,0:T(8,128)} %copy-done.36, f32[128,128]{1,0:T(8,128)} %copy-done.37, ...), custom_call_target="tpu_custom_call" | custom-call | flops 1 | bytes 1 | tf_op jit(solution)/shard_map/pallas_call | solution.py:62
  161.3 1.6 collective-permute-start.43
  162.9 2.0 collective-permute-start.44
  164.9 0.8 copy-done.15
  165.9 8.4 %shard_map.75 = f32[4,256,512]{2,1,0:T(8,128)} custom-call(s32[5]{0:T(128)} %stack.23.where, f32[512,256]{1,0:T(8,128)} %get-tuple-element.123.refs_0_, f32[512,256]{1,0:T(8,128)} %collective-permute-done.39.refs_1_, f32[512,256]{1,0:T(8,128)} %collective-permute-done.40.refs_2_, f32[512,256]{1,0:T(8,128)} %collective-permute-done.41.refs_3_, ...), custom_call_target="tpu_custom_call" | custom-call | flops 1 | bytes 1 | tf_op jit(solution)/shard_map/pallas_call | solution.py:62
  174.3 0.7 collective-permute-done.43.refs_4_
  175.0 7.4 %collective-permute-done.44.refs_5_ = f32[256,384]{1,0:T(8,128)S(1)} collective-permute-done((f32[256,384]{1,0:T(8,128)}, f32[256,384]{1,0:T(8,128)S(1)}, u32[]{:S(2)}, u32[]{:S(2)}) %collective-permute-start.44) | collective-permute-done | bytes 393248 | tf_op jit(solution)/shard_map/ppermute | solution.py:17
  182.4 0.7 copy-done.21
  183.1 4.2 %all-to-all-start.1 = ((f32[4,256,512]{2,1,0:T(8,128)}), f32[4,256,512]{2,1,0:T(8,128)S(1)}, u32[]{:S(2)}, u32[]{:S(2)}) async-start(f32[4,256,512]{2,1,0:T(8,128)} %shard_map.75), calls=%async_computation.1 | async-start | bytes 4194304 | tf_op jit(solution)/shard_map/all_to_all | solution.py:333
  188.4 0.7 collective-permute-done.48.refs_6_
  189.6 1.1 collective-permute-done.50.refs_8_
  190.8 0.8 copy-done.24
  191.5 5.0 %shard_map.76 = (f32[384,384]{1,0:T(8,128)}, f32[384,384]{1,0:T(8,128)}) custom-call(s32[5]{0:T(128)} %stack.23.where, f32[384,384]{1,0:T(8,128)} %get-tuple-element.131.refs_0_, f32[384,384]{1,0:T(8,128)} %get-tuple-element.132.refs_1_, f32[256,384]{1,0:T(8,128)} %get-tuple-element.133.refs_2_, f32[256,384]{1,0:T(8,128)} %copy-done.19, ...), custom_call_target="tpu_custom_call" | custom-call | flops 1 | bytes 1 | tf_op jit(solution)/shard_map/pallas_call | solution.py:62
  196.8 15.3 %collective-permute-done.52 = f32[384,384]{1,0:T(8,128)S(1)} collective-permute-done((f32[384,384]{1,0:T(8,128)}, f32[384,384]{1,0:T(8,128)S(1)}, u32[]{:S(2)}, u32[]{:S(2)}) %collective-permute-start.52) | collective-permute-done | bytes 589856 | tf_op jit(solution)/shard_map/ppermute | solution.py:25
  212.1 1.9 add_bitcast_fusion
  214.1 1.0 reduce_sum.19
  (155 shorter events, 12.6 us)
Async XLA Ops:
  7.2 44.5 %copy-start.42 = (s32[2,1024]{1,0:T(2,128)S(1)}, s32[2,1024]{1,0:T(2,128)}, u32[]{:S(2)}) copy-start(s32[2,1024]{1,0:T(2,128)} %param.5) | copy-start | bytes 24580
  7.2 57.6 %all-gather.5.cloned.1.call-start = ((), (), s32[]{:S(2)}) async-start(), calls=%async_computation.2 | async-start | bytes 2621440 | tf_op jit(solution)/shard_map/all_gather | solution.py:261
  7.9 75.6 %all-gather.7.cloned.1.call-start = ((), (), s32[]{:S(2)}) async-start(), calls=%async_computation.3 | async-start | bytes 2949120 | tf_op jit(solution)/shard_map/all_gather | solution.py:266
  10.0 33.4 %copy-start.3 = (f32[512,256]{1,0:T(8,128)S(1)}, f32[512,256]{1,0:T(8,128)}, u32[]{:S(2)}) copy-start(f32[512,256]{1,0:T(8,128)} %shard_map.67.refs_0_) | copy-start | bytes 1572868
  10.0 15.2 %collective-permute-start = (f32[512,256]{1,0:T(8,128)}, f32[512,256]{1,0:T(8,128)S(1)}, u32[]{:S(2)}, u32[]{:S(2)}) collective-permute-start(f32[512,256]{1,0:T(8,128)} %shard_map.67.refs_0_), channel_id=1, source_target_pairs={{0,2},{2,4},{4,6},{6,0},{1,3},{3,5},{5,7},{7,1},{8,10},{10,12},{12... | collective-permute-start | bytes 1572872 | tf_op jit(solution)/shard_map/ppermute | solution.py:17
  11.6 5.5 %collective-permute-start.3 = (f32[128,384]{1,0:T(8,128)}, f32[128,384]{1,0:T(8,128)S(1)}, u32[]{:S(2)}, u32[]{:S(2)}) collective-permute-start(f32[128,384]{1,0:T(8,128)} %bitcast.26), channel_id=1, source_target_pairs={{1,8},{8,1},{3,10},{10,3},{5,12},{12,5},{7,14},{14,7},{17,24},{24,... | collective-permute-start | bytes 589832 | tf_op jit(solution)/shard_map/ppermute | solution.py:258
  12.2 30.7 %collective-permute-start.4 = (f32[384,384]{1,0:T(8,128)}, f32[384,384]{1,0:T(8,128)S(1)}, u32[]{:S(2)}, u32[]{:S(2)}) collective-permute-start(f32[384,384]{1,0:T(8,128)} %bitcast.18), channel_id=1, source_target_pairs={{0,16},{16,32},{32,48},{48,0},{1,17},{17,33},{33,49},{49,1},{2,18}... | collective-permute-start | bytes 1769480 | tf_op jit(solution)/shard_map/ppermute | solution.py:17
  13.8 29.1 %collective-permute-start.5 = (f32[384,384]{1,0:T(8,128)}, f32[384,384]{1,0:T(8,128)S(1)}, u32[]{:S(2)}, u32[]{:S(2)}) collective-permute-start(f32[384,384]{1,0:T(8,128)} %bitcast.19), channel_id=1, source_target_pairs={{0,32},{16,48},{32,0},{48,16},{1,33},{17,49},{33,1},{49,17},{2,34}... | collective-permute-start | bytes 1769480 | tf_op jit(solution)/shard_map/ppermute | solution.py:17
  14.9 28.5 %collective-permute-start.6 = (f32[384,384]{1,0:T(8,128)}, f32[384,384]{1,0:T(8,128)S(1)}, u32[]{:S(2)}, u32[]{:S(2)}) collective-permute-start(f32[384,384]{1,0:T(8,128)} %bitcast.20), channel_id=1, source_target_pairs={{0,48},{16,0},{32,16},{48,32},{1,49},{17,1},{33,17},{49,33},{2,50}... | collective-permute-start | bytes 1769480 | tf_op jit(solution)/shard_map/ppermute | solution.py:17
  17.1 20.5 %collective-permute-start.1 = (f32[512,256]{1,0:T(8,128)}, f32[512,256]{1,0:T(8,128)S(1)}, u32[]{:S(2)}, u32[]{:S(2)}) collective-permute-start(f32[512,256]{1,0:T(8,128)} %shard_map.67.refs_0_), channel_id=1, source_target_pairs={{0,4},{2,6},{4,0},{6,2},{1,5},{3,7},{5,1},{7,3},{8,12},{10,14},{12... | collective-permute-start | bytes 1572872 | tf_op jit(solution)/shard_map/ppermute | solution.py:17
  25.2 27.7 %copy-start.12 = (f32[512,256]{1,0:T(8,128)}, f32[512,256]{1,0:T(8,128)S(1)}, u32[]{:S(2)}) copy-start(f32[512,256]{1,0:T(8,128)S(1)} %collective-permute-done.refs_1_) | copy-start | bytes 1572868
  25.2 17.6 %collective-permute-start.2 = (f32[512,256]{1,0:T(8,128)}, f32[512,256]{1,0:T(8,128)}, u32[]{:S(2)}, u32[]{:S(2)}) collective-permute-start(f32[512,256]{1,0:T(8,128)} %shard_map.67.refs_0_), channel_id=1, source_target_pairs={{0,6},{2,0},{4,2},{6,4},{1,7},{3,1},{5,3},{7,5},{8,14},{10,8},{12,... | collective-permute-start | bytes 1572872 | tf_op jit(solution)/shard_map/ppermute | solution.py:17
  31.2 42.2 %copy-start.4 = (f32[128,384]{1,0:T(8,128)}, f32[128,384]{1,0:T(8,128)S(1)}, u32[]{:S(2)}) copy-start(f32[128,384]{1,0:T(8,128)S(1)} %broadcast_select_fusion.refs_0_) | copy-start | bytes 589828
  43.4 4.2 %collective-permute-start.7 = (f32[512,256]{1,0:T(8,128)S(1)}, f32[512,256]{1,0:T(8,128)}, u32[]{:S(2)}, u32[]{:S(2)}) collective-permute-start(f32[512,256]{1,0:T(8,128)S(1)} %copy-done.3), channel_id=1, source_target_pairs={{0,1},{1,0},{2,3},{3,2},{4,5},{5,4},{6,7},{7,6},{8,9},{9,8},{10,11... | collective-permute-start | bytes 1572872 | tf_op jit(solution)/shard_map/ppermute | solution.py:25
  43.9 6.1 %collective-permute-start.8 = (f32[512,256]{1,0:T(8,128)S(1)}, f32[512,256]{1,0:T(8,128)}, u32[]{:S(2)}, u32[]{:S(2)}) collective-permute-start(f32[512,256]{1,0:T(8,128)S(1)} %collective-permute-done.refs_1_), channel_id=1, source_target_pairs={{0,1},{1,0},{2,3},{3,2},{4,5},{5,4},{6,7},{7,6},{8,9},{9,8},{10,11... | collective-permute-start | bytes 1572872 | tf_op jit(solution)/shard_map/ppermute | solution.py:25
  44.0 8.9 %collective-permute-start.9 = (f32[512,256]{1,0:T(8,128)S(1)}, f32[512,256]{1,0:T(8,128)}, u32[]{:S(2)}, u32[]{:S(2)}) collective-permute-start(f32[512,256]{1,0:T(8,128)S(1)} %collective-permute-done.1.refs_2_), channel_id=1, source_target_pairs={{0,1},{1,0},{2,3},{3,2},{4,5},{5,4},{6,7},{7,6},{8,9},{9,8},{10,11... | collective-permute-start | bytes 1572872 | tf_op jit(solution)/shard_map/ppermute | solution.py:25
  44.4 8.5 %collective-permute-start.10 = (f32[512,256]{1,0:T(8,128)}, f32[512,256]{1,0:T(8,128)}, u32[]{:S(2)}, u32[]{:S(2)}) collective-permute-start(f32[512,256]{1,0:T(8,128)} %collective-permute-done.2.refs_3_), channel_id=1, source_target_pairs={{0,1},{1,0},{2,3},{3,2},{4,5},{5,4},{6,7},{7,6},{8,9},{9,8},{10,11... | collective-permute-start | bytes 1572872 | tf_op jit(solution)/shard_map/ppermute | solution.py:25
  44.5 20.2 %collective-permute-start.11 = (f32[128,384]{1,0:T(8,128)S(1)}, f32[128,384]{1,0:T(8,128)}, u32[]{:S(2)}, u32[]{:S(2)}) collective-permute-start(f32[128,384]{1,0:T(8,128)S(1)} %broadcast_select_fusion.refs_0_), channel_id=1, source_target_pairs={{0,2},{2,4},{4,6},{6,0},{1,3},{3,5},{5,7},{7,1},{8,10},{10,12},{12... | collective-permute-start | bytes 589832 | tf_op jit(solution)/shard_map/ppermute | solution.py:17
  47.7 17.0 %collective-permute-start.12 = (f32[128,384]{1,0:T(8,128)S(1)}, f32[128,384]{1,0:T(8,128)S(1)}, u32[]{:S(2)}, u32[]{:S(2)}) collective-permute-start(f32[128,384]{1,0:T(8,128)S(1)} %broadcast_select_fusion.refs_0_), channel_id=1, source_target_pairs={{0,4},{2,6},{4,0},{6,2},{1,5},{3,7},{5,1},{7,3},{8,12},{10,14},{12... | collective-permute-start | bytes 589832 | tf_op jit(solution)/shard_map/ppermute | solution.py:17
  50.0 14.8 %collective-permute-start.13 = (f32[128,384]{1,0:T(8,128)S(1)}, f32[128,384]{1,0:T(8,128)S(1)}, u32[]{:S(2)}, u32[]{:S(2)}) collective-permute-start(f32[128,384]{1,0:T(8,128)S(1)} %broadcast_select_fusion.refs_0_), channel_id=1, source_target_pairs={{0,6},{2,0},{4,2},{6,4},{1,7},{3,1},{5,3},{7,5},{8,14},{10,8},{12,... | collective-permute-start | bytes 589832 | tf_op jit(solution)/shard_map/ppermute | solution.py:17
  64.8 25.2 %all-to-all-start = ((f32[16,128,128]{2,1,0:T(8,128)}), f32[16,128,128]{2,1,0:T(8,128)S(1)}, u32[]{:S(2)}, u32[]{:S(2)}) async-start(f32[16,128,128]{2,1,0:T(8,128)} %get-tuple-element.80), calls=%async_computation | async-start | bytes 2097152 | tf_op jit(solution)/shard_map/all_to_all | solution.py:280
  73.4 1.5 collective-permute-start.17
  73.5 1.9 collective-permute-start.18
  74.0 1.5 collective-permute-start.19
  74.1 1.7 collective-permute-start.20
  82.0 12.9 %collective-permute-start.21 = (f32[256,384]{1,0:T(8,128)}, f32[256,384]{1,0:T(8,128)S(1)}, u32[]{:S(2)}, u32[]{:S(2)}) collective-permute-start(f32[256,384]{1,0:T(8,128)} %shard_map.70.mine), channel_id=1, source_target_pairs={{0,8},{8,0},{1,9},{9,1},{2,10},{10,2},{3,11},{11,3},{4,12},{12,4},... | collective-permute-start | bytes 1179656 | tf_op jit(solution)/shard_map/ppermute | solution.py:25
  87.3 28.6 %collective-permute-start.22 = (f32[384,384]{1,0:T(8,128)}, f32[384,384]{1,0:T(8,128)S(1)}, u32[]{:S(2)}, u32[]{:S(2)}) collective-permute-start(f32[384,384]{1,0:T(8,128)} %get-tuple-element.99), channel_id=1, source_target_pairs={{0,16},{16,32},{32,48},{48,0},{1,17},{17,33},{33,49},{49,1},{2,18}... | collective-permute-start | bytes 1769480 | tf_op jit(solution)/shard_map/ppermute | solution.py:17
  88.8 27.6 %collective-permute-start.23 = (f32[384,384]{1,0:T(8,128)}, f32[384,384]{1,0:T(8,128)S(1)}, u32[]{:S(2)}, u32[]{:S(2)}) collective-permute-start(f32[384,384]{1,0:T(8,128)} %get-tuple-element.100), channel_id=1, source_target_pairs={{0,32},{16,48},{32,0},{48,16},{1,33},{17,49},{33,1},{49,17},{2,34}... | collective-permute-start | bytes 1769480 | tf_op jit(solution)/shard_map/ppermute | solution.py:17
  90.1 64.8 %copy-start.26 = (f32[128,128]{1,0:T(8,128)}, f32[128,128]{1,0:T(8,128)S(1)}, u32[]{:S(2)}) copy-start(f32[128,128]{1,0:T(8,128)S(1)} %reduce_sum.18.refs_0_) | copy-start | bytes 196612
  90.1 5.5 %collective-permute-start.14 = (f32[128,128]{1,0:T(8,128)S(1)}, f32[128,128]{1,0:T(8,128)S(1)}, u32[]{:S(2)}, u32[]{:S(2)}) collective-permute-start(f32[128,128]{1,0:T(8,128)S(1)} %reduce_sum.18.refs_0_), channel_id=1, source_target_pairs={{0,2},{2,4},{4,6},{6,0},{1,3},{3,5},{5,7},{7,1},{8,10},{10,12},{12... | collective-permute-start | bytes 196616 | tf_op jit(solution)/shard_map/ppermute | solution.py:17
  90.3 27.4 %collective-permute-start.24 = (f32[384,384]{1,0:T(8,128)}, f32[384,384]{1,0:T(8,128)S(1)}, u32[]{:S(2)}, u32[]{:S(2)}) collective-permute-start(f32[384,384]{1,0:T(8,128)} %get-tuple-element.101), channel_id=1, source_target_pairs={{0,48},{16,0},{32,16},{48,32},{1,49},{17,1},{33,17},{49,33},{2,50}... | collective-permute-start | bytes 1769480 | tf_op jit(solution)/shard_map/ppermute | solution.py:17
  94.9 5.8 %collective-permute-start.15 = (f32[128,128]{1,0:T(8,128)S(1)}, f32[128,128]{1,0:T(8,128)S(1)}, u32[]{:S(2)}, u32[]{:S(2)}) collective-permute-start(f32[128,128]{1,0:T(8,128)S(1)} %reduce_sum.18.refs_0_), channel_id=1, source_target_pairs={{0,4},{2,6},{4,0},{6,2},{1,5},{3,7},{5,1},{7,3},{8,12},{10,14},{12... | collective-permute-start | bytes 196616 | tf_op jit(solution)/shard_map/ppermute | solution.py:17
  95.6 51.5 %copy-start.35 = (f32[128,128]{1,0:T(8,128)}, f32[128,128]{1,0:T(8,128)S(1)}, u32[]{:S(2)}) copy-start(f32[128,128]{1,0:T(8,128)S(1)} %collective-permute-done.14.refs_1_) | copy-start | bytes 196612
  95.6 5.1 %collective-permute-start.16 = (f32[128,128]{1,0:T(8,128)S(1)}, f32[128,128]{1,0:T(8,128)S(1)}, u32[]{:S(2)}, u32[]{:S(2)}) collective-permute-start(f32[128,128]{1,0:T(8,128)S(1)} %reduce_sum.18.refs_0_), channel_id=1, source_target_pairs={{0,6},{2,0},{4,2},{6,4},{1,7},{3,1},{5,3},{7,5},{8,14},{10,8},{12,... | collective-permute-start | bytes 196616 | tf_op jit(solution)/shard_map/ppermute | solution.py:17
  100.7 1.3 collective-permute-start.30
  100.8 1.5 collective-permute-start.31
  102.0 1.3 collective-permute-start.32
  102.3 8.5 %collective-permute-start.36 = (f32[128,384]{1,0:T(8,128)}, f32[128,384]{1,0:T(8,128)S(1)}, u32[]{:S(2)}, u32[]{:S(2)}) collective-permute-start(f32[128,384]{1,0:T(8,128)} %get-tuple-element.108.refs_12_), channel_id=1, source_target_pairs={{0,2},{2,4},{4,6},{6,0},{1,3},{3,5},{5,7},{7,1},{8,10},{10,12},{12... | collective-permute-start | bytes 589832 | tf_op jit(solution)/shard_map/ppermute | solution.py:17
  103.3 12.6 %collective-permute-start.37 = (f32[128,384]{1,0:T(8,128)}, f32[128,384]{1,0:T(8,128)}, u32[]{:S(2)}, u32[]{:S(2)}) collective-permute-start(f32[128,384]{1,0:T(8,128)} %get-tuple-element.108.refs_12_), channel_id=1, source_target_pairs={{0,4},{2,6},{4,0},{6,2},{1,5},{3,7},{5,1},{7,3},{8,12},{10,14},{12... | collective-permute-start | bytes 589832 | tf_op jit(solution)/shard_map/ppermute | solution.py:17
  110.8 7.0 %collective-permute-start.38 = (f32[128,384]{1,0:T(8,128)}, f32[128,384]{1,0:T(8,128)}, u32[]{:S(2)}, u32[]{:S(2)}) collective-permute-start(f32[128,384]{1,0:T(8,128)} %get-tuple-element.108.refs_12_), channel_id=1, source_target_pairs={{0,6},{2,0},{4,2},{6,4},{1,7},{3,1},{5,3},{7,5},{8,14},{10,8},{12,... | collective-permute-start | bytes 589832 | tf_op jit(solution)/shard_map/ppermute | solution.py:17
  115.8 14.2 %collective-permute-start.25 = (f32[384,384]{1,0:T(8,128)}, f32[384,384]{1,0:T(8,128)S(1)}, u32[]{:S(2)}, u32[]{:S(2)}) collective-permute-start(f32[384,384]{1,0:T(8,128)} %get-tuple-element.98.refs_0_), channel_id=1, source_target_pairs={{0,1},{1,0},{2,3},{3,2},{4,5},{5,4},{6,7},{7,6},{8,9},{9,8},{10,11... | collective-permute-start | bytes 1769480 | tf_op jit(solution)/shard_map/ppermute | solution.py:25
  115.9 17.1 %collective-permute-start.26 = (f32[384,384]{1,0:T(8,128)S(1)}, f32[384,384]{1,0:T(8,128)S(1)}, u32[]{:S(2)}, u32[]{:S(2)}) collective-permute-start(f32[384,384]{1,0:T(8,128)S(1)} %collective-permute-done.22.refs_1_), channel_id=1, source_target_pairs={{0,1},{1,0},{2,3},{3,2},{4,5},{5,4},{6,7},{7,6},{8,9},{9,8},{10,11... | collective-permute-start | bytes 1769480 | tf_op jit(solution)/shard_map/ppermute | solution.py:25
  116.5 18.3 %collective-permute-start.27 = (f32[384,384]{1,0:T(8,128)S(1)}, f32[384,384]{1,0:T(8,128)S(1)}, u32[]{:S(2)}, u32[]{:S(2)}) collective-permute-start(f32[384,384]{1,0:T(8,128)S(1)} %collective-permute-done.23.refs_2_), channel_id=1, source_target_pairs={{0,1},{1,0},{2,3},{3,2},{4,5},{5,4},{6,7},{7,6},{8,9},{9,8},{10,11... | collective-permute-start | bytes 1769480 | tf_op jit(solution)/shard_map/ppermute | solution.py:25
  117.7 18.6 %collective-permute-start.28 = (f32[384,384]{1,0:T(8,128)S(1)}, f32[384,384]{1,0:T(8,128)S(1)}, u32[]{:S(2)}, u32[]{:S(2)}) collective-permute-start(f32[384,384]{1,0:T(8,128)S(1)} %collective-permute-done.24.refs_3_), channel_id=1, source_target_pairs={{0,1},{1,0},{2,3},{3,2},{4,5},{5,4},{6,7},{7,6},{8,9},{9,8},{10,11... | collective-permute-start | bytes 1769480 | tf_op jit(solution)/shard_map/ppermute | solution.py:25
  117.7 11.7 %collective-permute-start.33 = (f32[256,384]{1,0:T(8,128)}, f32[256,384]{1,0:T(8,128)S(1)}, u32[]{:S(2)}, u32[]{:S(2)}) collective-permute-start(f32[256,384]{1,0:T(8,128)} %get-tuple-element.107.refs_8_), channel_id=1, source_target_pairs={{0,16},{16,32},{32,48},{48,0},{1,17},{17,33},{33,49},{49,1},{2,18}... | collective-permute-start | bytes 1179656 | tf_op jit(solution)/shard_map/ppermute | solution.py:17
  129.4 25.4 %copy-start.18 = (f32[256,384]{1,0:T(8,128)}, f32[256,384]{1,0:T(8,128)S(1)}, u32[]{:S(2)}) copy-start(f32[256,384]{1,0:T(8,128)S(1)} %collective-permute-done.33.refs_9_) | copy-start | bytes 1179652
  129.4 30.5 %collective-permute-start.39 = (f32[512,256]{1,0:T(8,128)}, f32[512,256]{1,0:T(8,128)}, u32[]{:S(2)}, u32[]{:S(2)}) collective-permute-start(f32[512,256]{1,0:T(8,128)} %get-tuple-element.116), channel_id=1, source_target_pairs={{0,8},{8,64},{64,72},{72,0},{1,9},{9,65},{65,73},{73,1},{2,10},{10... | collective-permute-start | bytes 1572872 | tf_op jit(solution)/shard_map/ppermute | solution.py:21
  130.1 29.9 %collective-permute-start.40 = (f32[512,256]{1,0:T(8,128)}, f32[512,256]{1,0:T(8,128)}, u32[]{:S(2)}, u32[]{:S(2)}) collective-permute-start(f32[512,256]{1,0:T(8,128)} %get-tuple-element.117), channel_id=1, source_target_pairs={{0,64},{8,72},{64,0},{72,8},{1,65},{9,73},{65,1},{73,9},{2,66},{10... | collective-permute-start | bytes 1572872 | tf_op jit(solution)/shard_map/ppermute | solution.py:21
  133.0 27.0 %collective-permute-start.41 = (f32[512,256]{1,0:T(8,128)}, f32[512,256]{1,0:T(8,128)}, u32[]{:S(2)}, u32[]{:S(2)}) collective-permute-start(f32[512,256]{1,0:T(8,128)} %get-tuple-element.118), channel_id=1, source_target_pairs={{0,72},{8,0},{64,8},{72,64},{1,73},{9,1},{65,9},{73,65},{2,74},{10... | collective-permute-start | bytes 1572872 | tf_op jit(solution)/shard_map/ppermute | solution.py:21
  134.8 13.9 %collective-permute-start.34 = (f32[256,384]{1,0:T(8,128)}, f32[256,384]{1,0:T(8,128)}, u32[]{:S(2)}, u32[]{:S(2)}) collective-permute-start(f32[256,384]{1,0:T(8,128)} %get-tuple-element.107.refs_8_), channel_id=1, source_target_pairs={{0,32},{16,48},{32,0},{48,16},{1,33},{17,49},{33,1},{49,17},{2,34}... | collective-permute-start | bytes 1179656 | tf_op jit(solution)/shard_map/ppermute | solution.py:17
  137.2 17.7 %collective-permute-start.35 = (f32[256,384]{1,0:T(8,128)}, f32[256,384]{1,0:T(8,128)}, u32[]{:S(2)}, u32[]{:S(2)}) collective-permute-start(f32[256,384]{1,0:T(8,128)} %get-tuple-element.107.refs_8_), channel_id=1, source_target_pairs={{0,48},{16,0},{32,16},{48,32},{1,49},{17,1},{33,17},{49,33},{2,50}... | collective-permute-start | bytes 1179656 | tf_op jit(solution)/shard_map/ppermute | solution.py:17
  148.7 6.2 %collective-permute-start.29 = (f32[128,128]{1,0:T(8,128)S(1)}, f32[128,128]{1,0:T(8,128)S(1)}, u32[]{:S(2)}, u32[]{:S(2)}) collective-permute-start(f32[128,128]{1,0:T(8,128)S(1)} %reduce_sum.18.refs_0_), channel_id=1, source_target_pairs={{0,1},{1,0},{2,3},{3,2},{4,5},{5,4},{6,7},{7,6},{8,9},{9,8},{10,11... | collective-permute-start | bytes 196616 | tf_op jit(solution)/shard_map/ppermute | solution.py:25
  160.0 2.9 %collective-permute-start.45 = (f32[512,256]{1,0:T(8,128)}, f32[512,256]{1,0:T(8,128)S(1)}, u32[]{:S(2)}, u32[]{:S(2)}) collective-permute-start(f32[512,256]{1,0:T(8,128)} %collective-permute-done.39.refs_1_), channel_id=1, source_target_pairs={{0,1},{1,0},{2,3},{3,2},{4,5},{5,4},{6,7},{7,6},{8,9},{9,8},{10,11... | collective-permute-start | bytes 1572872 | tf_op jit(solution)/shard_map/ppermute | solution.py:25
  160.1 4.8 %collective-permute-start.46 = (f32[512,256]{1,0:T(8,128)}, f32[512,256]{1,0:T(8,128)S(1)}, u32[]{:S(2)}, u32[]{:S(2)}) collective-permute-start(f32[512,256]{1,0:T(8,128)} %collective-permute-done.40.refs_2_), channel_id=1, source_target_pairs={{0,1},{1,0},{2,3},{3,2},{4,5},{5,4},{6,7},{7,6},{8,9},{9,8},{10,11... | collective-permute-start | bytes 1572872 | tf_op jit(solution)/shard_map/ppermute | solution.py:25
  160.6 4.3 %collective-permute-start.47 = (f32[512,256]{1,0:T(8,128)}, f32[512,256]{1,0:T(8,128)S(1)}, u32[]{:S(2)}, u32[]{:S(2)}) collective-permute-start(f32[512,256]{1,0:T(8,128)} %collective-permute-done.41.refs_3_), channel_id=1, source_target_pairs={{0,1},{1,0},{2,3},{3,2},{4,5},{5,4},{6,7},{7,6},{8,9},{9,8},{10,11... | collective-permute-start | bytes 1572872 | tf_op jit(solution)/shard_map/ppermute | solution.py:25
  160.7 13.6 %collective-permute-start.42 = (f32[256,384]{1,0:T(8,128)}, f32[256,384]{1,0:T(8,128)S(1)}, u32[]{:S(2)}, u32[]{:S(2)}) collective-permute-start(f32[256,384]{1,0:T(8,128)} %get-tuple-element.120), channel_id=1, source_target_pairs={{0,16},{16,32},{32,48},{48,0},{1,17},{17,33},{33,49},{49,1},{2,18}... | collective-permute-start | bytes 1179656 | tf_op jit(solution)/shard_map/ppermute | solution.py:17
  161.3 13.7 %collective-permute-start.43 = (f32[256,384]{1,0:T(8,128)}, f32[256,384]{1,0:T(8,128)S(1)}, u32[]{:S(2)}, u32[]{:S(2)}) collective-permute-start(f32[256,384]{1,0:T(8,128)} %get-tuple-element.121), channel_id=1, source_target_pairs={{0,32},{16,48},{32,0},{48,16},{1,33},{17,49},{33,1},{49,17},{2,34}... | collective-permute-start | bytes 1179656 | tf_op jit(solution)/shard_map/ppermute | solution.py:17
  162.9 19.5 %collective-permute-start.44 = (f32[256,384]{1,0:T(8,128)}, f32[256,384]{1,0:T(8,128)S(1)}, u32[]{:S(2)}, u32[]{:S(2)}) collective-permute-start(f32[256,384]{1,0:T(8,128)} %get-tuple-element.122), channel_id=1, source_target_pairs={{0,48},{16,0},{32,16},{48,32},{1,49},{17,1},{33,17},{49,33},{2,50}... | collective-permute-start | bytes 1179656 | tf_op jit(solution)/shard_map/ppermute | solution.py:17
  183.1 31.0 %all-to-all-start.1 = ((f32[4,256,512]{2,1,0:T(8,128)}), f32[4,256,512]{2,1,0:T(8,128)S(1)}, u32[]{:S(2)}, u32[]{:S(2)}) async-start(f32[4,256,512]{2,1,0:T(8,128)} %shard_map.75), calls=%async_computation.1 | async-start | bytes 4194304 | tf_op jit(solution)/shard_map/all_to_all | solution.py:333
  187.4 1.7 collective-permute-start.48
  187.4 2.3 %collective-permute-start.49 = (f32[256,384]{1,0:T(8,128)S(1)}, f32[256,384]{1,0:T(8,128)S(1)}, u32[]{:S(2)}, u32[]{:S(2)}) collective-permute-start(f32[256,384]{1,0:T(8,128)S(1)} %collective-permute-done.42.refs_3_), channel_id=1, source_target_pairs={{0,1},{1,0},{2,3},{3,2},{4,5},{5,4},{6,7},{7,6},{8,9},{9,8},{10,11... | collective-permute-start | bytes 1179656 | tf_op jit(solution)/shard_map/ppermute | solution.py:25
  187.9 2.9 %collective-permute-start.50 = (f32[256,384]{1,0:T(8,128)S(1)}, f32[256,384]{1,0:T(8,128)S(1)}, u32[]{:S(2)}, u32[]{:S(2)}) collective-permute-start(f32[256,384]{1,0:T(8,128)S(1)} %collective-permute-done.43.refs_4_), channel_id=1, source_target_pairs={{0,1},{1,0},{2,3},{3,2},{4,5},{5,4},{6,7},{7,6},{8,9},{9,8},{10,11... | collective-permute-start | bytes 1179656 | tf_op jit(solution)/shard_map/ppermute | solution.py:25
  188.0 3.6 %collective-permute-start.51 = (f32[256,384]{1,0:T(8,128)}, f32[256,384]{1,0:T(8,128)}, u32[]{:S(2)}, u32[]{:S(2)}) collective-permute-start(f32[256,384]{1,0:T(8,128)} %copy-done.21), channel_id=1, source_target_pairs={{0,1},{1,0},{2,3},{3,2},{4,5},{5,4},{6,7},{7,6},{8,9},{9,8},{10,11... | collective-permute-start | bytes 1179656 | tf_op jit(solution)/shard_map/ppermute | solution.py:25
  196.5 15.7 %collective-permute-start.52 = (f32[384,384]{1,0:T(8,128)}, f32[384,384]{1,0:T(8,128)S(1)}, u32[]{:S(2)}, u32[]{:S(2)}) collective-permute-start(f32[384,384]{1,0:T(8,128)} %get-tuple-element.138), channel_id=1, source_target_pairs={{0,8},{8,0},{1,9},{9,1},{2,10},{10,2},{3,11},{11,3},{4,12},{12,4},... | collective-permute-start | bytes 1769480 | tf_op jit(solution)/shard_map/ppermute | solution.py:25
  (36 other events, 327.0 us)
Sparse Core Ops, SparseCore 0:
  9.7 33.4 all-gather.4
  44.8 35.3 all-gather.6

commit v3 on v2

--- a/solution.py
+++ b/solution.py
@@ -259,15 +259,15 @@
     inverse_x = [inverse] + [along(inverse, "x", d) for d in (1, 2, 3)]
     inverse_t = flipped(inverse)
     top_z = lax.all_gather(top_inverse, ("sub", "zl"), axis=0)
-    stripes, panel, inverse_x, inverse_t = lax.optimization_barrier(
-        (stripes, panel, inverse_x, inverse_t)
-    )
-
-    inverse_y = lax.all_gather(inverse_t, "y", axis=0)
-    panels = over_y(panel)
     owner = ancestors // block
     place = (y - owner // 2) % 4 + jnp.where(owner % 2 == core, 0, 4)
     index = (place * block + ancestors % block).reshape(-1)
+    stripes, panel, inverse_x, inverse_t, index, where = lax.optimization_barrier(
+        (stripes, panel, inverse_x, inverse_t, index, where)
+    )
+
+    inverse_y = lax.all_gather(inverse_t, "y", axis=0)
+    panels = over_y(panel)
     part, own0, own1, own2, own3, there0 = call(
         select_kernel, where, both_cores(stripes),
         [shape(16, share, share)] + [shape(block, stripe)] * 5,

time: 223 us -> 222 us (level)
    unnamed x87 -> x93, local copies, waits for them, and re-layouts: 5.73 us -> 6.51 us
where the time goes in v3:
time: 222 us; the launch traced here: 221 us
  waiting for transfers between devices  75.1 us (34%)
  starting transfers between devices  67.4 us (30%)
  Pallas kernels  53 us (24%)
  between operations  14.5 us (7%)
  local copies, waits for them, and re-layouts  7.17 us (3%)
  other arithmetic  4.06 us (2%)
    ppermute x24, waiting for transfers between devices, along(): return lax.ppermute(value, axis, [(i, (i + step) % 4) for i in range(4)])  51.9 us
    pallas_call x7, Pallas kernels, call(): pl.pallas_call(kernel, out_shape=list(outs), in_specs=[smem] * (1 + len(i...  46.8 us
    ppermute x24, starting transfers between devices, along(): return lax.ppermute(value, axis, [(i, (i + step) % 4) for i in range(4)])  41.3 us
    ppermute x25, waiting for transfers between devices, other(): return lax.ppermute(value, axis, [(0, 1), (1, 0)])  22.5 us
    all_to_all x1, starting transfers between devices, on_device(): cov = lax.all_to_all(part, ROWS, 0, 0).sum(0)  8.49 us
    ppermute x25, starting transfers between devices, other(): return lax.ppermute(value, axis, [(0, 1), (1, 0)])  7.19 us
    unnamed x93, local copies, waits for them, and re-layouts  6.51 us
    ppermute x3, starting transfers between devices, along_z(): lax.ppermute(value, ('sub', 'zl'), [(i, (i + step) % 4) for i in range(4)])  5.31 us
  transfers between devices with their start and end apart: 57, of which 25 were waited for; matrix products, arithmetic and copies ran while one was open for 2% of the time, Pallas kernels for 24%

profile of v3, /device:TPU:2, one launch (start us, length us, event | category | flops | bytes accessed | tf_op | source)
XLA Modules:
  0.0 221.3 jit_solution(3503845173992278845)
XLA Ops:
  7.2 0.7 all-gather.5.cloned.1.call-update
  8.0 2.0 shard_map.67.refs_0_
  10.0 1.6 collective-permute-start
  12.2 1.6 collective-permute-start.4
  13.8 1.1 collective-permute-start.5
  14.9 2.2 collective-permute-start.6
  17.1 2.9 %collective-permute-start.1 = (f32[512,256]{1,0:T(8,128)}, f32[512,256]{1,0:T(8,128)S(1)}, u32[]{:S(2)}, u32[]{:S(2)}) collective-permute-start(f32[512,256]{1,0:T(8,128)} %shard_map.67.refs_0_), channel_id=1, source_target_pairs={{0,4},{2,6},{4,0},{6,2},{1,5},{3,7},{5,1},{7,3},{8,12},{10,14},{12... | collective-permute-start | bytes 1572872 | tf_op jit(solution)/shard_map/ppermute | solution.py:17
  20.0 5.3 %collective-permute-done.refs_1_ = f32[512,256]{1,0:T(8,128)S(1)} collective-permute-done((f32[512,256]{1,0:T(8,128)}, f32[512,256]{1,0:T(8,128)S(1)}, u32[]{:S(2)}, u32[]{:S(2)}) %collective-permute-start) | collective-permute-done | bytes 524320 | tf_op jit(solution)/shard_map/ppermute | solution.py:17
  25.2 2.8 %collective-permute-start.2 = (f32[512,256]{1,0:T(8,128)}, f32[512,256]{1,0:T(8,128)}, u32[]{:S(2)}, u32[]{:S(2)}) collective-permute-start(f32[512,256]{1,0:T(8,128)} %shard_map.67.refs_0_), channel_id=1, source_target_pairs={{0,6},{2,0},{4,2},{6,4},{1,7},{3,1},{5,3},{7,5},{8,14},{10,8},{12,... | collective-permute-start | bytes 1572872 | tf_op jit(solution)/shard_map/ppermute | solution.py:17
  28.0 2.2 shard_map.68
  30.9 0.7 stack.23.where
  31.6 1.0 broadcast_select_fusion.refs_0_
  32.5 5.0 %collective-permute-done.1.refs_2_ = f32[512,256]{1,0:T(8,128)S(1)} collective-permute-done((f32[512,256]{1,0:T(8,128)}, f32[512,256]{1,0:T(8,128)S(1)}, u32[]{:S(2)}, u32[]{:S(2)}) %collective-permute-start.1) | collective-permute-done | bytes 524320 | tf_op jit(solution)/shard_map/ppermute | solution.py:17
  37.6 5.3 %collective-permute-done.2.refs_3_ = f32[512,256]{1,0:T(8,128)} collective-permute-done((f32[512,256]{1,0:T(8,128)}, f32[512,256]{1,0:T(8,128)}, u32[]{:S(2)}, u32[]{:S(2)}) %collective-permute-start.2) | collective-permute-done | bytes 524320 | tf_op jit(solution)/shard_map/ppermute | solution.py:17
  44.5 3.1 %collective-permute-start.11 = (f32[128,384]{1,0:T(8,128)S(1)}, f32[128,384]{1,0:T(8,128)}, u32[]{:S(2)}, u32[]{:S(2)}) collective-permute-start(f32[128,384]{1,0:T(8,128)S(1)} %broadcast_select_fusion.refs_0_), channel_id=1, source_target_pairs={{0,2},{2,4},{4,6},{6,0},{1,3},{3,5},{5,7},{7,1},{8,10},{10,12},{12... | collective-permute-start | bytes 589832 | tf_op jit(solution)/shard_map/ppermute | solution.py:17
  47.7 2.2 collective-permute-start.12
  49.9 1.7 collective-permute-start.13
  51.6 0.8 copy-done.16
  52.4 11.7 %shard_map.69 = (f32[16,128,128]{2,1,0:T(8,128)}, f32[512,256]{1,0:T(8,128)}, f32[512,256]{1,0:T(8,128)}, f32[512,256]{1,0:T(8,128)}, f32[512,256]{1,0:T(8,128)}, /*index=5*/f32[512,256]{1,0:T(8,128)}) custom-call(s32[5]{0:T(128)} %stack.23.where, s32[2048]{0:T(1024)} %bitcast.27, f32[512,256]{1,0:T(8,128)} %shard_map.67.refs_0_, f32[512,256]{1,0:T(8,128)} %copy-done.12, ...), custom_call_target="tpu_custom_call" | custom-call | flops 1 | bytes 1 | tf_op jit(solution)/shard_map/pallas_call | solution.py:62
  64.2 8.5 %all-to-all-start = ((f32[16,128,128]{2,1,0:T(8,128)}), f32[16,128,128]{2,1,0:T(8,128)S(1)}, u32[]{:S(2)}, u32[]{:S(2)}) async-start(f32[16,128,128]{2,1,0:T(8,128)} %get-tuple-element.84), calls=%async_computation | async-start | bytes 2097152 | tf_op jit(solution)/shard_map/all_to_all | solution.py:280
  75.5 0.7 copy-done.35
  76.2 5.1 %shard_map.70.mine = f32[256,384]{1,0:T(8,128)} custom-call(s32[5]{0:T(128)} %stack.23.where, f32[128,384]{1,0:T(8,128)} %copy-done.4, f32[128,384]{1,0:T(8,128)} %collective-permute-done.11.refs_1_, f32[128,384]{1,0:T(8,128)} %copy-done.30, f32[128,384]{1,0:T(8,128)} %copy-done.31, f32[128,384]{1,0:T(8,128)} %copy-done.32, f32[128,384]{1,0:T(8,128)} %copy-done.33, ...), custom_call_target="tpu_custom_call" | custom-call | flops 1 | bytes 1 | tf_op jit(solution)/shard_map/pallas_call | solution.py:62
  81.3 1.5 collective-permute-start.21
  82.8 3.8 %shard_map.72 = (f32[384,384]{1,0:T(8,128)}, f32[384,384]{1,0:T(8,128)}, f32[384,384]{1,0:T(8,128)}, f32[384,384]{1,0:T(8,128)}) custom-call(s32[5]{0:T(128)} %stack.23.where, f32[4,384,384]{2,1,0:T(8,128)} %bitcast.24), custom_call_target="tpu_custom_call" | custom-call | flops 1 | bytes 1 | tf_op jit(solution)/shard_map/pallas_call | solution.py:62
  86.6 1.5 collective-permute-start.22
  88.1 1.2 collective-permute-start.23
  89.6 2.1 collective-permute-start.24
  91.6 2.6 %collective-permute-done.21.came = f32[256,384]{1,0:T(8,128)S(1)} collective-permute-done((f32[256,384]{1,0:T(8,128)}, f32[256,384]{1,0:T(8,128)S(1)}, u32[]{:S(2)}, u32[]{:S(2)}) %collective-permute-start.21) | collective-permute-done | bytes 393248 | tf_op jit(solution)/shard_map/ppermute | solution.py:25
  94.2 1.1 collective-permute-start.15
  95.3 1.8 collective-permute-start.16
  97.1 2.0 shard_map.71
  99.1 0.9 collective-permute-done.15.refs_2_
  100.6 0.7 collective-permute-done.30.refs_5_
  101.6 0.9 collective-permute-start.36
  102.6 2.9 %collective-permute-start.37 = (f32[128,384]{1,0:T(8,128)}, f32[128,384]{1,0:T(8,128)}, u32[]{:S(2)}, u32[]{:S(2)}) collective-permute-start(f32[128,384]{1,0:T(8,128)} %get-tuple-element.112.refs_12_), channel_id=1, source_target_pairs={{0,4},{2,6},{4,0},{6,2},{1,5},{3,7},{5,1},{7,3},{8,12},{10,14},{12... | collective-permute-start | bytes 589832 | tf_op jit(solution)/shard_map/ppermute | solution.py:17
  105.5 4.6 %collective-permute-done.36.refs_13_ = f32[128,384]{1,0:T(8,128)S(1)} collective-permute-done((f32[128,384]{1,0:T(8,128)}, f32[128,384]{1,0:T(8,128)S(1)}, u32[]{:S(2)}, u32[]{:S(2)}) %collective-permute-start.36) | collective-permute-done | bytes 196640 | tf_op jit(solution)/shard_map/ppermute | solution.py:17
  110.1 1.9 collective-permute-start.38
  112.0 3.2 %collective-permute-done.37.refs_14_ = f32[128,384]{1,0:T(8,128)} collective-permute-done((f32[128,384]{1,0:T(8,128)}, f32[128,384]{1,0:T(8,128)}, u32[]{:S(2)}, u32[]{:S(2)}) %collective-permute-start.37) | collective-permute-done | bytes 196640 | tf_op jit(solution)/shard_map/ppermute | solution.py:17
  115.9 1.1 collective-permute-done.24.refs_3_
  117.0 1.1 collective-permute-start.33
  118.1 10.7 %collective-permute-done.33.refs_9_ = f32[256,384]{1,0:T(8,128)S(1)} collective-permute-done((f32[256,384]{1,0:T(8,128)}, f32[256,384]{1,0:T(8,128)S(1)}, u32[]{:S(2)}, u32[]{:S(2)}) %collective-permute-start.33) | collective-permute-done | bytes 393248 | tf_op jit(solution)/shard_map/ppermute | solution.py:17
  129.4 2.9 %collective-permute-start.40 = (f32[512,256]{1,0:T(8,128)}, f32[512,256]{1,0:T(8,128)}, u32[]{:S(2)}, u32[]{:S(2)}) collective-permute-start(f32[512,256]{1,0:T(8,128)} %get-tuple-element.121), channel_id=1, source_target_pairs={{0,64},{8,72},{64,0},{72,8},{1,65},{9,73},{65,1},{73,9},{2,66},{10... | collective-permute-start | bytes 1572872 | tf_op jit(solution)/shard_map/ppermute | solution.py:21
  132.3 1.8 collective-permute-start.41
  134.1 1.6 collective-permute-start.34
  135.7 0.8 copy-done.11
  136.5 1.5 collective-permute-start.35
  138.0 8.4 %shard_map.73 = (f32[384,384]{1,0:T(8,128)}, f32[384,384]{1,0:T(8,128)}) custom-call(s32[5]{0:T(128)} %stack.23.where, f32[384,384]{1,0:T(8,128)} %get-tuple-element.102.refs_0_, f32[384,384]{1,0:T(8,128)} %copy-done.5, f32[384,384]{1,0:T(8,128)} %copy-done.6, f32[384,384]{1,0:T(8,128)} %copy-done.7, f32[384,384]{1,0:T(8,128)} %copy-done.8, ...), custom_call_target="tpu_custom_call" | custom-call | flops 1 | bytes 1 | tf_op jit(solution)/shard_map/pallas_call | solution.py:62
  146.5 1.5 collective-permute-done.34.refs_10_
  148.0 5.8 %collective-permute-done.35.refs_11_ = f32[256,384]{1,0:T(8,128)} collective-permute-done((f32[256,384]{1,0:T(8,128)}, f32[256,384]{1,0:T(8,128)}, u32[]{:S(2)}, u32[]{:S(2)}) %collective-permute-start.35) | collective-permute-done | bytes 393248 | tf_op jit(solution)/shard_map/ppermute | solution.py:17
  154.4 4.5 %shard_map.74 = (f32[128,384]{1,0:T(8,128)}, f32[256,384]{1,0:T(8,128)}, f32[256,384]{1,0:T(8,128)}, f32[256,384]{1,0:T(8,128)}, f32[256,384]{1,0:T(8,128)}) custom-call(s32[5]{0:T(128)} %stack.23.where, f32[128,128]{1,0:T(8,128)} %copy-done.29, f32[128,128]{1,0:T(8,128)} %copy-done.38, f32[128,128]{1,0:T(8,128)} %copy-done.39, f32[128,128]{1,0:T(8,128)} %copy-done.40, ...), custom_call_target="tpu_custom_call" | custom-call | flops 1 | bytes 1 | tf_op jit(solution)/shard_map/pallas_call | solution.py:62
  160.3 1.9 collective-permute-start.43
  162.2 2.0 collective-permute-start.44
  164.2 0.8 copy-done.18
  165.2 8.4 %shard_map.75 = f32[4,256,512]{2,1,0:T(8,128)} custom-call(s32[5]{0:T(128)} %stack.23.where, f32[512,256]{1,0:T(8,128)} %get-tuple-element.127.refs_0_, f32[512,256]{1,0:T(8,128)} %collective-permute-done.39.refs_1_, f32[512,256]{1,0:T(8,128)} %collective-permute-done.40.refs_2_, f32[512,256]{1,0:T(8,128)} %collective-permute-done.41.refs_3_, ...), custom_call_target="tpu_custom_call" | custom-call | flops 1 | bytes 1 | tf_op jit(solution)/shard_map/pallas_call | solution.py:62
  174.0 7.6 %collective-permute-done.44.refs_5_ = f32[256,384]{1,0:T(8,128)S(1)} collective-permute-done((f32[256,384]{1,0:T(8,128)}, f32[256,384]{1,0:T(8,128)S(1)}, u32[]{:S(2)}, u32[]{:S(2)}) %collective-permute-start.44) | collective-permute-done | bytes 393248 | tf_op jit(solution)/shard_map/ppermute | solution.py:17
  181.6 0.7 copy-done.24
  182.3 4.4 %all-to-all-start.1 = ((f32[4,256,512]{2,1,0:T(8,128)}), f32[4,256,512]{2,1,0:T(8,128)S(1)}, u32[]{:S(2)}, u32[]{:S(2)}) async-start(f32[4,256,512]{2,1,0:T(8,128)} %shard_map.75), calls=%async_computation.1 | async-start | bytes 4194304 | tf_op jit(solution)/shard_map/all_to_all | solution.py:333
  187.7 0.7 collective-permute-done.48.refs_6_
  189.0 1.1 collective-permute-done.50.refs_8_
  190.1 0.7 copy-done.27
  190.8 5.0 %shard_map.76 = (f32[384,384]{1,0:T(8,128)}, f32[384,384]{1,0:T(8,128)}) custom-call(s32[5]{0:T(128)} %stack.23.where, f32[384,384]{1,0:T(8,128)} %get-tuple-element.135.refs_0_, f32[384,384]{1,0:T(8,128)} %get-tuple-element.136.refs_1_, f32[256,384]{1,0:T(8,128)} %get-tuple-element.137.refs_2_, f32[256,384]{1,0:T(8,128)} %copy-done.22, ...), custom_call_target="tpu_custom_call" | custom-call | flops 1 | bytes 1 | tf_op jit(solution)/shard_map/pallas_call | solution.py:62
  196.1 15.3 %collective-permute-done.52 = f32[384,384]{1,0:T(8,128)S(1)} collective-permute-done((f32[384,384]{1,0:T(8,128)}, f32[384,384]{1,0:T(8,128)S(1)}, u32[]{:S(2)}, u32[]{:S(2)}) %collective-permute-start.52) | collective-permute-done | bytes 589856 | tf_op jit(solution)/shard_map/ppermute | solution.py:25
  211.5 1.9 add_bitcast_fusion
  213.4 1.0 reduce_sum.19
  (161 shorter events, 12.9 us)
Async XLA Ops:
  7.2 23.1 %copy-start.45 = (s32[2,1024]{1,0:T(2,128)S(1)}, s32[2,1024]{1,0:T(2,128)}, u32[]{:S(2)}) copy-start(s32[2,1024]{1,0:T(2,128)} %param.5) | copy-start | bytes 24580
  7.2 57.0 %all-gather.5.cloned.1.call-start = ((), (), s32[]{:S(2)}) async-start(), calls=%async_computation.2 | async-start | bytes 2621440 | tf_op jit(solution)/shard_map/all_gather | solution.py:261
  7.9 74.9 %all-gather.7.cloned.1.call-start = ((), (), s32[]{:S(2)}) async-start(), calls=%async_computation.3 | async-start | bytes 2949120 | tf_op jit(solution)/shard_map/all_gather | solution.py:269
  10.0 33.4 %copy-start.3 = (f32[512,256]{1,0:T(8,128)S(1)}, f32[512,256]{1,0:T(8,128)}, u32[]{:S(2)}) copy-start(f32[512,256]{1,0:T(8,128)} %shard_map.67.refs_0_) | copy-start | bytes 1572868
  10.0 15.2 %collective-permute-start = (f32[512,256]{1,0:T(8,128)}, f32[512,256]{1,0:T(8,128)S(1)}, u32[]{:S(2)}, u32[]{:S(2)}) collective-permute-start(f32[512,256]{1,0:T(8,128)} %shard_map.67.refs_0_), channel_id=1, source_target_pairs={{0,2},{2,4},{4,6},{6,0},{1,3},{3,5},{5,7},{7,1},{8,10},{10,12},{12... | collective-permute-start | bytes 1572872 | tf_op jit(solution)/shard_map/ppermute | solution.py:17
  11.6 5.5 %collective-permute-start.3 = (f32[128,384]{1,0:T(8,128)}, f32[128,384]{1,0:T(8,128)S(1)}, u32[]{:S(2)}, u32[]{:S(2)}) collective-permute-start(f32[128,384]{1,0:T(8,128)} %bitcast.26), channel_id=1, source_target_pairs={{1,8},{8,1},{3,10},{10,3},{5,12},{12,5},{7,14},{14,7},{17,24},{24,... | collective-permute-start | bytes 589832 | tf_op jit(solution)/shard_map/ppermute | solution.py:258
  12.2 30.7 %collective-permute-start.4 = (f32[384,384]{1,0:T(8,128)}, f32[384,384]{1,0:T(8,128)S(1)}, u32[]{:S(2)}, u32[]{:S(2)}) collective-permute-start(f32[384,384]{1,0:T(8,128)} %bitcast.18), channel_id=1, source_target_pairs={{0,16},{16,32},{32,48},{48,0},{1,17},{17,33},{33,49},{49,1},{2,18}... | collective-permute-start | bytes 1769480 | tf_op jit(solution)/shard_map/ppermute | solution.py:17
  13.8 29.1 %collective-permute-start.5 = (f32[384,384]{1,0:T(8,128)}, f32[384,384]{1,0:T(8,128)S(1)}, u32[]{:S(2)}, u32[]{:S(2)}) collective-permute-start(f32[384,384]{1,0:T(8,128)} %bitcast.19), channel_id=1, source_target_pairs={{0,32},{16,48},{32,0},{48,16},{1,33},{17,49},{33,1},{49,17},{2,34}... | collective-permute-start | bytes 1769480 | tf_op jit(solution)/shard_map/ppermute | solution.py:17
  14.9 28.5 %collective-permute-start.6 = (f32[384,384]{1,0:T(8,128)}, f32[384,384]{1,0:T(8,128)S(1)}, u32[]{:S(2)}, u32[]{:S(2)}) collective-permute-start(f32[384,384]{1,0:T(8,128)} %bitcast.20), channel_id=1, source_target_pairs={{0,48},{16,0},{32,16},{48,32},{1,49},{17,1},{33,17},{49,33},{2,50}... | collective-permute-start | bytes 1769480 | tf_op jit(solution)/shard_map/ppermute | solution.py:17
  17.1 20.5 %collective-permute-start.1 = (f32[512,256]{1,0:T(8,128)}, f32[512,256]{1,0:T(8,128)S(1)}, u32[]{:S(2)}, u32[]{:S(2)}) collective-permute-start(f32[512,256]{1,0:T(8,128)} %shard_map.67.refs_0_), channel_id=1, source_target_pairs={{0,4},{2,6},{4,0},{6,2},{1,5},{3,7},{5,1},{7,3},{8,12},{10,14},{12... | collective-permute-start | bytes 1572872 | tf_op jit(solution)/shard_map/ppermute | solution.py:17
  25.2 27.2 %copy-start.12 = (f32[512,256]{1,0:T(8,128)}, f32[512,256]{1,0:T(8,128)S(1)}, u32[]{:S(2)}) copy-start(f32[512,256]{1,0:T(8,128)S(1)} %collective-permute-done.refs_1_) | copy-start | bytes 1572868
  25.2 17.6 %collective-permute-start.2 = (f32[512,256]{1,0:T(8,128)}, f32[512,256]{1,0:T(8,128)}, u32[]{:S(2)}, u32[]{:S(2)}) collective-permute-start(f32[512,256]{1,0:T(8,128)} %shard_map.67.refs_0_), channel_id=1, source_target_pairs={{0,6},{2,0},{4,2},{6,4},{1,7},{3,1},{5,3},{7,5},{8,14},{10,8},{12,... | collective-permute-start | bytes 1572872 | tf_op jit(solution)/shard_map/ppermute | solution.py:17
  32.5 40.2 %copy-start.4 = (f32[128,384]{1,0:T(8,128)}, f32[128,384]{1,0:T(8,128)S(1)}, u32[]{:S(2)}) copy-start(f32[128,384]{1,0:T(8,128)S(1)} %broadcast_select_fusion.refs_0_) | copy-start | bytes 589828
  43.4 4.2 %collective-permute-start.7 = (f32[512,256]{1,0:T(8,128)S(1)}, f32[512,256]{1,0:T(8,128)S(1)}, u32[]{:S(2)}, u32[]{:S(2)}) collective-permute-start(f32[512,256]{1,0:T(8,128)S(1)} %copy-done.3), channel_id=1, source_target_pairs={{0,1},{1,0},{2,3},{3,2},{4,5},{5,4},{6,7},{7,6},{8,9},{9,8},{10,11... | collective-permute-start | bytes 1572872 | tf_op jit(solution)/shard_map/ppermute | solution.py:25
  43.9 5.9 %collective-permute-start.8 = (f32[512,256]{1,0:T(8,128)S(1)}, f32[512,256]{1,0:T(8,128)S(1)}, u32[]{:S(2)}, u32[]{:S(2)}) collective-permute-start(f32[512,256]{1,0:T(8,128)S(1)} %collective-permute-done.refs_1_), channel_id=1, source_target_pairs={{0,1},{1,0},{2,3},{3,2},{4,5},{5,4},{6,7},{7,6},{8,9},{9,8},{10,11... | collective-permute-start | bytes 1572872 | tf_op jit(solution)/shard_map/ppermute | solution.py:25
  44.0 7.6 %collective-permute-start.9 = (f32[512,256]{1,0:T(8,128)S(1)}, f32[512,256]{1,0:T(8,128)S(1)}, u32[]{:S(2)}, u32[]{:S(2)}) collective-permute-start(f32[512,256]{1,0:T(8,128)S(1)} %collective-permute-done.1.refs_2_), channel_id=1, source_target_pairs={{0,1},{1,0},{2,3},{3,2},{4,5},{5,4},{6,7},{7,6},{8,9},{9,8},{10,11... | collective-permute-start | bytes 1572872 | tf_op jit(solution)/shard_map/ppermute | solution.py:25
  44.4 8.0 %collective-permute-start.10 = (f32[512,256]{1,0:T(8,128)}, f32[512,256]{1,0:T(8,128)}, u32[]{:S(2)}, u32[]{:S(2)}) collective-permute-start(f32[512,256]{1,0:T(8,128)} %collective-permute-done.2.refs_3_), channel_id=1, source_target_pairs={{0,1},{1,0},{2,3},{3,2},{4,5},{5,4},{6,7},{7,6},{8,9},{9,8},{10,11... | collective-permute-start | bytes 1572872 | tf_op jit(solution)/shard_map/ppermute | solution.py:25
  44.5 19.6 %collective-permute-start.11 = (f32[128,384]{1,0:T(8,128)S(1)}, f32[128,384]{1,0:T(8,128)}, u32[]{:S(2)}, u32[]{:S(2)}) collective-permute-start(f32[128,384]{1,0:T(8,128)S(1)} %broadcast_select_fusion.refs_0_), channel_id=1, source_target_pairs={{0,2},{2,4},{4,6},{6,0},{1,3},{3,5},{5,7},{7,1},{8,10},{10,12},{12... | collective-permute-start | bytes 589832 | tf_op jit(solution)/shard_map/ppermute | solution.py:17
  47.7 16.5 %collective-permute-start.12 = (f32[128,384]{1,0:T(8,128)S(1)}, f32[128,384]{1,0:T(8,128)S(1)}, u32[]{:S(2)}, u32[]{:S(2)}) collective-permute-start(f32[128,384]{1,0:T(8,128)S(1)} %broadcast_select_fusion.refs_0_), channel_id=1, source_target_pairs={{0,4},{2,6},{4,0},{6,2},{1,5},{3,7},{5,1},{7,3},{8,12},{10,14},{12... | collective-permute-start | bytes 589832 | tf_op jit(solution)/shard_map/ppermute | solution.py:17
  49.9 14.3 %collective-permute-start.13 = (f32[128,384]{1,0:T(8,128)S(1)}, f32[128,384]{1,0:T(8,128)S(1)}, u32[]{:S(2)}, u32[]{:S(2)}) collective-permute-start(f32[128,384]{1,0:T(8,128)S(1)} %broadcast_select_fusion.refs_0_), channel_id=1, source_target_pairs={{0,6},{2,0},{4,2},{6,4},{1,7},{3,1},{5,3},{7,5},{8,14},{10,8},{12,... | collective-permute-start | bytes 589832 | tf_op jit(solution)/shard_map/ppermute | solution.py:17
  64.2 25.1 %all-to-all-start = ((f32[16,128,128]{2,1,0:T(8,128)}), f32[16,128,128]{2,1,0:T(8,128)S(1)}, u32[]{:S(2)}, u32[]{:S(2)}) async-start(f32[16,128,128]{2,1,0:T(8,128)} %get-tuple-element.84), calls=%async_computation | async-start | bytes 2097152 | tf_op jit(solution)/shard_map/all_to_all | solution.py:280
  72.7 1.5 collective-permute-start.17
  72.8 1.9 collective-permute-start.18
  73.3 1.5 collective-permute-start.19
  73.4 1.7 collective-permute-start.20
  81.3 12.9 %collective-permute-start.21 = (f32[256,384]{1,0:T(8,128)}, f32[256,384]{1,0:T(8,128)S(1)}, u32[]{:S(2)}, u32[]{:S(2)}) collective-permute-start(f32[256,384]{1,0:T(8,128)} %shard_map.70.mine), channel_id=1, source_target_pairs={{0,8},{8,0},{1,9},{9,1},{2,10},{10,2},{3,11},{11,3},{4,12},{12,4},... | collective-permute-start | bytes 1179656 | tf_op jit(solution)/shard_map/ppermute | solution.py:25
  86.6 28.6 %collective-permute-start.22 = (f32[384,384]{1,0:T(8,128)}, f32[384,384]{1,0:T(8,128)S(1)}, u32[]{:S(2)}, u32[]{:S(2)}) collective-permute-start(f32[384,384]{1,0:T(8,128)} %get-tuple-element.103), channel_id=1, source_target_pairs={{0,16},{16,32},{32,48},{48,0},{1,17},{17,33},{33,49},{49,1},{2,18}... | collective-permute-start | bytes 1769480 | tf_op jit(solution)/shard_map/ppermute | solution.py:17
  88.1 27.6 %collective-permute-start.23 = (f32[384,384]{1,0:T(8,128)}, f32[384,384]{1,0:T(8,128)S(1)}, u32[]{:S(2)}, u32[]{:S(2)}) collective-permute-start(f32[384,384]{1,0:T(8,128)} %get-tuple-element.104), channel_id=1, source_target_pairs={{0,32},{16,48},{32,0},{48,16},{1,33},{17,49},{33,1},{49,17},{2,34}... | collective-permute-start | bytes 1769480 | tf_op jit(solution)/shard_map/ppermute | solution.py:17
  89.4 64.4 %copy-start.29 = (f32[128,128]{1,0:T(8,128)}, f32[128,128]{1,0:T(8,128)S(1)}, u32[]{:S(2)}) copy-start(f32[128,128]{1,0:T(8,128)S(1)} %reduce_sum.18.refs_0_) | copy-start | bytes 196612
  89.4 6.0 %collective-permute-start.14 = (f32[128,128]{1,0:T(8,128)S(1)}, f32[128,128]{1,0:T(8,128)S(1)}, u32[]{:S(2)}, u32[]{:S(2)}) collective-permute-start(f32[128,128]{1,0:T(8,128)S(1)} %reduce_sum.18.refs_0_), channel_id=1, source_target_pairs={{0,2},{2,4},{4,6},{6,0},{1,3},{3,5},{5,7},{7,1},{8,10},{10,12},{12... | collective-permute-start | bytes 196616 | tf_op jit(solution)/shard_map/ppermute | solution.py:17
  89.6 27.4 %collective-permute-start.24 = (f32[384,384]{1,0:T(8,128)}, f32[384,384]{1,0:T(8,128)S(1)}, u32[]{:S(2)}, u32[]{:S(2)}) collective-permute-start(f32[384,384]{1,0:T(8,128)} %get-tuple-element.105), channel_id=1, source_target_pairs={{0,48},{16,0},{32,16},{48,32},{1,49},{17,1},{33,17},{49,33},{2,50}... | collective-permute-start | bytes 1769480 | tf_op jit(solution)/shard_map/ppermute | solution.py:17
  94.2 5.8 %collective-permute-start.15 = (f32[128,128]{1,0:T(8,128)S(1)}, f32[128,128]{1,0:T(8,128)S(1)}, u32[]{:S(2)}, u32[]{:S(2)}) collective-permute-start(f32[128,128]{1,0:T(8,128)S(1)} %reduce_sum.18.refs_0_), channel_id=1, source_target_pairs={{0,4},{2,6},{4,0},{6,2},{1,5},{3,7},{5,1},{7,3},{8,12},{10,14},{12... | collective-permute-start | bytes 196616 | tf_op jit(solution)/shard_map/ppermute | solution.py:17
  95.3 51.1 %copy-start.38 = (f32[128,128]{1,0:T(8,128)}, f32[128,128]{1,0:T(8,128)S(1)}, u32[]{:S(2)}) copy-start(f32[128,128]{1,0:T(8,128)S(1)} %collective-permute-done.14.refs_1_) | copy-start | bytes 196612
  95.3 4.7 %collective-permute-start.16 = (f32[128,128]{1,0:T(8,128)S(1)}, f32[128,128]{1,0:T(8,128)S(1)}, u32[]{:S(2)}, u32[]{:S(2)}) collective-permute-start(f32[128,128]{1,0:T(8,128)S(1)} %reduce_sum.18.refs_0_), channel_id=1, source_target_pairs={{0,6},{2,0},{4,2},{6,4},{1,7},{3,1},{5,3},{7,5},{8,14},{10,8},{12,... | collective-permute-start | bytes 196616 | tf_op jit(solution)/shard_map/ppermute | solution.py:17
  100.0 1.3 collective-permute-start.30
  100.1 1.5 collective-permute-start.31
  101.3 1.3 collective-permute-start.32
  101.6 8.5 %collective-permute-start.36 = (f32[128,384]{1,0:T(8,128)}, f32[128,384]{1,0:T(8,128)S(1)}, u32[]{:S(2)}, u32[]{:S(2)}) collective-permute-start(f32[128,384]{1,0:T(8,128)} %get-tuple-element.112.refs_12_), channel_id=1, source_target_pairs={{0,2},{2,4},{4,6},{6,0},{1,3},{3,5},{5,7},{7,1},{8,10},{10,12},{12... | collective-permute-start | bytes 589832 | tf_op jit(solution)/shard_map/ppermute | solution.py:17
  102.6 12.5 %collective-permute-start.37 = (f32[128,384]{1,0:T(8,128)}, f32[128,384]{1,0:T(8,128)}, u32[]{:S(2)}, u32[]{:S(2)}) collective-permute-start(f32[128,384]{1,0:T(8,128)} %get-tuple-element.112.refs_12_), channel_id=1, source_target_pairs={{0,4},{2,6},{4,0},{6,2},{1,5},{3,7},{5,1},{7,3},{8,12},{10,14},{12... | collective-permute-start | bytes 589832 | tf_op jit(solution)/shard_map/ppermute | solution.py:17
  110.1 6.9 %collective-permute-start.38 = (f32[128,384]{1,0:T(8,128)}, f32[128,384]{1,0:T(8,128)}, u32[]{:S(2)}, u32[]{:S(2)}) collective-permute-start(f32[128,384]{1,0:T(8,128)} %get-tuple-element.112.refs_12_), channel_id=1, source_target_pairs={{0,6},{2,0},{4,2},{6,4},{1,7},{3,1},{5,3},{7,5},{8,14},{10,8},{12,... | collective-permute-start | bytes 589832 | tf_op jit(solution)/shard_map/ppermute | solution.py:17
  115.1 14.2 %collective-permute-start.25 = (f32[384,384]{1,0:T(8,128)}, f32[384,384]{1,0:T(8,128)S(1)}, u32[]{:S(2)}, u32[]{:S(2)}) collective-permute-start(f32[384,384]{1,0:T(8,128)} %get-tuple-element.102.refs_0_), channel_id=1, source_target_pairs={{0,1},{1,0},{2,3},{3,2},{4,5},{5,4},{6,7},{7,6},{8,9},{9,8},{10,11... | collective-permute-start | bytes 1769480 | tf_op jit(solution)/shard_map/ppermute | solution.py:25
  115.2 17.1 %collective-permute-start.26 = (f32[384,384]{1,0:T(8,128)S(1)}, f32[384,384]{1,0:T(8,128)S(1)}, u32[]{:S(2)}, u32[]{:S(2)}) collective-permute-start(f32[384,384]{1,0:T(8,128)S(1)} %collective-permute-done.22.refs_1_), channel_id=1, source_target_pairs={{0,1},{1,0},{2,3},{3,2},{4,5},{5,4},{6,7},{7,6},{8,9},{9,8},{10,11... | collective-permute-start | bytes 1769480 | tf_op jit(solution)/shard_map/ppermute | solution.py:25
  115.8 18.3 %collective-permute-start.27 = (f32[384,384]{1,0:T(8,128)S(1)}, f32[384,384]{1,0:T(8,128)S(1)}, u32[]{:S(2)}, u32[]{:S(2)}) collective-permute-start(f32[384,384]{1,0:T(8,128)S(1)} %collective-permute-done.23.refs_2_), channel_id=1, source_target_pairs={{0,1},{1,0},{2,3},{3,2},{4,5},{5,4},{6,7},{7,6},{8,9},{9,8},{10,11... | collective-permute-start | bytes 1769480 | tf_op jit(solution)/shard_map/ppermute | solution.py:25
  117.0 18.6 %collective-permute-start.28 = (f32[384,384]{1,0:T(8,128)S(1)}, f32[384,384]{1,0:T(8,128)S(1)}, u32[]{:S(2)}, u32[]{:S(2)}) collective-permute-start(f32[384,384]{1,0:T(8,128)S(1)} %collective-permute-done.24.refs_3_), channel_id=1, source_target_pairs={{0,1},{1,0},{2,3},{3,2},{4,5},{5,4},{6,7},{7,6},{8,9},{9,8},{10,11... | collective-permute-start | bytes 1769480 | tf_op jit(solution)/shard_map/ppermute | solution.py:25
  117.0 11.7 %collective-permute-start.33 = (f32[256,384]{1,0:T(8,128)}, f32[256,384]{1,0:T(8,128)S(1)}, u32[]{:S(2)}, u32[]{:S(2)}) collective-permute-start(f32[256,384]{1,0:T(8,128)} %get-tuple-element.111.refs_8_), channel_id=1, source_target_pairs={{0,16},{16,32},{32,48},{48,0},{1,17},{17,33},{33,49},{49,1},{2,18}... | collective-permute-start | bytes 1179656 | tf_op jit(solution)/shard_map/ppermute | solution.py:17
  128.8 25.1 %copy-start.21 = (f32[256,384]{1,0:T(8,128)}, f32[256,384]{1,0:T(8,128)S(1)}, u32[]{:S(2)}) copy-start(f32[256,384]{1,0:T(8,128)S(1)} %collective-permute-done.33.refs_9_) | copy-start | bytes 1179652
  128.8 30.2 %collective-permute-start.39 = (f32[512,256]{1,0:T(8,128)}, f32[512,256]{1,0:T(8,128)}, u32[]{:S(2)}, u32[]{:S(2)}) collective-permute-start(f32[512,256]{1,0:T(8,128)} %get-tuple-element.120), channel_id=1, source_target_pairs={{0,8},{8,64},{64,72},{72,0},{1,9},{9,65},{65,73},{73,1},{2,10},{10... | collective-permute-start | bytes 1572872 | tf_op jit(solution)/shard_map/ppermute | solution.py:21
  129.4 29.6 %collective-permute-start.40 = (f32[512,256]{1,0:T(8,128)}, f32[512,256]{1,0:T(8,128)}, u32[]{:S(2)}, u32[]{:S(2)}) collective-permute-start(f32[512,256]{1,0:T(8,128)} %get-tuple-element.121), channel_id=1, source_target_pairs={{0,64},{8,72},{64,0},{72,8},{1,65},{9,73},{65,1},{73,9},{2,66},{10... | collective-permute-start | bytes 1572872 | tf_op jit(solution)/shard_map/ppermute | solution.py:21
  132.3 26.7 %collective-permute-start.41 = (f32[512,256]{1,0:T(8,128)}, f32[512,256]{1,0:T(8,128)}, u32[]{:S(2)}, u32[]{:S(2)}) collective-permute-start(f32[512,256]{1,0:T(8,128)} %get-tuple-element.122), channel_id=1, source_target_pairs={{0,72},{8,0},{64,8},{72,64},{1,73},{9,1},{65,9},{73,65},{2,74},{10... | collective-permute-start | bytes 1572872 | tf_op jit(solution)/shard_map/ppermute | solution.py:21
  134.1 13.9 %collective-permute-start.34 = (f32[256,384]{1,0:T(8,128)}, f32[256,384]{1,0:T(8,128)}, u32[]{:S(2)}, u32[]{:S(2)}) collective-permute-start(f32[256,384]{1,0:T(8,128)} %get-tuple-element.111.refs_8_), channel_id=1, source_target_pairs={{0,32},{16,48},{32,0},{48,16},{1,33},{17,49},{33,1},{49,17},{2,34}... | collective-permute-start | bytes 1179656 | tf_op jit(solution)/shard_map/ppermute | solution.py:17
  136.5 17.3 %collective-permute-start.35 = (f32[256,384]{1,0:T(8,128)}, f32[256,384]{1,0:T(8,128)}, u32[]{:S(2)}, u32[]{:S(2)}) collective-permute-start(f32[256,384]{1,0:T(8,128)} %get-tuple-element.111.refs_8_), channel_id=1, source_target_pairs={{0,48},{16,0},{32,16},{48,32},{1,49},{17,1},{33,17},{49,33},{2,50}... | collective-permute-start | bytes 1179656 | tf_op jit(solution)/shard_map/ppermute | solution.py:17
  148.0 5.8 %collective-permute-start.29 = (f32[128,128]{1,0:T(8,128)S(1)}, f32[128,128]{1,0:T(8,128)S(1)}, u32[]{:S(2)}, u32[]{:S(2)}) collective-permute-start(f32[128,128]{1,0:T(8,128)S(1)} %reduce_sum.18.refs_0_), channel_id=1, source_target_pairs={{0,1},{1,0},{2,3},{3,2},{4,5},{5,4},{6,7},{7,6},{8,9},{9,8},{10,11... | collective-permute-start | bytes 196616 | tf_op jit(solution)/shard_map/ppermute | solution.py:25
  159.0 3.2 %collective-permute-start.45 = (f32[512,256]{1,0:T(8,128)}, f32[512,256]{1,0:T(8,128)S(1)}, u32[]{:S(2)}, u32[]{:S(2)}) collective-permute-start(f32[512,256]{1,0:T(8,128)} %collective-permute-done.39.refs_1_), channel_id=1, source_target_pairs={{0,1},{1,0},{2,3},{3,2},{4,5},{5,4},{6,7},{7,6},{8,9},{9,8},{10,11... | collective-permute-start | bytes 1572872 | tf_op jit(solution)/shard_map/ppermute | solution.py:25
  159.1 5.1 %collective-permute-start.46 = (f32[512,256]{1,0:T(8,128)}, f32[512,256]{1,0:T(8,128)S(1)}, u32[]{:S(2)}, u32[]{:S(2)}) collective-permute-start(f32[512,256]{1,0:T(8,128)} %collective-permute-done.40.refs_2_), channel_id=1, source_target_pairs={{0,1},{1,0},{2,3},{3,2},{4,5},{5,4},{6,7},{7,6},{8,9},{9,8},{10,11... | collective-permute-start | bytes 1572872 | tf_op jit(solution)/shard_map/ppermute | solution.py:25
  159.6 4.7 %collective-permute-start.47 = (f32[512,256]{1,0:T(8,128)}, f32[512,256]{1,0:T(8,128)S(1)}, u32[]{:S(2)}, u32[]{:S(2)}) collective-permute-start(f32[512,256]{1,0:T(8,128)} %collective-permute-done.41.refs_3_), channel_id=1, source_target_pairs={{0,1},{1,0},{2,3},{3,2},{4,5},{5,4},{6,7},{7,6},{8,9},{9,8},{10,11... | collective-permute-start | bytes 1572872 | tf_op jit(solution)/shard_map/ppermute | solution.py:25
  159.6 13.9 %collective-permute-start.42 = (f32[256,384]{1,0:T(8,128)}, f32[256,384]{1,0:T(8,128)S(1)}, u32[]{:S(2)}, u32[]{:S(2)}) collective-permute-start(f32[256,384]{1,0:T(8,128)} %get-tuple-element.124), channel_id=1, source_target_pairs={{0,16},{16,32},{32,48},{48,0},{1,17},{17,33},{33,49},{49,1},{2,18}... | collective-permute-start | bytes 1179656 | tf_op jit(solution)/shard_map/ppermute | solution.py:17
  160.3 13.7 %collective-permute-start.43 = (f32[256,384]{1,0:T(8,128)}, f32[256,384]{1,0:T(8,128)S(1)}, u32[]{:S(2)}, u32[]{:S(2)}) collective-permute-start(f32[256,384]{1,0:T(8,128)} %get-tuple-element.125), channel_id=1, source_target_pairs={{0,32},{16,48},{32,0},{48,16},{1,33},{17,49},{33,1},{49,17},{2,34}... | collective-permute-start | bytes 1179656 | tf_op jit(solution)/shard_map/ppermute | solution.py:17
  162.2 19.4 %collective-permute-start.44 = (f32[256,384]{1,0:T(8,128)}, f32[256,384]{1,0:T(8,128)S(1)}, u32[]{:S(2)}, u32[]{:S(2)}) collective-permute-start(f32[256,384]{1,0:T(8,128)} %get-tuple-element.126), channel_id=1, source_target_pairs={{0,48},{16,0},{32,16},{48,32},{1,49},{17,1},{33,17},{49,33},{2,50}... | collective-permute-start | bytes 1179656 | tf_op jit(solution)/shard_map/ppermute | solution.py:17
  182.3 31.1 %all-to-all-start.1 = ((f32[4,256,512]{2,1,0:T(8,128)}), f32[4,256,512]{2,1,0:T(8,128)S(1)}, u32[]{:S(2)}, u32[]{:S(2)}) async-start(f32[4,256,512]{2,1,0:T(8,128)} %shard_map.75), calls=%async_computation.1 | async-start | bytes 4194304 | tf_op jit(solution)/shard_map/all_to_all | solution.py:333
  186.7 1.7 collective-permute-start.48
  186.7 2.3 %collective-permute-start.49 = (f32[256,384]{1,0:T(8,128)S(1)}, f32[256,384]{1,0:T(8,128)S(1)}, u32[]{:S(2)}, u32[]{:S(2)}) collective-permute-start(f32[256,384]{1,0:T(8,128)S(1)} %collective-permute-done.42.refs_3_), channel_id=1, source_target_pairs={{0,1},{1,0},{2,3},{3,2},{4,5},{5,4},{6,7},{7,6},{8,9},{9,8},{10,11... | collective-permute-start | bytes 1179656 | tf_op jit(solution)/shard_map/ppermute | solution.py:25
  187.2 2.9 %collective-permute-start.50 = (f32[256,384]{1,0:T(8,128)S(1)}, f32[256,384]{1,0:T(8,128)S(1)}, u32[]{:S(2)}, u32[]{:S(2)}) collective-permute-start(f32[256,384]{1,0:T(8,128)S(1)} %collective-permute-done.43.refs_4_), channel_id=1, source_target_pairs={{0,1},{1,0},{2,3},{3,2},{4,5},{5,4},{6,7},{7,6},{8,9},{9,8},{10,11... | collective-permute-start | bytes 1179656 | tf_op jit(solution)/shard_map/ppermute | solution.py:25
  187.3 3.6 %collective-permute-start.51 = (f32[256,384]{1,0:T(8,128)}, f32[256,384]{1,0:T(8,128)}, u32[]{:S(2)}, u32[]{:S(2)}) collective-permute-start(f32[256,384]{1,0:T(8,128)} %copy-done.24), channel_id=1, source_target_pairs={{0,1},{1,0},{2,3},{3,2},{4,5},{5,4},{6,7},{7,6},{8,9},{9,8},{10,11... | collective-permute-start | bytes 1179656 | tf_op jit(solution)/shard_map/ppermute | solution.py:25
  195.8 15.7 %collective-permute-start.52 = (f32[384,384]{1,0:T(8,128)}, f32[384,384]{1,0:T(8,128)S(1)}, u32[]{:S(2)}, u32[]{:S(2)}) collective-permute-start(f32[384,384]{1,0:T(8,128)} %get-tuple-element.142), channel_id=1, source_target_pairs={{0,8},{8,0},{1,9},{9,1},{2,10},{10,2},{3,11},{11,3},{4,12},{12,4},... | collective-permute-start | bytes 1769480 | tf_op jit(solution)/shard_map/ppermute | solution.py:25
  (39 other events, 332.8 us)
Sparse Core Ops, SparseCore 0:
  9.7 33.4 all-gather.4
  44.8 35.3 all-gather.6
